TPU v7x, 32 devices: a whole 2x2x4 slice. The times are simulated.
32 devices in a mesh: expert: 16 (over z, y, x), replica: 2 (over core).
Axes of the slice: x: 2, y: 2, z: 4, core: 2. Of those that a mesh axis runs over, the one named last changes fastest.
Arguments:
- tokens: bfloat16 [8192, 1024], P(('expert', 'replica')), may hold values from -6 to 6
- routes: int32 [8192, 1], P(('expert', 'replica')), may hold values from 0 to 15; in each aligned block of 256 rows (0 to 255, 256 to 511, ...) at most 32 rows name the same one
- cotangent: bfloat16 [8192, 1024], P(('expert', 'replica')), may hold values from -6 to 6
- ln_gain: bfloat16 [2, 16, 1024], P(None, 'expert'), may hold values from 0.5 to 1.5
- ln_shift: bfloat16 [2, 16, 1024], P(None, 'expert'), may hold values from -0.59765625 to 0.59765625
- w_in: bfloat16 [2, 16, 1024, 4096], P(None, 'expert', None, 'replica'), may hold values from -0.1875 to 0.1875
- b_in: bfloat16 [2, 16, 4096], P(None, 'expert'), may hold values from -0.59765625 to 0.59765625
- w_out: bfloat16 [2, 16, 4096, 1024], P(None, 'expert', 'replica'), may hold values from -0.09375 to 0.09375
- b_out: bfloat16 [2, 16, 1024], P(None, 'expert'), may hold values from -0.59765625 to 0.59765625
- centroid: bfloat16 [16, 1024], P('expert'), may hold values from -0.125 to 0.125
Outputs:
- mixed: bfloat16 [8192, 1024], P(('expert', 'replica'))
- grad_tokens: bfloat16 [8192, 1024], P(('expert', 'replica'))
- grad_w_in: float32 [2, 16, 1024, 4096], P(None, 'expert', None, 'replica')
- grad_w_out: float32 [2, 16, 4096, 1024], P(None, 'expert', 'replica')
- grad_b_in: float32 [2, 16, 4096], P(None, 'expert')
- grad_b_out: float32 [2, 16, 1024], P(None, 'expert')
- grad_gain: float32 [2, 16, 1024], P(None, 'expert')
- grad_shift: float32 [2, 16, 1024], P(None, 'expert')
- grad_centroid: float32 [16, 1024], P('expert')
- mean_gate: float32 [16], P('expert')
- load: float32 [16], P('expert')
Inputs may be any that keep to these rules, and one draw needn't show every extreme that they name: `routes`: in each aligned block of 256 rows (the rows of one device) no expert is named by more than 32 rows; every expert is named by some row.
All inputs are finite; a program needn't handle non-finite values.
Results may differ from a plain program's by a relative error of at most 0.007.
Values may be sent and summed in bfloat16 or wider, within the bound.
No kernel may reach another device: no remote copies, remote signals or barrier semaphores. Data moves between devices by JAX's collectives and lax.ppermute only.
A program may use at most 256 MiB of HBM per device.

v0:
```python
import jax
import jax.numpy as jnp
from jax import lax
from jax.sharding import PartitionSpec as P

epsilon = 1e-05
root_half = 0.7071067811865476
inv_root_two_pi = 0.3989422804014327


def slot_of_tokens(routes, experts, capacity):
    route = routes[:, 0]
    labels = jnp.arange(experts, dtype=jnp.int32)
    onehot = (route[:, None] == labels[None, :]).astype(jnp.int32)
    earlier = jnp.cumsum(onehot, axis=0) - onehot
    return route * capacity + jnp.sum(earlier * onehot, axis=1)


def gelu_slope(hidden):
    return (
        0.5 * (1.0 + lax.erf(hidden * root_half))
        + hidden * jnp.exp(-0.5 * hidden * hidden) * inv_root_two_pi
    )


def on_device(tokens, routes, cotangent, ln_gain, ln_shift, w_in, b_in, w_out, b_out, centroid):
    experts = lax.axis_size("expert")
    replicas = lax.axis_size("replica")
    tok_dev = tokens.shape[0]
    row_width = tokens.shape[1]
    sublayers = ln_gain.shape[0]
    capacity = 2 * tok_dev // experts
    slot_count = experts * capacity
    slot_ids = slot_of_tokens(routes, experts, capacity)
    owners = (
        jnp.zeros((slot_count,), jnp.int32).at[slot_ids].set(jnp.arange(tok_dev, dtype=jnp.int32))
    )
    filled = (
        jnp.zeros((slot_count,), jnp.bfloat16).at[slot_ids].set(jnp.ones((tok_dev,), jnp.bfloat16))
    )

    def pack_slots(values):
        picked = jnp.take(values, owners, axis=0)
        cleared = jnp.where(filled[:, None] > 0, picked, jnp.zeros_like(picked))
        return cleared.reshape(experts, capacity, row_width)

    def unpack_slots(returned):
        return jnp.take(returned.reshape(slot_count, row_width), slot_ids, axis=0).astype(
            jnp.float32
        )

    sent_mask = filled.reshape(experts, capacity)
    received, live_mask = (
        lax.all_to_all(pack_slots(tokens), "expert", split_axis=0, concat_axis=0, tiled=True),
        lax.all_to_all(sent_mask, "expert", split_axis=0, concat_axis=0, tiled=True),
    )
    full_first, full_second = (
        lax.all_gather(w_in, "replica", axis=3, tiled=True),
        lax.all_gather(w_out, "replica", axis=2, tiled=True),
    )
    received = received.reshape(slot_count, row_width)
    live_rows = live_mask.reshape(slot_count).astype(jnp.float32)
    center = centroid[0]
    gains = ln_gain[:, 0].astype(jnp.float32)
    shifts = ln_shift[:, 0].astype(jnp.float32)
    first_bias = b_in[:, 0].astype(jnp.float32)
    second_bias = b_out[:, 0].astype(jnp.float32)
    inputs = received.astype(jnp.float32)
    logits = jnp.dot(received, center, preferred_element_type=jnp.float32)
    gate_value = jax.nn.sigmoid(logits)
    state = inputs
    saved = []
    for layer in range(sublayers):
        average = jnp.mean(state, axis=1, keepdims=True)
        centered = state - average
        variance = jnp.mean(centered * centered, axis=1, keepdims=True)
        inv_scale = lax.rsqrt(variance + epsilon)
        normed = centered * inv_scale
        lowered = (normed * gains[layer] + shifts[layer]).astype(jnp.bfloat16)
        hidden = (
            jnp.dot(lowered, full_first[layer, 0], preferred_element_type=jnp.float32)
            + first_bias[layer]
        )
        activated = jax.nn.gelu(hidden, approximate=False).astype(jnp.bfloat16)
        second = (
            jnp.dot(activated, full_second[layer, 0], preferred_element_type=jnp.float32)
            + second_bias[layer]
        )
        saved.append((normed, inv_scale, lowered, hidden, activated))
        state = state + second
    branch = (gate_value[:, None] * state).astype(jnp.bfloat16)
    returned = lax.all_to_all(
        branch.reshape(experts, capacity, row_width),
        "expert",
        split_axis=0,
        concat_axis=0,
        tiled=True,
    )
    mixed = (tokens.astype(jnp.float32) + unpack_slots(returned)).astype(jnp.bfloat16)
    cot_slots = lax.all_to_all(
        pack_slots(cotangent), "expert", split_axis=0, concat_axis=0, tiled=True
    )
    upstream = cot_slots.reshape(slot_count, row_width).astype(jnp.float32)
    dgate = jnp.sum(upstream * state, axis=1)
    dlogit = dgate * gate_value * (1.0 - gate_value)
    carried = gate_value[:, None] * upstream
    grads_first = [None] * sublayers
    grads_second = [None] * sublayers
    grads_bias_first = [None] * sublayers
    grads_bias_second = [None] * sublayers
    grads_gain = [None] * sublayers
    grads_shift = [None] * sublayers
    for layer in reversed(range(sublayers)):
        normed, inv_scale, lowered, hidden, activated = saved[layer]
        w_first = full_first[layer, 0]
        w_second = full_second[layer, 0]
        dsecond = carried.astype(jnp.bfloat16)

        def second_term(first_row, row_count, activated=activated, dsecond=dsecond):
            return lax.dot_general(
                activated, dsecond, (((0,), (0,)), ((), ())), preferred_element_type=jnp.float32
            )

        grads_second[layer] = lax.psum_scatter(
            second_term(jnp.int32(0), w_second.shape[0] // replicas * lax.axis_size("replica")),
            "replica",
            scatter_dimension=0,
            tiled=True,
        )
        grads_bias_second[layer] = jnp.sum(dsecond.astype(jnp.float32), axis=0)
        dact = lax.dot_general(
            dsecond, w_second, (((1,), (1,)), ((), ())), preferred_element_type=jnp.float32
        )
        dhidden = (dact * gelu_slope(hidden)).astype(jnp.bfloat16)
        first_full = lax.dot_general(
            lowered, dhidden, (((0,), (0,)), ((), ())), preferred_element_type=jnp.float32
        )
        grads_first[layer] = lax.psum_scatter(
            first_full, "replica", scatter_dimension=1, tiled=True
        )
        grads_bias_first[layer] = jnp.sum(dhidden.astype(jnp.float32), axis=0)
        dnormed = lax.dot_general(
            dhidden, w_first, (((1,), (1,)), ((), ())), preferred_element_type=jnp.float32
        )
        grads_gain[layer] = jnp.sum(dnormed * normed, axis=0)
        grads_shift[layer] = jnp.sum(dnormed, axis=0)
        dxhat = dnormed * gains[layer]
        carried = carried + inv_scale * (
            dxhat
            - jnp.mean(dxhat, axis=1, keepdims=True)
            - normed * jnp.mean(dxhat * normed, axis=1, keepdims=True)
        )
    grad_center_local = jnp.sum(dlogit[:, None] * inputs, axis=0)
    drow = (carried + dlogit[:, None] * center.astype(jnp.float32)[None, :]).astype(jnp.bfloat16)
    grad_return = lax.all_to_all(
        drow.reshape(experts, capacity, row_width),
        "expert",
        split_axis=0,
        concat_axis=0,
        tiled=True,
    )
    grad_tokens = (cotangent.astype(jnp.float32) + unpack_slots(grad_return)).astype(jnp.bfloat16)
    gate_total = jnp.sum(gate_value * live_rows)
    count_total = jnp.sum(live_rows)
    summed = lax.psum(
        (
            jnp.stack(grads_gain),
            jnp.stack(grads_shift),
            jnp.stack(grads_bias_first),
            jnp.stack(grads_bias_second),
            grad_center_local,
            gate_total,
            count_total,
        ),
        "replica",
    )
    mean_gate = (summed[5] / summed[6]).reshape(1)
    load = (summed[6] / (tok_dev * replicas)).reshape(1)
    return (
        mixed,
        grad_tokens,
        jnp.stack(grads_first)[:, None],
        jnp.stack(grads_second)[:, None],
        summed[2][:, None],
        summed[3][:, None],
        summed[0][:, None],
        summed[1][:, None],
        summed[4][None],
        mean_gate,
        load,
    )


def solution(mesh):
    return jax.shard_map(
        on_device,
        mesh=mesh,
        in_specs=(
            P(("expert", "replica"), None),
            P(("expert", "replica"), None),
            P(("expert", "replica"), None),
            P(None, "expert", None),
            P(None, "expert", None),
            P(None, "expert", None, "replica"),
            P(None, "expert", None),
            P(None, "expert", "replica", None),
            P(None, "expert", None),
            P("expert", None),
        ),
        out_specs=(
            P(("expert", "replica"), None),
            P(("expert", "replica"), None),
            P(None, "expert", None, "replica"),
            P(None, "expert", "replica", None),
            P(None, "expert", None),
            P(None, "expert", None),
            P(None, "expert", None),
            P(None, "expert", None),
            P("expert", None),
            P("expert"),
            P("expert"),
        ),
        check_vma=False,
    )
```

profile of v0, /device:TPU:8, one launch (start us, length us, event | category | flops | bytes accessed | tf_op | source)
XLA Modules:
  0.0 348.6 jit_solution(5352335202257040848)
XLA Ops:
  7.2 0.7 all-gather.3.cloned.1.call-update
  8.0 0.7 all-gather.5.cloned.1.call-update
  8.7 0.6 reduce-window.6
  9.7 2.2 scatter_custom_fusion
  11.8 0.7 all_to_all.24
  12.5 7.2 %all-to-all-start.4 = ((bf16[16,1,32]{2,1,0:T(2,128)(2,1)}), bf16[16,1,32]{2,1,0:T(2,128)(2,1)S(1)}, u32[]{:S(2)}, u32[]{:S(2)}) async-start(bf16[16,1,32]{2,1,0:T(2,128)(2,1)} %all_to_all.24), calls=%async_computation.8 | async-start | bytes 16384 | tf_op jit(solution)/shard_map/all_to_all | solution.py:55
  19.7 1.4 scatter_custom_fusion.1
  21.2 2.1 gather_fusion.2
  23.3 2.1 gather_fusion
  25.4 1.6 select_select_fusion
  27.1 6.9 %all-to-all-start = ((bf16[16,32,1024]{2,1,0:T(8,128)(2,1)}), bf16[16,32,1024]{2,1,0:T(8,128)(2,1)S(1)}, u32[]{:S(2)}, u32[]{:S(2)}) async-start(bf16[16,32,1024]{2,1,0:T(8,128)(2,1)} %bitcast.144), calls=%async_computation | async-start | bytes 2097152 | tf_op jit(solution)/shard_map/all_to_all | solution.py:54
  34.1 0.6 fusion.88
  34.7 24.3 %all-to-all-done = bf16[16,32,1024]{2,1,0:T(8,128)(2,1)S(1)} async-done(((bf16[16,32,1024]{2,1,0:T(8,128)(2,1)}), bf16[16,32,1024]{2,1,0:T(8,128)(2,1)S(1)}, u32[]{:S(2)}, u32[]{:S(2)}) %all-to-all-start) | async-done | bytes 1048608 | tf_op jit(solution)/shard_map/all_to_all | solution.py:54
  58.9 4.8 %all-to-all-start.2 = ((bf16[16,32,1024]{2,1,0:T(8,128)(2,1)}), bf16[16,32,1024]{2,1,0:T(8,128)(2,1)S(1)}, u32[]{:S(2)}, u32[]{:S(2)}) async-start(bf16[16,32,1024]{2,1,0:T(8,128)(2,1)} %bitcast.143), calls=%async_computation.2 | async-start | bytes 2097152 | tf_op jit(solution)/shard_map/all_to_all | solution.py:100
  63.9 0.6 convert_reduce_fusion.5
  64.7 0.4 fusion.75
  65.0 0.6 multiply_reduce_fusion.5
  66.2 0.4 fusion.42
  66.7 21.1 %all-to-all-done.2 = bf16[16,32,1024]{2,1,0:T(8,128)(2,1)S(1)} async-done(((bf16[16,32,1024]{2,1,0:T(8,128)(2,1)}), bf16[16,32,1024]{2,1,0:T(8,128)(2,1)S(1)}, u32[]{:S(2)}, u32[]{:S(2)}) %all-to-all-start.2) | async-done | bytes 1048608 | tf_op jit(solution)/shard_map/all_to_all | solution.py:100
  87.7 1.9 convert_reduce_fusion.3
  89.6 0.4 fusion.45
  90.1 25.4 %fusion.2 = (bf16[512,4096]{1,0:T(8,128)(2,1)}, f32[512,4096]{1,0:T(8,128)}) fusion(f32[4096]{0:T(1024)S(1)} %bitcast.161, bf16[512,1024]{1,0:T(8,128)(2,1)S(1)} %bitcast.148, bf16[2,1,1024,4096]{3,2,1,0:T(8,128)(2,1)} %all-gather.3.cloned.1.call-done), kind=kOutput, calls=%fused_computation.14 | convolution fusion | flops 4433379328 | bytes 22036480 | tf_op jit(solution)/shard_map/dot_general | solution.py:81
  115.6 8.3 %fusion.91 = (f32[512]{0:T(512)S(1)}, f32[512,1024]{1,0:T(8,128)S(1)}) fusion(f32[1024]{0:T(1024)S(1)} %bitcast.178, bf16[512,4096]{1,0:T(8,128)(2,1)} %get-tuple-element.88, bf16[2,1,4096,1024]{3,2,1,0:T(8,128)(2,1)} %all-gather.5.cloned.1.call-done, bf16[512,1024]{1,0:T(8,128)(2,1)S(1)} %bitcast.135), kind=kOutput, calls=%fused_computation.175 | convolution fusion | flops 4297063936 | bytes 15734784 | tf_op jit(solution)/shard_map/dot_general | solution.py:86
  124.0 0.3 multiply_reduce_fusion.2
  124.3 26.4 %fusion.5 = (bf16[512,4096]{1,0:T(8,128)(2,1)}, f32[512,4096]{1,0:T(8,128)S(1)}) fusion(f32[4096]{0:T(1024)S(1)} %bitcast.164, bf16[2,1,1024,4096]{3,2,1,0:T(8,128)(2,1)} %all-gather.3.cloned.1.call-done, f32[512,1024]{1,0:T(8,128)S(1)} %get-tuple-element.91, f32[1024]{0:T(1024)S(1)} %bitcast.176, f32[1024]{0:T(1024)S(1)} %bitcast.169, ...), kind=kOutput, calls=%fused_computation.17 | convolution fusion | flops 4436000768 | bytes 23097344 | tf_op jit(solution)/shard_map/dot_general | solution.py:81
  150.7 9.8 %convert_reduce_fusion = (f32[4096]{0:T(1024)S(1)}, bf16[512,4096]{1,0:T(8,128)(2,1)S(1)}) fusion(f32[512,4096]{1,0:T(8,128)S(1)} %get-tuple-element.93, f32[4096]{0:T(1024)S(1)} %bitcast.165, bf16[512,1024]{1,0:T(8,128)(2,1)S(1)} %bitcast.147, bf16[2,1,4096,1024]{3,2,1,0:T(8,128)(2,1)} %all-gather.5.cloned.1.call-done), kind=kOutput, calls=%fused_computation.34 | convolution fusion | flops 4322226176 | bytes 22052864 | tf_op jit(solution)/shard_map/dot_general | solution.py:131
  160.6 1.9 copy-done.31
  162.5 8.8 %fusion.84 = f32[1024,4096]{1,0:T(8,128)} fusion(bf16[512,4096]{1,0:T(8,128)(2,1)S(1)} %get-tuple-element.97, f32[512,1024]{1,0:T(8,128)S(1)} %get-tuple-element.91, f32[1024]{0:T(1024)S(1)} %bitcast.177, f32[1024]{0:T(1024)S(1)} %bitcast.170, f32[512]{0:T(512)S(1)} %add_rsqrt_fusion.1, f32[512]{0:T(512)S(1)} %broadcast_multiply_fusion.5), kind=kOutput, calls=%fused_computation.170 | convolution fusion | flops 4297588736 | bytes 23080960 | tf_op jit(solution)/shard_map/dot_general | solution.py:135
  171.4 0.6 copy-done.9
  172.2 9.1 %multiply_reduce_fusion = (f32[1024]{0:T(1024)S(1)}, f32[512]{0:T(512)S(1)}, f32[512]{0:T(512)S(1)}, f32[1024]{0:T(1024)S(1)}, f32[512,1024]{1,0:T(8,128)S(1)}) fusion(f32[512,1024]{1,0:T(8,128)S(1)} %get-tuple-element.91, f32[512]{0:T(512)S(1)} %add_rsqrt_fusion.1, f32[512]{0:T(512)S(1)} %broadcast_multiply_fusion.5, f32[1024]{0:T(1024)S(1)} %bitcast.171, ...), kind=kOutput, calls=%fused_computation.107 | convolution fusion | flops 4299682816 | bytes 16797696 | tf_op jit(solution)/shard_map/dot_general | solution.py:142
  181.3 13.1 %fusion.64 = (f32[512]{0:T(512)S(1)}, bf16[512,1024]{1,0:T(8,128)(2,1)}, bf16[512,1024]{1,0:T(8,128)(2,1)}, f32[1024]{0:T(1024)S(1)}, f32[512,1024]{1,0:T(8,128)S(1)}) fusion(bf16[16,32,1024]{2,1,0:T(8,128)(2,1)S(1)} %copy-done.5, f32[512]{0:T(512)S(1)} %copy-done.16, f32[512]{0:T(512)S(1)} %broadcast_multiply_fusion.3, f32[512,1024]{1,0:T(8,128)} %copy-done.6, ...), kind=kOutput, calls=%fused_computation.106 | convolution fusion | flops 4305451520 | bytes 22044672 | tf_op jit(solution)/shard_map/dot_general | solution.py:86
  194.5 10.0 %convert_reduce_fusion.1 = (f32[4096]{0:T(1024)S(1)}, bf16[512,4096]{1,0:T(8,128)(2,1)S(1)}) fusion(f32[512,4096]{1,0:T(8,128)S(1)} %bitcast.184, f32[4096]{0:T(1024)S(1)} %bitcast.162, bf16[2,1,4096,1024]{3,2,1,0:T(8,128)(2,1)} %all-gather.5.cloned.1.call-done, f32[512,1024]{1,0:T(8,128)S(1)} %get-tuple-element.75), kind=kOutput, calls=%fused_computation.35 | convolution fusion | flops 4322750464 | bytes 23101440 | tf_op jit(solution)/shard_map/dot_general | solution.py:131
  204.6 2.0 copy-done.32
  206.5 8.8 %fusion.65 = f32[1024,4096]{1,0:T(8,128)} fusion(bf16[512,4096]{1,0:T(8,128)(2,1)S(1)} %get-tuple-element.99, bf16[512,1024]{1,0:T(8,128)(2,1)S(1)} %bitcast.136, f32[1024]{0:T(1024)S(1)} %bitcast.155, f32[512]{0:T(512)S(1)} %div.43, f32[1024]{0:T(1024)S(1)} %bitcast.150, f32[512]{0:T(512)S(1)} %rsqrt.22), kind=kOutput, calls=%fused_computation.118 | convolution fusion | flops 4298113024 | bytes 22032384 | tf_op jit(solution)/shard_map/dot_general | solution.py:135
  215.4 13.7 %fusion.81 = f32[4096,1024]{1,0:T(8,128)} fusion(bf16[512,4096]{1,0:T(8,128)(2,1)} %get-tuple-element.88, f32[512,1024]{1,0:T(8,128)S(1)} %get-tuple-element.75), kind=kOutput, calls=%fused_computation.167 | convolution fusion | flops 4295491584 | bytes 23068672 | tf_op jit(solution)/shard_map/dot_general | solution.py:120
  229.2 14.9 %fusion.92 = f32[4096,1024]{1,0:T(8,128)} fusion(bf16[512,4096]{1,0:T(8,128)(2,1)} %get-tuple-element.92, bf16[512,1024]{1,0:T(8,128)(2,1)} %get-tuple-element.73), kind=kOutput, calls=%fused_computation.176 | convolution fusion | flops 4294967296 | bytes 22020096 | tf_op jit(solution)/shard_map/dot_general | solution.py:120
  244.1 0.7 copy-done.18
  244.8 8.8 %fusion.59 = (f32[1024]{0:T(1024)S(1)}, f32[512]{0:T(512)S(1)}, f32[512]{0:T(512)S(1)}, f32[1024]{0:T(1024)S(1)}, f32[512,1024]{1,0:T(8,128)S(1)}) fusion(f32[512]{0:T(512)S(1)} %div.43, f32[512]{0:T(512)S(1)} %rsqrt.22, bf16[16,32,1024]{2,1,0:T(8,128)(2,1)S(1)} %all-to-all-done, f32[1024]{0:T(1024)S(1)} %bitcast.151, bf16[512,4096]{1,0:T(8,128)(2,1)} %copy-done.32, ...), kind=kOutput, calls=%fused_computation.98 | convolution fusion | flops 4300207104 | bytes 15749120 | tf_op jit(solution)/shard_map/dot_general | solution.py:142
  253.7 0.9 fusion.56
  254.6 29.7 %all_to_all.30 = bf16[16,32,1024]{2,1,0:T(8,128)(2,1)} all-to-all(bf16[16,32,1024]{2,1,0:T(8,128)(2,1)S(1)} %bitcast.145), channel_id=1, replica_groups=mesh['expert'=16,'replica'=2] {'expert'}, dimensions={0} | all-to-all | bytes 2097152 | tf_op jit(solution)/shard_map/all_to_all | solution.py:155
  284.3 4.6 %all-to-all-start.1 = ((bf16[16,32,1024]{2,1,0:T(8,128)(2,1)}), bf16[16,32,1024]{2,1,0:T(8,128)(2,1)S(1)}, u32[]{:S(2)}, u32[]{:S(2)}) async-start(bf16[16,32,1024]{2,1,0:T(8,128)(2,1)} %bitcast.146), calls=%async_computation.1 | async-start | bytes 2097152 | tf_op jit(solution)/shard_map/all_to_all | solution.py:92
  289.4 5.0 %all-reduce = (f32[2,1,4096]{2,1,0:T(1,128)}, f32[2,1,1024]{2,1,0:T(1,128)}, f32[2,1,1024]{2,1,0:T(1,128)}, f32[2,1,1024]{2,1,0:T(1,128)}, f32[1,1024]{1,0:T(1,128)}, /*index=5*/f32[]{:T(128)}, f32[]{:T(128)}) all-reduce(f32[2,1,4096]{2,1,0:T(1,128)S(1)} %broadcast_in_dim.83, ...), channel_id=1, replica_groups=mesh['expert'=16,'replica'=2] {'replica'}, use_global_device_ids=true, to_apply=%region_20.23 | all-reduce | flops 15362 | bytes 122896 | tf_op jit(solution)/shard_map/psum | solution.py:165
  296.5 3.2 gather_fusion.3
  299.6 13.2 %all-to-all-done.1 = bf16[16,32,1024]{2,1,0:T(8,128)(2,1)S(1)} async-done(((bf16[16,32,1024]{2,1,0:T(8,128)(2,1)}), bf16[16,32,1024]{2,1,0:T(8,128)(2,1)S(1)}, u32[]{:S(2)}, u32[]{:S(2)}) %all-to-all-start.1) | async-done | bytes 1048608 | tf_op jit(solution)/shard_map/all_to_all | solution.py:92
  312.8 1.2 gather_fusion.1
  314.0 1.3 add_convert_fusion.1
  315.4 11.9 %maximum_bitcast_fusion = f32[2,1,1024,2048]{3,2,1,0:T(8,128)} fusion(f32[1,1024,2048]{2,1,0:T(8,128)} %bitcast.139, f32[1,1024,2048]{2,1,0:T(8,128)} %bitcast.140), kind=kLoop, calls=%fused_computation.6 | loop fusion | flops 4194304 | bytes 33554432
  327.2 12.0 %maximum_bitcast_fusion.1 = f32[2,1,2048,1024]{3,2,1,0:T(8,128)} fusion(f32[1,2048,1024]{2,1,0:T(8,128)} %bitcast.142, f32[1,2048,1024]{2,1,0:T(8,128)} %bitcast.141), kind=kLoop, calls=%fused_computation.7 | loop fusion | flops 4194304 | bytes 33554432
  (126 shorter events, 2.5 us)
Async XLA Ops:
  7.2 1.5 copy-start.22
  7.2 14.0 %copy-start = (bf16[256,1024]{1,0:T(8,128)(2,1)S(1)}, bf16[256,1024]{1,0:T(8,128)(2,1)}, u32[]{:S(2)}) copy-start(bf16[256,1024]{1,0:T(8,128)(2,1)} %param.16) | copy-start | bytes 1572868
  7.2 82.9 %all-gather.3.cloned.1.call-start = ((), (), s32[]{:S(2)}) async-start(), calls=%async_computation.9 | async-start | bytes 25165824 | tf_op jit(solution)/shard_map/all_gather | solution.py:58
  7.9 15.3 %copy-start.2 = (bf16[256,1024]{1,0:T(8,128)(2,1)S(1)}, bf16[256,1024]{1,0:T(8,128)(2,1)}, u32[]{:S(2)}) copy-start(bf16[256,1024]{1,0:T(8,128)(2,1)} %param.14) | copy-start | bytes 1572868
  7.9 107.7 %all-gather.5.cloned.1.call-start = ((), (), s32[]{:S(2)}) async-start(), calls=%async_computation.10 | async-start | bytes 25165824 | tf_op jit(solution)/shard_map/all_gather | solution.py:59
  9.6 11.5 %copy-start.27 = (s32[256]{0:T(256)}, s32[256]{0:T(256)S(1)}, u32[]{:S(2)}) copy-start(s32[256]{0:T(256)S(1)} %fusion.73) | copy-start | bytes 3076
  12.5 14.5 %all-to-all-start.4 = ((bf16[16,1,32]{2,1,0:T(2,128)(2,1)}), bf16[16,1,32]{2,1,0:T(2,128)(2,1)S(1)}, u32[]{:S(2)}, u32[]{:S(2)}) async-start(bf16[16,1,32]{2,1,0:T(2,128)(2,1)} %all_to_all.24), calls=%async_computation.8 | async-start | bytes 16384 | tf_op jit(solution)/shard_map/all_to_all | solution.py:55
  23.3 10.7 %copy-start.24 = (bf16[2,1,1024]{2,0,1:T(2,128)(2,1)S(1)}, bf16[2,1,1024]{2,0,1:T(2,128)(2,1)}, u32[]{:S(2)}) copy-start(bf16[2,1,1024]{2,0,1:T(2,128)(2,1)} %param.17) | copy-start | bytes 12292
  23.3 10.7 %copy-start.25 = (bf16[2,1,1024]{2,0,1:T(2,128)(2,1)S(1)}, bf16[2,1,1024]{2,0,1:T(2,128)(2,1)}, u32[]{:S(2)}) copy-start(bf16[2,1,1024]{2,0,1:T(2,128)(2,1)} %param.18) | copy-start | bytes 12292
  23.3 10.7 %copy-start.26 = (bf16[2,1,1024]{2,0,1:T(2,128)(2,1)S(1)}, bf16[2,1,1024]{2,0,1:T(2,128)(2,1)}, u32[]{:S(2)}) copy-start(bf16[2,1,1024]{2,0,1:T(2,128)(2,1)} %param.22) | copy-start | bytes 12292
  23.3 40.6 %copy-start.12 = (bf16[2,1,4096]{2,0,1:T(2,128)(2,1)S(1)}, bf16[2,1,4096]{2,0,1:T(2,128)(2,1)}, u32[]{:S(2)}) copy-start(bf16[2,1,4096]{2,0,1:T(2,128)(2,1)} %param.20) | copy-start | bytes 49156
  23.3 41.3 %copy-start.17 = (bf16[1,1024]{1,0:T(2,128)(2,1)S(1)}, bf16[1,1024]{1,0:T(2,128)(2,1)}, u32[]{:S(2)}) copy-start(bf16[1,1024]{1,0:T(2,128)(2,1)} %param.23) | copy-start | bytes 6148
  27.1 31.9 %all-to-all-start = ((bf16[16,32,1024]{2,1,0:T(8,128)(2,1)}), bf16[16,32,1024]{2,1,0:T(8,128)(2,1)S(1)}, u32[]{:S(2)}, u32[]{:S(2)}) async-start(bf16[16,32,1024]{2,1,0:T(8,128)(2,1)} %bitcast.144), calls=%async_computation | async-start | bytes 2097152 | tf_op jit(solution)/shard_map/all_to_all | solution.py:54
  34.0 81.6 %copy-start.13 = (f32[1,1,1024]{2,0,1:T(1,128)}, f32[1,1,1024]{2,0,1:T(1,128)S(1)}, u32[]{:S(2)}) copy-start(f32[1,1,1024]{2,0,1:T(1,128)S(1)} %get-tuple-element.81) | copy-start | bytes 12292
  34.0 81.5 %copy-start.20 = (f32[1,1,1024]{2,0,1:T(1,128)}, f32[1,1,1024]{2,0,1:T(1,128)S(1)}, u32[]{:S(2)}) copy-start(f32[1,1,1024]{2,0,1:T(1,128)S(1)} %get-tuple-element.83) | copy-start | bytes 12292
  58.9 28.8 %all-to-all-start.2 = ((bf16[16,32,1024]{2,1,0:T(8,128)(2,1)}), bf16[16,32,1024]{2,1,0:T(8,128)(2,1)S(1)}, u32[]{:S(2)}, u32[]{:S(2)}) async-start(bf16[16,32,1024]{2,1,0:T(8,128)(2,1)} %bitcast.143), calls=%async_computation.2 | async-start | bytes 2097152 | tf_op jit(solution)/shard_map/all_to_all | solution.py:100
  63.7 251.7 %reduce-scatter.7.cloned.1.call-start = ((), (), s32[]{:S(2)}) async-start(), calls=%async_computation.12 | async-start | bytes 25165824 | tf_op jit(solution)/shard_map/reduce_scatter | solution.py:138
  65.7 0.6 copy-start.15
  66.2 49.3 %copy-start.8 = (f32[16,32]{1,0:T(8,128)}, f32[16,32]{1,0:T(8,128)S(1)}, u32[]{:S(2)}) copy-start(f32[16,32]{1,0:T(8,128)S(1)} %broadcast_multiply_fusion) | copy-start | bytes 6148
  66.7 48.9 %copy-start.10 = (f32[16,32]{1,0:T(8,128)}, f32[16,32]{1,0:T(8,128)S(1)}, u32[]{:S(2)}) copy-start(f32[16,32]{1,0:T(8,128)S(1)} %add_rsqrt_fusion) | copy-start | bytes 6148
  87.7 27.8 %copy-start.4 = (bf16[16,32,1024]{2,1,0:T(8,128)(2,1)}, bf16[16,32,1024]{2,1,0:T(8,128)(2,1)S(1)}, u32[]{:S(2)}) copy-start(bf16[16,32,1024]{2,1,0:T(8,128)(2,1)S(1)} %all-to-all-done.2) | copy-start | bytes 3145732
  123.9 48.2 %copy-start.6 = (f32[512,1024]{1,0:T(8,128)}, f32[512,1024]{1,0:T(8,128)S(1)}, u32[]{:S(2)}) copy-start(f32[512,1024]{1,0:T(8,128)S(1)} %get-tuple-element.91) | copy-start | bytes 6291460
  124.3 26.4 %copy-start.7 = (bf16[16,32,1024]{2,1,0:T(8,128)(2,1)S(1)}, bf16[16,32,1024]{2,1,0:T(8,128)(2,1)}, u32[]{:S(2)}) copy-start(bf16[16,32,1024]{2,1,0:T(8,128)(2,1)} %get-tuple-element.68) | copy-start | bytes 3145732
  160.6 1.9 copy-start.31
  171.3 0.7 copy-start.9
  171.3 0.8 copy-start.11
  171.3 144.1 %reduce-scatter.5.cloned.1.call-start = ((), (), s32[]{:S(2)}) async-start(), calls=%async_computation.11 | async-start | bytes 25165824 | tf_op jit(solution)/shard_map/reduce_scatter | solution.py:138
  172.1 9.2 %copy-start.5 = (bf16[16,32,1024]{2,1,0:T(8,128)(2,1)S(1)}, bf16[16,32,1024]{2,1,0:T(8,128)(2,1)}, u32[]{:S(2)}) copy-start(bf16[16,32,1024]{2,1,0:T(8,128)(2,1)} %copy-done.4) | copy-start | bytes 3145732
  172.1 9.2 %copy-start.16 = (f32[512]{0:T(512)S(1)}, f32[512]{0:T(512)}, u32[]{:S(2)}) copy-start(f32[512]{0:T(512)} %copy-done.15) | copy-start | bytes 6148
  172.1 9.2 %copy-start.29 = (f32[1,1,1024]{2,0,1:T(1,128)S(1)}, f32[1,1,1024]{2,0,1:T(1,128)}, u32[]{:S(2)}) copy-start(f32[1,1,1024]{2,0,1:T(1,128)} %get-tuple-element.78) | copy-start | bytes 12292
  172.2 9.2 %copy-start.30 = (bf16[512,4096]{1,0:T(8,128)(2,1)S(1)}, bf16[512,4096]{1,0:T(8,128)(2,1)}, u32[]{:S(2)}) copy-start(bf16[512,4096]{1,0:T(8,128)(2,1)} %get-tuple-element.92) | copy-start | bytes 12582916
  172.2 22.3 %slice-start = ((s8[8388608]{0:T(1024)(128)(4,1)}), s8[4194304]{0:T(1024)(128)(4,1)S(1)}, s32[]{:S(2)}) async-start(s8[8388608]{0:T(1024)(128)(4,1)} %bitcast.183), calls=%async_computation.15 | async-start | bytes 8388608
  181.3 13.2 %slice-start.1 = ((s8[8388608]{0:T(1024)(128)(4,1)}), s8[4194304]{0:T(1024)(128)(4,1)S(1)}, s32[]{:S(2)}) async-start(s8[8388608]{0:T(1024)(128)(4,1)} %bitcast.183), calls=%async_computation.16 | async-start | bytes 8388608
  194.5 12.0 %copy-start.14 = (f32[1,1,1024]{2,0,1:T(1,128)S(1)}, f32[1,1,1024]{2,0,1:T(1,128)}, u32[]{:S(2)}) copy-start(f32[1,1,1024]{2,0,1:T(1,128)} %copy-done.13) | copy-start | bytes 12292
  194.5 12.0 %copy-start.21 = (f32[1,1,1024]{2,0,1:T(1,128)S(1)}, f32[1,1,1024]{2,0,1:T(1,128)}, u32[]{:S(2)}) copy-start(f32[1,1,1024]{2,0,1:T(1,128)} %copy-done.20) | copy-start | bytes 12292
  204.6 2.0 copy-start.32
  215.3 111.9 %reduce-scatter.9.cloned.1.call-start = ((), (), s32[]{:S(2)}) async-start(), calls=%async_computation.13 | async-start | bytes 25165824 | tf_op jit(solution)/shard_map/reduce_scatter | solution.py:124
  229.1 98.1 %reduce-scatter.11.cloned.1.call-start = ((), (), s32[]{:S(2)}) async-start(), calls=%async_computation.14 | async-start | bytes 25165824 | tf_op jit(solution)/shard_map/reduce_scatter | solution.py:124
  244.1 0.7 copy-start.18
  253.6 35.2 %copy-start.23 = (s32[256,1]{0,1:T(1,128)S(1)}, s32[256,1]{0,1:T(1,128)}, u32[]{:S(2)}) copy-start(s32[256,1]{0,1:T(1,128)} %param.15) | copy-start | bytes 3076
  253.6 35.2 %copy-start.28 = (s32[256]{0:T(256)S(1)}, s32[256]{0:T(256)}, u32[]{:S(2)}) copy-start(s32[256]{0:T(256)} %copy-done.27) | copy-start | bytes 3076
  253.6 35.4 %copy-start.19 = (f32[1024]{0:T(1024)S(1)}, f32[1024]{0:T(1024)}, u32[]{:S(2)}) copy-start(f32[1024]{0:T(1024)} %get-tuple-element.67) | copy-start | bytes 12292
  254.6 59.5 %copy-start.1 = (bf16[256,1024]{1,0:T(8,128)(2,1)S(1)}, bf16[256,1024]{1,0:T(8,128)(2,1)}, u32[]{:S(2)}) copy-start(bf16[256,1024]{1,0:T(8,128)(2,1)} %param.16) | copy-start | bytes 1572868
  254.6 59.4 %copy-start.3 = (bf16[256,1024]{1,0:T(8,128)(2,1)S(1)}, bf16[256,1024]{1,0:T(8,128)(2,1)}, u32[]{:S(2)}) copy-start(bf16[256,1024]{1,0:T(8,128)(2,1)} %param.14) | copy-start | bytes 1572868
  284.3 28.6 %all-to-all-start.1 = ((bf16[16,32,1024]{2,1,0:T(8,128)(2,1)}), bf16[16,32,1024]{2,1,0:T(8,128)(2,1)S(1)}, u32[]{:S(2)}, u32[]{:S(2)}) async-start(bf16[16,32,1024]{2,1,0:T(8,128)(2,1)} %bitcast.146), calls=%async_computation.1 | async-start | bytes 2097152 | tf_op jit(solution)/shard_map/all_to_all | solution.py:92
Sparse Core Ops, SparseCore 0:
  9.6 31.4 all-gather.2
  42.7 31.2 all-gather.4
  171.4 25.4 reduce-scatter.6
  215.4 25.8 reduce-scatter.4
  243.5 27.4 reduce-scatter.8
  273.2 27.5 reduce-scatter.10
where the time goes:
time: 354 us; the launch traced here: 349 us
  matrix products  158 us (45%)
  waiting for transfers between devices  60 us (17%)
  blocking collectives  34.7 us (10%)
  other arithmetic  33.5 us (9%)
  starting transfers between devices  23.9 us (7%)
  local copies, waits for them, and re-layouts  19.6 us (6%)
  between operations  19.4 us (5%)
    dot_general x2, matrix products, on_device(): jnp.dot(lowered, full_first[layer, 0], preferred_element_type=jnp.float32)  51.8 us
    all_to_all x1, blocking collectives, on_device(): lax.all_to_all(drow.reshape(experts, capacity, row_width), 'expert', spli...  29.7 us
    dot_general x2, matrix products, second_term(): lax.dot_general(activated, dsecond, (((0,), (0,)), ((), ())), preferred_e...  28.6 us
    all_to_all x1, waiting for transfers between devices, on_device(): lax.all_to_all(pack_slots(tokens), 'expert', split_axis=0, concat_axis=0,...  24.3 us
    unnamed x4, other arithmetic  23.9 us
    dot_general x2, matrix products, on_device(): jnp.dot(activated, full_second[layer, 0], preferred_element_type=jnp.floa...  21.5 us
    all_to_all x1, waiting for transfers between devices, on_device(): lax.all_to_all(pack_slots(cotangent), 'expert', split_axis=0, concat_axis...  21.1 us
    dot_general x2, matrix products, on_device(): lax.dot_general(dsecond, w_second, (((1,), (1,)), ((), ())), preferred_el...  19.9 us
  transfers between devices with their start and end apart: 10, of which 3 were waited for; matrix products, arithmetic and copies ran while one was open for 40% of the time, Pallas kernels for 0%

commit v1 on v0

v1 whole, which is shorter than its diff:
```python
import jax
import jax.numpy as jnp
from jax import lax
from jax.experimental import pallas as pl
from jax.experimental.pallas import tpu as pltpu
from jax.sharding import PartitionSpec as P

EPS = 1e-05
F32 = jnp.float32
BF16 = jnp.bfloat16
PAD_MARK = 64.0
PAD_LIMIT = 32.0
SWAP = [(0, 1), (1, 0)]


def dot_nn(a, b):
    return lax.dot_general(a, b, (((1,), (0,)), ((), ())), preferred_element_type=F32)


def dot_nt(a, b):
    return lax.dot_general(a, b, (((1,), (1,)), ((), ())), preferred_element_type=F32)


def dot_tn(a, b):
    return lax.dot_general(a, b, (((0,), (0,)), ((), ())), preferred_element_type=F32)


def gelu_and_slope(v):
    e = jnp.exp(v * v * -0.5)
    t = 1.0 / (1.0 + 0.23164189 * jnp.abs(v))
    q = t * (0.127414796 + t * (-0.142248368 + t * (0.7107068705 + t * (-0.7265760135 + t * 0.5307027145))))
    q = q * e
    phi = jnp.where(v >= 0.0, 1.0 - q, q)
    return v * phi, phi + v * (e * 0.3989422804014327)


def params(mib=56):
    return pltpu.CompilerParams(vmem_limit_bytes=mib << 20)


def cost():
    return pl.CostEstimate(flops=0, bytes_accessed=0, transcendentals=0)


def whole(shape):
    return pl.BlockSpec(shape, lambda *_: (0,) * len(shape))


def sds(shape, dtype):
    return jax.ShapeDtypeStruct(shape, dtype)


def slots_kernel(experts, capacity, routes_ref, slot_ref):
    n = routes_ref.shape[0]
    lanes = max(128, experts)
    route = routes_ref[...]
    onehot = route == lax.broadcasted_iota(jnp.int32, (n, lanes), 1)
    hot = jnp.where(onehot, 1.0, 0.0)
    rows = lax.broadcasted_iota(jnp.int32, (n, n), 0)
    cols = lax.broadcasted_iota(jnp.int32, (n, n), 1)
    lower = jnp.where(cols < rows, 1.0, 0.0).astype(BF16)
    earlier = dot_nn(lower, hot.astype(BF16))
    rank = jnp.sum(earlier * hot, axis=1, keepdims=True)
    slot_ref[...] = route * capacity + rank.astype(jnp.int32)


def spread(slot, slots):
    n = slot.shape[0]
    return jnp.where(slot == lax.broadcasted_iota(jnp.int32, (n, slots), 1), 1.0, 0.0)


def pack_kernel(marked, slot_ref, values_ref, out_ref):
    slots = out_ref.shape[0]
    hot = spread(slot_ref[...], slots).astype(BF16)
    packed = dot_tn(hot, values_ref[...])
    out_ref[...] = packed.astype(BF16)
    if marked:
        filled = dot_tn(hot, jnp.ones((hot.shape[0], 128), BF16))
        first = packed[:, :128] + (1.0 - filled) * PAD_MARK
        out_ref[:, :128] = first.astype(BF16)


def pack(marked, slot, values, slots):
    return pl.pallas_call(
        lambda *refs: pack_kernel(marked, *refs),
        out_shape=sds((slots, values.shape[1]), BF16),
        compiler_params=params(),
        cost_estimate=cost(),
        name="pack",
    )(slot, values)


def unpack_kernel(slot_ref, returned_ref, base_ref, out_ref):
    hot = spread(slot_ref[...], returned_ref.shape[0]).astype(BF16)
    picked = dot_nn(hot, returned_ref[...])
    out_ref[...] = (base_ref[...].astype(F32) + picked).astype(BF16)


def unpack(slot, returned, base):
    return pl.pallas_call(
        unpack_kernel,
        out_shape=sds(base.shape, BF16),
        compiler_params=params(),
        cost_estimate=cost(),
        name="unpack",
    )(slot, returned, base)


def norm_stats(h):
    mu = jnp.mean(h, axis=1, keepdims=True)
    c = h - mu
    r = lax.rsqrt(jnp.mean(c * c, axis=1, keepdims=True) + EPS)
    return mu, r, c * r


def ffn_step(low_ref, w_in_ref, b_in_ref, w_out_ref, act_ref, slope_ref, acc_ref):
    hidden = dot_nn(low_ref[...], w_in_ref[...]) + b_in_ref[...].astype(F32)
    act, slope = gelu_and_slope(hidden)
    act = act.astype(BF16)
    act_ref[...] = act
    slope_ref[...] = slope.astype(BF16)
    acc_ref[...] += dot_nn(act, w_out_ref[...])


def first_kernel(
    x_ref, gain_ref, shift_ref, center_ref, w_in_ref, b_in_ref, w_out_ref,
    low_ref, act_ref, slope_ref, part_ref, row_ref, acc_ref,
):
    i = pl.program_id(0)

    @pl.when(i == 0)
    def _():
        x = x_ref[...].astype(F32)
        mu, r, xhat = norm_stats(x)
        low_ref[...] = (xhat * gain_ref[...].astype(F32) + shift_ref[...].astype(F32)).astype(BF16)
        logit = jnp.sum(x * center_ref[...].astype(F32), axis=1, keepdims=True)
        gate = jax.nn.sigmoid(logit)
        live = jnp.where(x[:, :1] < PAD_LIMIT, 1.0, 0.0)
        lane = lax.broadcasted_iota(jnp.int32, row_ref.shape, 1)
        row_ref[...] = jnp.where(
            lane == 0, mu, jnp.where(lane == 1, r, jnp.where(lane == 2, gate, live))
        )
        acc_ref[...] = jnp.zeros_like(acc_ref)

    ffn_step(low_ref, w_in_ref, b_in_ref, w_out_ref, act_ref, slope_ref, acc_ref)

    @pl.when(i == pl.num_programs(0) - 1)
    def _():
        part_ref[...] = acc_ref[...].astype(BF16)


def second_kernel(
    own, x_ref, mine_ref, theirs_ref, bias_ref, gain_ref, shift_ref, last_bias_ref, w_in_ref, b_in_ref, w_out_ref,
    low_ref, act_ref, slope_ref, part_ref, xhat_ref, row_ref, acc_ref,
):
    i = pl.program_id(0)

    @pl.when(i == 0)
    def _():
        h = (
            x_ref[...].astype(F32)
            + bias_ref[...].astype(F32)
            + (mine_ref[...].astype(F32) + theirs_ref[...].astype(F32))
        )
        mu, r, xhat = norm_stats(h)
        low_ref[...] = (xhat * gain_ref[...].astype(F32) + shift_ref[...].astype(F32)).astype(BF16)
        xhat_ref[...] = xhat.astype(BF16)
        row_ref[...] = jnp.broadcast_to(r, row_ref.shape)
        if own:
            acc_ref[...] = h + last_bias_ref[...].astype(F32)
        else:
            acc_ref[...] = jnp.zeros_like(acc_ref)

    ffn_step(low_ref, w_in_ref, b_in_ref, w_out_ref, act_ref, slope_ref, acc_ref)

    @pl.when(i == pl.num_programs(0) - 1)
    def _():
        part_ref[...] = acc_ref[...].astype(part_ref.dtype)


def weight_specs(layer, depth, width, blk):
    w_in = pl.BlockSpec((None, None, depth, blk), lambda i: (layer, 0, 0, i))
    b_in = pl.BlockSpec((None, 1, blk), lambda i: (layer, 0, i))
    w_out = pl.BlockSpec((None, None, blk, depth), lambda i: (layer, 0, i, 0))
    return w_in, b_in, w_out


def vec_spec(layer, depth):
    return pl.BlockSpec((None, 1, depth), lambda i: (layer, 0, 0))


def forward_first(x, gain, shift, center, w_in, b_in, w_out, blk):
    rows, depth = x.shape
    half = w_in.shape[3]
    wi, bi, wo = weight_specs(0, depth, half, blk)
    return pl.pallas_call(
        first_kernel,
        grid=(half // blk,),
        in_specs=[whole(x.shape), vec_spec(0, depth), vec_spec(0, depth), whole(center.shape), wi, bi, wo],
        out_specs=[
            whole(x.shape),
            pl.BlockSpec((rows, blk), lambda i: (0, i)),
            pl.BlockSpec((rows, blk), lambda i: (0, i)),
            whole(x.shape),
            whole((rows, 128)),
        ],
        out_shape=[
            sds(x.shape, BF16),
            sds((rows, half), BF16),
            sds((rows, half), BF16),
            sds(x.shape, BF16),
            sds((rows, 128), F32),
        ],
        scratch_shapes=[pltpu.VMEM(x.shape, F32)],
        compiler_params=params(),
        cost_estimate=cost(),
        name="forward_first",
    )(x, gain, shift, center, w_in, b_in, w_out)


def forward_second(own, x, mine, theirs, bias, gain, shift, w_in, b_in, w_out, blk):
    rows, depth = x.shape
    half = w_in.shape[3]
    wi, bi, wo = weight_specs(1, depth, half, blk)
    return pl.pallas_call(
        lambda *refs: second_kernel(own, *refs),
        grid=(half // blk,),
        in_specs=[
            whole(x.shape), whole(x.shape), whole(x.shape),
            vec_spec(0, depth), vec_spec(1, depth), vec_spec(1, depth), vec_spec(1, depth), wi, bi, wo,
        ],
        out_specs=[
            whole(x.shape),
            pl.BlockSpec((rows, blk), lambda i: (0, i)),
            pl.BlockSpec((rows, blk), lambda i: (0, i)),
            whole(x.shape),
            whole(x.shape),
            whole((rows, 128)),
        ],
        out_shape=[
            sds(x.shape, BF16),
            sds((rows, half), BF16),
            sds((rows, half), BF16),
            sds(x.shape, F32 if own else BF16),
            sds(x.shape, BF16),
            sds((rows, 128), F32),
        ],
        scratch_shapes=[pltpu.VMEM(x.shape, F32)],
        compiler_params=params(),
        cost_estimate=cost(),
        name="forward_second",
    )(x, mine, theirs, bias, gain, shift, bias, w_in, b_in, w_out)


def branch_kernel(part_ref, theirs_ref, row_ref, out_ref, branch_ref):
    out = part_ref[...] + theirs_ref[...].astype(F32)
    out_ref[...] = out
    branch_ref[...] = (row_ref[:, 2:3] * out).astype(BF16)


def gated(part, theirs, row):
    return pl.pallas_call(
        branch_kernel,
        out_shape=[sds(part.shape, F32), sds(part.shape, BF16)],
        compiler_params=params(),
        cost_estimate=cost(),
        name="gated",
    )(part, theirs, row)


def back_step(ds_ref, w_in_ref, w_out_ref, slope_ref, dh_ref, bias_ref, acc_ref):
    dact = dot_nt(ds_ref[...], w_out_ref[...])
    dh = (dact * slope_ref[...].astype(F32)).astype(BF16)
    dh_ref[...] = dh
    bias_ref[...] = jnp.sum(dh.astype(F32), axis=0, keepdims=True)
    acc_ref[...] += dot_nt(dh, w_in_ref[...])


def row_sum(v):
    return jnp.sum(v, axis=0, keepdims=True)


def back_second_kernel(
    dy_ref, row_ref, xhat_ref, w_in_ref, w_out_ref, slope_ref,
    ds_ref, dh_ref, part_ref, sums_ref, bias_ref, acc_ref,
):
    i = pl.program_id(0)

    @pl.when(i == 0)
    def _():
        ds_ref[...] = (row_ref[:, 2:3] * dy_ref[...].astype(F32)).astype(BF16)
        acc_ref[...] = jnp.zeros_like(acc_ref)

    back_step(ds_ref, w_in_ref, w_out_ref, slope_ref, dh_ref, bias_ref, acc_ref)

    @pl.when(i == pl.num_programs(0) - 1)
    def _():
        dn = acc_ref[...]
        part_ref[...] = dn.astype(BF16)
        sums_ref[0:1, :] = row_sum(dn * xhat_ref[...].astype(F32))
        sums_ref[1:2, :] = row_sum(dn)
        sums_ref[2:3, :] = row_sum(ds_ref[...].astype(F32))


def back_first_kernel(
    own, dy_ref, row_ref, mine_ref, theirs_ref, xhat_ref, row1_ref, gain_ref, x_ref, w_in_ref, w_out_ref, slope_ref,
    ds_ref, dh_ref, part_ref, sums_ref, bias_ref, *more,
):
    acc_ref = more[-1]
    i = pl.program_id(0)

    @pl.when(i == 0)
    def _():
        dn = mine_ref[...].astype(F32) + theirs_ref[...].astype(F32)
        dxhat = dn * gain_ref[...].astype(F32)
        xhat = xhat_ref[...].astype(F32)
        m1 = jnp.mean(dxhat, axis=1, keepdims=True)
        m2 = jnp.mean(dxhat * xhat, axis=1, keepdims=True)
        carry = row_ref[:, 2:3] * dy_ref[...].astype(F32) + row1_ref[:, 0:1] * (dxhat - m1 - xhat * m2)
        if own:
            more[0][...] = carry
        ds_ref[...] = carry.astype(BF16)
        acc_ref[...] = jnp.zeros_like(acc_ref)

    back_step(ds_ref, w_in_ref, w_out_ref, slope_ref, dh_ref, bias_ref, acc_ref)

    @pl.when(i == pl.num_programs(0) - 1)
    def _():
        dn = acc_ref[...]
        part_ref[...] = dn.astype(part_ref.dtype)
        xhat = (x_ref[...].astype(F32) - row_ref[:, 0:1]) * row_ref[:, 1:2]
        sums_ref[0:1, :] = row_sum(dn * xhat)
        sums_ref[1:2, :] = row_sum(dn)
        sums_ref[2:3, :] = row_sum(ds_ref[...].astype(F32))


def backward_second(dy, row, xhat, w_in, w_out, slope, blk):
    rows, depth = dy.shape
    half = w_in.shape[3]
    wi, _, wo = weight_specs(1, depth, half, blk)
    by_column = pl.BlockSpec((rows, blk), lambda i: (0, i))
    return pl.pallas_call(
        back_second_kernel,
        grid=(half // blk,),
        in_specs=[whole(dy.shape), whole(row.shape), whole(dy.shape), wi, wo, by_column],
        out_specs=[whole(dy.shape), by_column, whole(dy.shape), whole((8, depth)), pl.BlockSpec((1, blk), lambda i: (0, i))],
        out_shape=[
            sds(dy.shape, BF16),
            sds((rows, half), BF16),
            sds(dy.shape, BF16),
            sds((8, depth), F32),
            sds((1, half), F32),
        ],
        scratch_shapes=[pltpu.VMEM(dy.shape, F32)],
        compiler_params=params(),
        cost_estimate=cost(),
        name="backward_second",
    )(dy, row, xhat, w_in, w_out, slope)


def backward_first(own, dy, row, mine, theirs, xhat, row1, gain, x, w_in, w_out, slope, blk):
    rows, depth = dy.shape
    half = w_in.shape[3]
    wi, _, wo = weight_specs(0, depth, half, blk)
    by_column = pl.BlockSpec((rows, blk), lambda i: (0, i))
    full = whole(dy.shape)
    return pl.pallas_call(
        lambda *refs: back_first_kernel(own, *refs),
        grid=(half // blk,),
        in_specs=[full, whole(row.shape), full, full, full, whole(row.shape), vec_spec(1, depth), full, wi, wo, by_column],
        out_specs=[full, by_column, full, whole((8, depth)), pl.BlockSpec((1, blk), lambda i: (0, i))]
        + ([full] if own else []),
        out_shape=[
            sds(dy.shape, BF16),
            sds((rows, half), BF16),
            sds(dy.shape, F32 if own else BF16),
            sds((8, depth), F32),
            sds((1, half), F32),
        ]
        + ([sds(dy.shape, F32)] if own else []),
        scratch_shapes=[pltpu.VMEM(dy.shape, F32)],
        compiler_params=params(),
        cost_estimate=cost(),
        name="backward_first",
    )(dy, row, mine, theirs, xhat, row1, gain, x, w_in, w_out, slope)


def input_kernel(dy_ref, out_ref, row_ref, x_ref, part_ref, theirs_ref, carry_ref, gain_ref, center_ref, drow_ref, sums_ref):
    x = x_ref[...].astype(F32)
    gate = row_ref[:, 2:3]
    live = row_ref[:, 3:4]
    dgate = jnp.sum(dy_ref[...].astype(F32) * out_ref[...], axis=1, keepdims=True)
    dlogit = dgate * gate * (1.0 - gate)
    dxhat = (part_ref[...] + theirs_ref[...].astype(F32)) * gain_ref[...].astype(F32)
    r = row_ref[:, 1:2]
    xhat = (x - row_ref[:, 0:1]) * r
    m1 = jnp.mean(dxhat, axis=1, keepdims=True)
    m2 = jnp.mean(dxhat * xhat, axis=1, keepdims=True)
    carry = carry_ref[...] + r * (dxhat - m1 - xhat * m2)
    drow_ref[...] = (carry + dlogit * center_ref[...].astype(F32)).astype(BF16)
    sums_ref[0:1, :] = row_sum(dlogit * x)
    sums_ref[1:2, :] = jnp.broadcast_to(row_sum(gate * live), (1, x.shape[1]))
    sums_ref[2:3, :] = jnp.broadcast_to(row_sum(live), (1, x.shape[1]))


def input_gradient(dy, out, row, x, part, theirs, carry, gain, center):
    depth = x.shape[1]
    return pl.pallas_call(
        input_kernel,
        grid=(1,),
        in_specs=[whole(dy.shape), whole(dy.shape), whole(row.shape)] + [whole(dy.shape)] * 4
        + [vec_spec(0, depth), whole(center.shape)],
        out_specs=[whole(dy.shape), whole((8, depth))],
        out_shape=[sds(dy.shape, BF16), sds((8, depth), F32)],
        compiler_params=params(),
        cost_estimate=cost(),
        name="input_gradient",
    )(dy, out, row, x, part, theirs, carry, gain, center)


def weight_kernel(a00_ref, a01_ref, b00_ref, b01_ref, a10_ref, a11_ref, b10_ref, b11_ref, out_ref):
    layer = pl.program_id(0)

    @pl.when(layer == 0)
    def _():
        out_ref[...] = dot_tn(a00_ref[...], b00_ref[...]) + dot_tn(a01_ref[...], b01_ref[...])

    @pl.when(layer == 1)
    def _():
        out_ref[...] = dot_tn(a10_ref[...], b10_ref[...]) + dot_tn(a11_ref[...], b11_ref[...])


def weight_gradient(layers, blk):
    rows, left = layers[0][0][0].shape
    right = layers[0][1][0].shape[1]
    steps = left // blk
    last = steps - 1
    in0_a = pl.BlockSpec((rows, blk), lambda k, i: (0, jnp.where(k == 0, i, last)))
    in1_a = pl.BlockSpec((rows, blk), lambda k, i: (0, jnp.where(k == 1, i, 0)))
    b = whole((rows, right))
    args = [*layers[0][0], *layers[0][1], *layers[1][0], *layers[1][1]]
    return pl.pallas_call(
        weight_kernel,
        grid=(2, steps),
        in_specs=[in0_a, in0_a, b, b, in1_a, in1_a, b, b],
        out_specs=pl.BlockSpec((None, None, blk, right), lambda k, i: (k, 0, i, 0)),
        out_shape=sds((2, 1, left, right), F32),
        compiler_params=params(),
        cost_estimate=cost(),
        name="weight_gradient",
    )(*args)


def on_device(tokens, routes, cotangent, ln_gain, ln_shift, w_in, b_in, w_out, b_out, centroid):
    experts = lax.axis_size("expert")
    replicas = lax.axis_size("replica")
    here = lax.axis_index("replica")
    tok_dev, depth = tokens.shape
    half = w_in.shape[3]
    capacity = 2 * tok_dev // experts
    slots = experts * capacity
    blk = 512

    def exchange(v):
        moved = lax.all_to_all(
            v.reshape(experts, capacity, depth), "expert", split_axis=0, concat_axis=0, tiled=True
        )
        return moved.reshape(slots, depth)

    def swap(v):
        return lax.ppermute(v, "replica", SWAP)

    slot = pl.pallas_call(
        lambda *refs: slots_kernel(experts, capacity, *refs),
        out_shape=sds((tok_dev, 1), jnp.int32),
        compiler_params=params(),
        cost_estimate=cost(),
        name="slots",
    )(routes)
    b_half = lax.dynamic_slice_in_dim(b_in, here * half, half, axis=2)
    x_own = exchange(pack(True, slot, tokens, slots))
    x_par = swap(x_own)
    sent_cot = pack(False, slot, cotangent, slots)
    sent_cot, x_own = lax.optimization_barrier((sent_cot, x_own))
    dy_own = exchange(sent_cot)

    def first(x):
        return forward_first(x, ln_gain, ln_shift, centroid, w_in, b_half, w_out, blk)

    low0_own, act0_own, slope0_own, p0_own, row_own = first(x_own)
    p0_own_there = swap(p0_own)
    low0_par, act0_par, slope0_par, p0_par, row_par = first(x_par)
    p0_par_there = swap(p0_par)

    def second(own, x, mine, theirs):
        return forward_second(own, x, mine, theirs, b_out, ln_gain, ln_shift, w_in, b_half, w_out, blk)

    low1_par, act1_par, slope1_par, p1_par, xhat1_par, row1_par = second(False, x_par, p0_par, p0_own_there)
    p1_there = swap(p1_par)
    low1_own, act1_own, slope1_own, p1_own, xhat1_own, row1_own = second(True, x_own, p0_own, p0_par_there)
    out, branch = gated(p1_own, p1_there, row_own)
    branch, dy_own = lax.optimization_barrier((branch, dy_own))
    returned = exchange(branch)
    dy_par = swap(dy_own)

    ds1_own, dh1_own, n1_own, sums1_own, bias1_own = backward_second(
        dy_own, row_own, xhat1_own, w_in, w_out, slope1_own, blk
    )
    n1_own_there = swap(n1_own)
    ds1_par, dh1_par, n1_par, sums1_par, bias1_par = backward_second(
        dy_par, row_par, xhat1_par, w_in, w_out, slope1_par, blk
    )
    n1_par_there = swap(n1_par)
    ds0_par, dh0_par, n0_par, sums0_par, bias0_par = backward_first(
        False, dy_par, row_par, n1_par, n1_own_there, xhat1_par, row1_par, ln_gain, x_par, w_in, w_out, slope0_par, blk
    )
    n0_there = swap(n0_par)
    ds0_own, dh0_own, n0_own, sums0_own, bias0_own, carry_own = backward_first(
        True, dy_own, row_own, n1_own, n1_par_there, xhat1_own, row1_own, ln_gain, x_own, w_in, w_out, slope0_own, blk
    )
    drow, sums_in = input_gradient(
        dy_own, out, row_own, x_own, n0_own, n0_there, carry_own, ln_gain, centroid
    )
    drow, returned = lax.optimization_barrier((drow, returned))
    grad_returned = exchange(drow)

    grad_out = weight_gradient(
        [((act0_own, act0_par), (ds0_own, ds0_par)), ((act1_own, act1_par), (ds1_own, ds1_par))], 512
    )
    grad_in = weight_gradient(
        [((low0_own, low0_par), (dh0_own, dh0_par)), ((low1_own, low1_par), (dh1_own, dh1_par))], 256
    )
    mixed = unpack(slot, returned, tokens)

    sums0 = sums0_own + sums0_par
    sums1 = sums1_own + sums1_par
    bias = jnp.concatenate([bias0_own + bias0_par, bias1_own + bias1_par])
    local = jnp.concatenate([sums0, sums1, sums_in, bias.reshape(-1, depth)], axis=0)
    other = swap(local)
    total = local + other
    others_bias = other[24:].reshape(2, half)
    grad_b_in = jnp.where(
        here == 0,
        jnp.concatenate([bias, others_bias], axis=1),
        jnp.concatenate([others_bias, bias], axis=1),
    )
    grad_b_out = jnp.stack([sums0[2], sums1[2]])
    grad_gain = jnp.stack([total[0], total[8]])
    grad_shift = jnp.stack([total[1], total[9]])
    gate_total = total[17, :1]
    count_total = total[18, :1]
    grad_tokens = unpack(slot, grad_returned, cotangent)
    return (
        mixed,
        grad_tokens,
        grad_in,
        grad_out,
        grad_b_in[:, None],
        grad_b_out[:, None],
        grad_gain[:, None],
        grad_shift[:, None],
        total[16][None],
        gate_total / count_total,
        count_total / (tok_dev * replicas),
    )


def solution(mesh):
    rows = P(("expert", "replica"), None)
    by_expert = P(None, "expert", None)
    first_weight = P(None, "expert", None, "replica")
    second_weight = P(None, "expert", "replica", None)
    return jax.shard_map(
        on_device,
        mesh=mesh,
        in_specs=(
            rows, rows, rows, by_expert, by_expert, first_weight, by_expert, second_weight, by_expert,
            P("expert", None),
        ),
        out_specs=(
            rows, rows, first_weight, second_weight, by_expert, by_expert, by_expert, by_expert,
            P("expert", None), P("expert"), P("expert"),
        ),
        check_vma=False,
    )
```

time: 354 us -> 234 us (0.66)
  Pallas kernels: 0 us -> 161 us
  matrix products: 158 us -> 0 us
  waiting for transfers between devices: 60 us -> 21.1 us
  blocking collectives: 34.7 us -> 0 us
  other arithmetic: 33.5 us -> 0.14 us
  between operations: 19.4 us -> 5.32 us
    pallas_call x0 -> x17, Pallas kernels: none -> 161 us  [the longest x2 33 us: weight_gradient(): pl.pallas_call(weight_kernel, grid=(2, steps), in_specs=[in0_a, in0_a, b,...]
    dot_general x13 -> x0, matrix products: 158 us -> none  [the longest x2 51.8 us: on_device(): jnp.dot(lowered, full_first[layer, 0], preferred_element_type=jnp.float32)]
    all_to_all x4, waiting for transfers between devices: 58.5 us -> 21.1 us  [exchange(): lax.all_to_all(v.reshape(experts, capacity, depth), 'expert', split_axis=...]
    all_to_all x1 -> x0, blocking collectives: 29.7 us -> none  [on_device(): lax.all_to_all(drow.reshape(experts, capacity, row_width), 'expert', spli...]
    unnamed x4 -> x0, other arithmetic: 23.9 us -> none
    unnamed x70 -> x57, local copies, waits for them, and re-layouts: 5.62 us -> 15.3 us
    gather x4 -> x0, local copies, waits for them, and re-layouts: 8.46 us -> none  [the longest x2 4.34 us: unpack_slots(): jnp.take(returned.reshape(slot_count, row_width), slot_ids, axis=0)]
    psum x1 -> x0, blocking collectives: 5.05 us -> none  [on_device(): lax.psum((jnp.stack(grads_gain), jnp.stack(grads_shift), jnp.stack(grads_...]
  transfers between devices with their start and end apart: 10 -> 13, of which waited for: 3 -> 1; matrix products, arithmetic and copies ran while one was open for 40% -> 3% of each run, Pallas kernels for 0% -> 66%
where the time goes in v1:
time: 234 us; the launch traced here: 231 us
  Pallas kernels  161 us (69%)
  starting transfers between devices  27.4 us (12%)
  waiting for transfers between devices  21.1 us (9%)
  local copies, waits for them, and re-layouts  16.5 us (7%)
  between operations  5.32 us (2%)
    pallas_call x2, Pallas kernels, weight_gradient(): pl.pallas_call(weight_kernel, grid=(2, steps), in_specs=[in0_a, in0_a, b,...  33 us
    pallas_call x2, Pallas kernels, forward_second(): pl.pallas_call(lambda *refs: second_kernel(own, *refs), grid=(half // blk...  28.5 us
    pallas_call x2, Pallas kernels, backward_first(): pl.pallas_call(lambda *refs: back_first_kernel(own, *refs), grid=(half //...  28.1 us
    all_to_all x4, starting transfers between devices, exchange(): lax.all_to_all(v.reshape(experts, capacity, depth), 'expert', split_axis=...  26 us
    pallas_call x2, Pallas kernels, forward_first(): pl.pallas_call(first_kernel, grid=(half // blk,), in_specs=[whole(x.shape...  25.9 us
    pallas_call x2, Pallas kernels, backward_second(): pl.pallas_call(back_second_kernel, grid=(half // blk,), in_specs=[whole(d...  22.3 us
    all_to_all x4, waiting for transfers between devices, exchange(): lax.all_to_all(v.reshape(experts, capacity, depth), 'expert', split_axis=...  21.1 us
    unnamed x57, local copies, waits for them, and re-layouts  15.3 us
  transfers between devices with their start and end apart: 13, of which 1 were waited for; matrix products, arithmetic and copies ran while one was open for 3% of the time, Pallas kernels for 66%

profile of v1, /device:TPU:8, one launch (start us, length us, event | category | flops | bytes accessed | tf_op | source)
XLA Modules:
  0.0 231.4 jit_solution(16630111062172614986)
XLA Ops:
  0.7 1.5 copy.21.refs_0_
  2.2 1.9 slots.1.refs_0_.slot_ref
  4.1 2.7 %pack.3 = bf16[512,1024]{1,0:T(8,128)(2,1)} custom-call(s32[256,1]{1,0:T(8,128)} %slots.1.refs_0_.slot_ref, bf16[256,1024]{1,0:T(8,128)(2,1)} %base_ref.2), custom_call_target="tpu_custom_call" | custom-call | tf_op jit(solution)/shard_map/pack/pallas_call | solution.py:84
  6.8 7.2 %all-to-all-start = ((bf16[16,32,1024]{2,1,0:T(8,128)(2,1)}), bf16[16,32,1024]{2,1,0:T(8,128)(2,1)S(1)}, u32[]{:S(2)}, u32[]{:S(2)}) async-start(bf16[16,32,1024]{2,1,0:T(8,128)(2,1)} %bitcast.30), calls=%async_computation | async-start | bytes 2097152 | tf_op jit(solution)/shard_map/all_to_all | solution.py:465
  14.0 0.6 copy.23.gain_ref.refs_4_.refs_6_
  14.6 0.6 copy.42.b_in_ref.refs_8_
  15.3 0.6 copy.24.shift_ref.refs_5_
  15.9 2.6 %pack.2 = bf16[512,1024]{1,0:T(8,128)(2,1)} custom-call(s32[256,1]{1,0:T(8,128)} %slots.1.refs_0_.slot_ref, bf16[256,1024]{1,0:T(8,128)(2,1)} %base_ref.3), custom_call_target="tpu_custom_call" | custom-call | tf_op jit(solution)/shard_map/pack/pallas_call | solution.py:84
  18.5 21.0 %all-to-all-done = bf16[16,32,1024]{2,1,0:T(8,128)(2,1)S(1)} async-done(((bf16[16,32,1024]{2,1,0:T(8,128)(2,1)}), bf16[16,32,1024]{2,1,0:T(8,128)(2,1)S(1)}, u32[]{:S(2)}, u32[]{:S(2)}) %all-to-all-start) | async-done | bytes 1048608 | tf_op jit(solution)/shard_map/all_to_all | solution.py:465
  39.5 1.0 copy-done.2
  40.6 13.0 %forward_first.2 = (bf16[512,1024]{1,0:T(8,128)(2,1)}, bf16[512,2048]{1,0:T(8,128)(2,1)}, bf16[512,2048]{1,0:T(8,128)(2,1)}, bf16[512,1024]{1,0:T(8,128)(2,1)}, f32[512,128]{1,0:T(8,128)}) custom-call(bf16[512,1024]{1,0:T(8,128)(2,1)} %bitcast.19, bf16[2,1,1024]{2,1,0:T(2,128)(2,1)} %copy.23.gain_ref.refs_4_.refs_6_, ...), custom_call_target="tpu_custom_call" | custom-call | tf_op jit(solution)/shard_map/forward_first/pallas_call | solution.py:196
  53.6 0.1 collective-permute-start.2
  53.6 4.7 %all-to-all-start.1 = ((bf16[16,32,1024]{2,1,0:T(8,128)(2,1)}), bf16[16,32,1024]{2,1,0:T(8,128)(2,1)S(1)}, u32[]{:S(2)}, u32[]{:S(2)}) async-start(bf16[16,32,1024]{2,1,0:T(8,128)(2,1)} %bitcast.29), calls=%async_computation.1 | async-start | bytes 2097152 | tf_op jit(solution)/shard_map/all_to_all | solution.py:465
  58.4 0.6 copy.27.refs_3_.refs_6_
  59.0 1.0 copy-done.4
  60.0 13.0 %forward_first.3 = (bf16[512,1024]{1,0:T(8,128)(2,1)}, bf16[512,2048]{1,0:T(8,128)(2,1)}, bf16[512,2048]{1,0:T(8,128)(2,1)}, bf16[512,1024]{1,0:T(8,128)(2,1)}, f32[512,128]{1,0:T(8,128)}) custom-call(bf16[512,1024]{1,0:T(8,128)(2,1)} %copy-done.4, bf16[2,1,1024]{2,1,0:T(2,128)(2,1)} %copy.23.gain_ref.refs_4_.refs_6_, ...), custom_call_target="tpu_custom_call" | custom-call | tf_op jit(solution)/shard_map/forward_first/pallas_call | solution.py:196
  73.0 14.1 %forward_second.3 = (bf16[512,1024]{1,0:T(8,128)(2,1)}, bf16[512,2048]{1,0:T(8,128)(2,1)}, bf16[512,2048]{1,0:T(8,128)(2,1)}, bf16[512,1024]{1,0:T(8,128)(2,1)},...) custom-call(bf16[512,1024]{1,0:T(8,128)(2,1)} %copy-done.4, bf16[512,1024]{1,0:T(8,128)(2,1)} %get-tuple-element.66.refs_1_, ...), custom_call_target="tpu_custom_call" | custom-call | tf_op jit(solution)/shard_map/forward_second/pallas_call | solution.py:225
  87.1 0.5 collective-permute-start.3
  87.7 1.0 copy-done.9
  88.7 14.4 %forward_second.2 = (bf16[512,1024]{1,0:T(8,128)(2,1)}, bf16[512,2048]{1,0:T(8,128)(2,1)}, bf16[512,2048]{1,0:T(8,128)(2,1)}, f32[512,1024]{1,0:T(8,128)}, bf16[...) custom-call(bf16[512,1024]{1,0:T(8,128)(2,1)} %bitcast.20, bf16[512,1024]{1,0:T(8,128)(2,1)} %get-tuple-element.65.refs_1_, ...), custom_call_target="tpu_custom_call" | custom-call | tf_op jit(solution)/shard_map/forward_second/pallas_call | solution.py:225
  103.1 1.0 copy-done.11
  104.1 3.9 %gated.1 = (f32[512,1024]{1,0:T(8,128)}, bf16[512,1024]{1,0:T(8,128)(2,1)}) custom-call(f32[512,1024]{1,0:T(8,128)} %get-tuple-element.67.part_ref, bf16[512,1024]{1,0:T(8,128)(2,1)} %copy-done.11, f32[512,128]{1,0:T(8,128)} %get-tuple-element.69.row_ref.refs_1_), custom_call_target="tpu_custom_call" | custom-call | tf_op jit(solution)/shard_map/gated/pallas_call | solution.py:262
  108.0 0.9 copy-done.3
  108.9 11.1 %backward_second.2 = (bf16[512,1024]{1,0:T(8,128)(2,1)}, bf16[512,2048]{1,0:T(8,128)(2,1)}, bf16[512,1024]{1,0:T(8,128)(2,1)}, f32[8,1024]{1,0:T(8,128)}, f32[1,2048]{1,0:T(1,128)}) custom-call(bf16[512,1024]{1,0:T(8,128)(2,1)} %bitcast.24, f32[512,128]{1,0:T(8,128)} %get-tuple-element.69.row_ref.refs_1_, ...), custom_call_target="tpu_custom_call" | custom-call | tf_op jit(solution)/shard_map/backward_second/pallas_call | solution.py:342
  120.1 0.1 collective-permute-start.6
  120.1 6.9 %all-to-all-start.2 = ((bf16[16,32,1024]{2,1,0:T(8,128)(2,1)}), bf16[16,32,1024]{2,1,0:T(8,128)(2,1)S(1)}, u32[]{:S(2)}, u32[]{:S(2)}) async-start(bf16[16,32,1024]{2,1,0:T(8,128)(2,1)} %bitcast.32), calls=%async_computation.2 | async-start | bytes 2097152 | tf_op jit(solution)/shard_map/all_to_all | solution.py:465
  127.1 1.0 copy-done.7
  128.0 11.1 %backward_second.3 = (bf16[512,1024]{1,0:T(8,128)(2,1)}, bf16[512,2048]{1,0:T(8,128)(2,1)}, bf16[512,1024]{1,0:T(8,128)(2,1)}, f32[8,1024]{1,0:T(8,128)}, f32[1,2048]{1,0:T(1,128)}) custom-call(bf16[512,1024]{1,0:T(8,128)(2,1)} %copy-done.7, f32[512,128]{1,0:T(8,128)} %get-tuple-element.77.row_ref.refs_1_, ...), custom_call_target="tpu_custom_call" | custom-call | tf_op jit(solution)/shard_map/backward_second/pallas_call | solution.py:342
  139.2 0.1 collective-permute-start.5
  139.3 13.6 %backward_first.3 = (bf16[512,1024]{1,0:T(8,128)(2,1)}, bf16[512,2048]{1,0:T(8,128)(2,1)}, bf16[512,1024]{1,0:T(8,128)(2,1)}, f32[8,1024]{1,0:T(8,128)}, f32[1,2048]{1,0:T(1,128)}) custom-call(bf16[512,1024]{1,0:T(8,128)(2,1)} %copy-done.7, f32[512,128]{1,0:T(8,128)} %get-tuple-element.77.row_ref.refs_1_, bf16[512,1024]{1,0:T(8,128)(2,1)} %get-tuple-element.80.refs_2_, ...), custom_call_target="tpu_custom_call" | custom-call | tf_op jit(solution)/shard_map/backward_first/pallas_call | solution.py:367
  152.8 0.5 collective-permute-start.7
  153.4 1.0 copy-done.8
  154.4 14.6 %backward_first.2 = (bf16[512,1024]{1,0:T(8,128)(2,1)}, bf16[512,2048]{1,0:T(8,128)(2,1)}, f32[512,1024]{1,0:T(8,128)}, f32[8,1024]{1,0:T(8,128)}, f32[1,2048]{1,0:T(1,128)}, /*index=5*/f32[512,1024]{1,0:T(8,128)}) custom-call(bf16[512,1024]{1,0:T(8,128)(2,1)} %bitcast.25, f32[512,128]{1,0:T(8,128)} %get-tuple-element.69.row_ref.refs_1_, ...), custom_call_target="tpu_custom_call" | custom-call | tf_op jit(solution)/shard_map/backward_first/pallas_call | solution.py:367
  168.9 1.0 copy-done.10
  169.9 6.7 %input_gradient.1 = (bf16[512,1024]{1,0:T(8,128)(2,1)}, f32[8,1024]{1,0:T(8,128)}) custom-call(bf16[512,1024]{1,0:T(8,128)(2,1)} %bitcast.26, f32[512,1024]{1,0:T(8,128)} %get-tuple-element.73.out_ref, f32[512,128]{1,0:T(8,128)} %get-tuple-element.69.row_ref.refs_1_, bf16[512,1024]{1,0:T(8,128)(2,1)} %bitcast.22, f32[512,1024]{1,0:T(8,128)} %get-tuple-element.83.part_ref, ...), custom_call_target="tpu_custom_call" | custom-call | tf_op jit(solution)/shard_map/input_gradient/pallas_call | solution.py:408
  176.7 7.1 %all-to-all-start.3 = ((bf16[16,32,1024]{2,1,0:T(8,128)(2,1)}), bf16[16,32,1024]{2,1,0:T(8,128)(2,1)S(1)}, u32[]{:S(2)}, u32[]{:S(2)}) async-start(bf16[16,32,1024]{2,1,0:T(8,128)(2,1)} %bitcast.31), calls=%async_computation.3 | async-start | bytes 2097152 | tf_op jit(solution)/shard_map/all_to_all | solution.py:465
  184.0 0.1 collective-permute-start.8
  184.1 2.7 %unpack.2 = bf16[256,1024]{1,0:T(8,128)(2,1)} custom-call(s32[256,1]{1,0:T(8,128)} %slots.1.refs_0_.slot_ref, bf16[512,1024]{1,0:T(8,128)(2,1)} %bitcast.28, bf16[256,1024]{1,0:T(8,128)(2,1)} %base_ref.2), custom_call_target="tpu_custom_call" | custom-call | tf_op jit(solution)/shard_map/unpack/pallas_call | solution.py:100
  186.8 0.6 copy.39
  187.4 16.8 %weight_gradient.3 = f32[2,1,2048,1024]{3,2,1,0:T(8,128)} custom-call(bf16[512,2048]{1,0:T(8,128)(2,1)} %get-tuple-element.100.a00_ref, bf16[512,2048]{1,0:T(8,128)(2,1)} %get-tuple-element.101.a01_ref, bf16[512,1024]{1,0:T(8,128)(2,1)} %get-tuple-element.102.b00_ref, bf16[512,1024]{1,0:T(8,128)(2,1)} %get-tuple-element.103.b01_ref, ...), custom_call_target="tpu_custom_call" | custom-call | tf_op jit(solution)/shard_map/weight_gradient/pallas_call | solution.py:442
  204.2 16.2 %weight_gradient.2 = f32[2,1,1024,2048]{3,2,1,0:T(8,128)} custom-call(bf16[512,1024]{1,0:T(8,128)(2,1)} %get-tuple-element.92.a00_ref, bf16[512,1024]{1,0:T(8,128)(2,1)} %get-tuple-element.93.a01_ref, bf16[512,2048]{1,0:T(8,128)(2,1)} %get-tuple-element.94.b00_ref, bf16[512,2048]{1,0:T(8,128)(2,1)} %get-tuple-element.95.b01_ref, ...), custom_call_target="tpu_custom_call" | custom-call | tf_op jit(solution)/shard_map/weight_gradient/pallas_call | solution.py:442
  220.5 0.6 copy.38
  221.2 0.5 fusion.2
  223.7 0.6 fusion.3
  224.3 0.6 copy.40
  224.9 0.6 copy.41
  225.5 1.0 copy-done.5
  226.5 2.7 %unpack.3 = bf16[256,1024]{1,0:T(8,128)(2,1)} custom-call(s32[256,1]{1,0:T(8,128)} %slots.1.refs_0_.slot_ref, bf16[512,1024]{1,0:T(8,128)(2,1)} %bitcast.27, bf16[256,1024]{1,0:T(8,128)(2,1)} %base_ref.3), custom_call_target="tpu_custom_call" | custom-call | tf_op jit(solution)/shard_map/unpack/pallas_call | solution.py:100
  (70 shorter events, 0.4 us)
Async XLA Ops:
  0.6 14.0 %copy-start = (bf16[2,1,4096]{2,0,1:T(2,128)(2,1)S(1)}, bf16[2,1,4096]{2,0,1:T(2,128)(2,1)}, u32[]{:S(2)}) copy-start(bf16[2,1,4096]{2,0,1:T(2,128)(2,1)} %param.16) | copy-start | bytes 49156
  0.7 13.3 %copy-start.21 = (bf16[2,1,1024]{2,0,1:T(2,128)(2,1)S(1)}, bf16[2,1,1024]{2,0,1:T(2,128)(2,1)}, u32[]{:S(2)}) copy-start(bf16[2,1,1024]{2,0,1:T(2,128)(2,1)} %param.13) | copy-start | bytes 12292
  2.2 13.1 %copy-start.22 = (bf16[2,1,1024]{2,0,1:T(2,128)(2,1)S(1)}, bf16[2,1,1024]{2,0,1:T(2,128)(2,1)}, u32[]{:S(2)}) copy-start(bf16[2,1,1024]{2,0,1:T(2,128)(2,1)} %param.14) | copy-start | bytes 12292
  6.8 32.8 %all-to-all-start = ((bf16[16,32,1024]{2,1,0:T(8,128)(2,1)}), bf16[16,32,1024]{2,1,0:T(8,128)(2,1)S(1)}, u32[]{:S(2)}, u32[]{:S(2)}) async-start(bf16[16,32,1024]{2,1,0:T(8,128)(2,1)} %bitcast.30), calls=%async_computation | async-start | bytes 2097152 | tf_op jit(solution)/shard_map/all_to_all | solution.py:465
  39.5 1.0 copy-start.2
  39.5 19.4 %collective-permute-start = (bf16[512,1024]{1,0:T(8,128)(2,1)S(1)}, bf16[512,1024]{1,0:T(8,128)(2,1)S(1)}, u32[]{:S(2)}, u32[]{:S(2)}) collective-permute-start(bf16[512,1024]{1,0:T(8,128)(2,1)S(1)} %bitcast.18), channel_id=1, source_target_pairs={{0,1},{1,0},{2,3},{3,2},{4,5},{5,4},{6,7},{7,6},{8,9},{9,8},{10,11... | collective-permute-start | bytes 3145736 | tf_op jit(solution)/shard_map/ppermute | solution.py:471
  53.5 4.8 %copy-start.23 = (bf16[2,1,1024]{2,0,1:T(2,128)(2,1)S(1)}, bf16[2,1,1024]{2,0,1:T(2,128)(2,1)}, u32[]{:S(2)}) copy-start(bf16[2,1,1024]{2,0,1:T(2,128)(2,1)} %param.18) | copy-start | bytes 12292
  53.6 19.5 %collective-permute-start.2 = (bf16[512,1024]{1,0:T(8,128)(2,1)}, bf16[512,1024]{1,0:T(8,128)(2,1)}, u32[]{:S(2)}, u32[]{:S(2)}) collective-permute-start(bf16[512,1024]{1,0:T(8,128)(2,1)} %get-tuple-element.65.refs_1_), channel_id=1, source_target_pairs={{0,1},{1,0},{2,3},{3,2},{4,5},{5,4},{6,7},{7,6},{8,9},{9,8},{10,11... | collective-permute-start | bytes 3145736 | tf_op jit(solution)/shard_map/ppermute | solution.py:471
  53.6 54.3 %all-to-all-start.1 = ((bf16[16,32,1024]{2,1,0:T(8,128)(2,1)}), bf16[16,32,1024]{2,1,0:T(8,128)(2,1)S(1)}, u32[]{:S(2)}, u32[]{:S(2)}) async-start(bf16[16,32,1024]{2,1,0:T(8,128)(2,1)} %bitcast.29), calls=%async_computation.1 | async-start | bytes 2097152 | tf_op jit(solution)/shard_map/all_to_all | solution.py:465
  59.0 1.0 copy-start.4
  73.0 14.7 %collective-permute-start.1 = (bf16[512,1024]{1,0:T(8,128)(2,1)}, bf16[512,1024]{1,0:T(8,128)(2,1)S(1)}, u32[]{:S(2)}, u32[]{:S(2)}) collective-permute-start(bf16[512,1024]{1,0:T(8,128)(2,1)} %get-tuple-element.66.refs_1_), channel_id=1, source_target_pairs={{0,1},{1,0},{2,3},{3,2},{4,5},{5,4},{6,7},{7,6},{8,9},{9,8},{10,11... | collective-permute-start | bytes 3145736 | tf_op jit(solution)/shard_map/ppermute | solution.py:471
  87.1 16.0 %collective-permute-start.3 = (bf16[512,1024]{1,0:T(8,128)(2,1)}, bf16[512,1024]{1,0:T(8,128)(2,1)S(1)}, u32[]{:S(2)}, u32[]{:S(2)}) collective-permute-start(bf16[512,1024]{1,0:T(8,128)(2,1)} %get-tuple-element.68), channel_id=1, source_target_pairs={{0,1},{1,0},{2,3},{3,2},{4,5},{5,4},{6,7},{7,6},{8,9},{9,8},{10,11... | collective-permute-start | bytes 3145736 | tf_op jit(solution)/shard_map/ppermute | solution.py:471
  87.7 1.0 copy-start.9
  103.1 1.0 copy-start.11
  108.0 1.0 copy-start.3
  108.0 19.1 %collective-permute-start.4 = (bf16[512,1024]{1,0:T(8,128)(2,1)S(1)}, bf16[512,1024]{1,0:T(8,128)(2,1)S(1)}, u32[]{:S(2)}, u32[]{:S(2)}) collective-permute-start(bf16[512,1024]{1,0:T(8,128)(2,1)S(1)} %bitcast.23), channel_id=1, source_target_pairs={{0,1},{1,0},{2,3},{3,2},{4,5},{5,4},{6,7},{7,6},{8,9},{9,8},{10,11... | collective-permute-start | bytes 3145736 | tf_op jit(solution)/shard_map/ppermute | solution.py:471
  120.1 19.2 %collective-permute-start.6 = (bf16[512,1024]{1,0:T(8,128)(2,1)}, bf16[512,1024]{1,0:T(8,128)(2,1)}, u32[]{:S(2)}, u32[]{:S(2)}) collective-permute-start(bf16[512,1024]{1,0:T(8,128)(2,1)} %get-tuple-element.76.refs_2_), channel_id=1, source_target_pairs={{0,1},{1,0},{2,3},{3,2},{4,5},{5,4},{6,7},{7,6},{8,9},{9,8},{10,11... | collective-permute-start | bytes 3145736 | tf_op jit(solution)/shard_map/ppermute | solution.py:471
  120.1 56.5 %all-to-all-start.2 = ((bf16[16,32,1024]{2,1,0:T(8,128)(2,1)}), bf16[16,32,1024]{2,1,0:T(8,128)(2,1)S(1)}, u32[]{:S(2)}, u32[]{:S(2)}) async-start(bf16[16,32,1024]{2,1,0:T(8,128)(2,1)} %bitcast.32), calls=%async_computation.2 | async-start | bytes 2097152 | tf_op jit(solution)/shard_map/all_to_all | solution.py:465
  127.1 1.0 copy-start.7
  139.2 14.2 %collective-permute-start.5 = (bf16[512,1024]{1,0:T(8,128)(2,1)}, bf16[512,1024]{1,0:T(8,128)(2,1)S(1)}, u32[]{:S(2)}, u32[]{:S(2)}) collective-permute-start(bf16[512,1024]{1,0:T(8,128)(2,1)} %get-tuple-element.80.refs_2_), channel_id=1, source_target_pairs={{0,1},{1,0},{2,3},{3,2},{4,5},{5,4},{6,7},{7,6},{8,9},{9,8},{10,11... | collective-permute-start | bytes 3145736 | tf_op jit(solution)/shard_map/ppermute | solution.py:471
  152.8 16.1 %collective-permute-start.7 = (bf16[512,1024]{1,0:T(8,128)(2,1)}, bf16[512,1024]{1,0:T(8,128)(2,1)S(1)}, u32[]{:S(2)}, u32[]{:S(2)}) collective-permute-start(bf16[512,1024]{1,0:T(8,128)(2,1)} %get-tuple-element.86), channel_id=1, source_target_pairs={{0,1},{1,0},{2,3},{3,2},{4,5},{5,4},{6,7},{7,6},{8,9},{9,8},{10,11... | collective-permute-start | bytes 3145736 | tf_op jit(solution)/shard_map/ppermute | solution.py:471
  153.4 1.0 copy-start.8
  168.9 1.0 copy-start.10
  176.6 7.2 %copy-start.13 = (f32[8,1024]{1,0:T(8,128)S(1)}, f32[8,1024]{1,0:T(8,128)}, u32[]{:S(2)}) copy-start(f32[8,1024]{1,0:T(8,128)} %get-tuple-element.114) | copy-start | bytes 98308
  176.6 7.2 %copy-start.14 = (f32[8,1024]{1,0:T(8,128)S(1)}, f32[8,1024]{1,0:T(8,128)}, u32[]{:S(2)}) copy-start(f32[8,1024]{1,0:T(8,128)} %get-tuple-element.115) | copy-start | bytes 98308
  176.6 7.2 %copy-start.17 = (f32[1,2048]{1,0:T(1,128)S(1)}, f32[1,2048]{1,0:T(1,128)}, u32[]{:S(2)}) copy-start(f32[1,2048]{1,0:T(1,128)} %get-tuple-element.110) | copy-start | bytes 24580
  176.6 7.2 %copy-start.18 = (f32[1,2048]{1,0:T(1,128)S(1)}, f32[1,2048]{1,0:T(1,128)}, u32[]{:S(2)}) copy-start(f32[1,2048]{1,0:T(1,128)} %get-tuple-element.111) | copy-start | bytes 24580
  176.6 7.2 %copy-start.19 = (f32[1,2048]{1,0:T(1,128)S(1)}, f32[1,2048]{1,0:T(1,128)}, u32[]{:S(2)}) copy-start(f32[1,2048]{1,0:T(1,128)} %get-tuple-element.109) | copy-start | bytes 24580
  176.6 7.2 %copy-start.20 = (f32[1,2048]{1,0:T(1,128)S(1)}, f32[1,2048]{1,0:T(1,128)}, u32[]{:S(2)}) copy-start(f32[1,2048]{1,0:T(1,128)} %get-tuple-element.108) | copy-start | bytes 24580
  176.6 7.3 %copy-start.15 = (f32[8,1024]{1,0:T(8,128)S(1)}, f32[8,1024]{1,0:T(8,128)}, u32[]{:S(2)}) copy-start(f32[8,1024]{1,0:T(8,128)} %get-tuple-element.113) | copy-start | bytes 98308
  176.7 7.3 %copy-start.16 = (f32[8,1024]{1,0:T(8,128)S(1)}, f32[8,1024]{1,0:T(8,128)}, u32[]{:S(2)}) copy-start(f32[8,1024]{1,0:T(8,128)} %get-tuple-element.112) | copy-start | bytes 98308
  176.7 7.3 %copy-start.12 = (f32[8,1024]{1,0:T(8,128)S(1)}, f32[8,1024]{1,0:T(8,128)}, u32[]{:S(2)}) copy-start(f32[8,1024]{1,0:T(8,128)} %get-tuple-element.116) | copy-start | bytes 98308
  176.7 7.4 %copy-start.6 = (bf16[16,32,1024]{2,1,0:T(8,128)(2,1)}, bf16[16,32,1024]{2,1,0:T(8,128)(2,1)S(1)}, u32[]{:S(2)}) copy-start(bf16[16,32,1024]{2,1,0:T(8,128)(2,1)S(1)} %all-to-all-done.2) | copy-start | bytes 3145732
  176.7 48.8 %all-to-all-start.3 = ((bf16[16,32,1024]{2,1,0:T(8,128)(2,1)}), bf16[16,32,1024]{2,1,0:T(8,128)(2,1)S(1)}, u32[]{:S(2)}, u32[]{:S(2)}) async-start(bf16[16,32,1024]{2,1,0:T(8,128)(2,1)} %bitcast.31), calls=%async_computation.3 | async-start | bytes 2097152 | tf_op jit(solution)/shard_map/all_to_all | solution.py:465
  184.0 36.4 %collective-permute-start.8 = (f32[28,1024]{1,0:T(8,128)S(1)}, f32[28,1024]{1,0:T(8,128)S(1)}, u32[]{:S(2)}, u32[]{:S(2)}) collective-permute-start(f32[28,1024]{1,0:T(8,128)S(1)} %pad_maximum_fusion), channel_id=1, source_target_pairs={{0,1},{1,0},{2,3},{3,2},{4,5},{5,4},{6,7},{7,6},{8,9},{9,8},{10,11... | collective-permute-start | bytes 344072 | tf_op jit(solution)/shard_map/ppermute | solution.py:471
  204.2 25.0 %copy-start.1 = (bf16[2,1,4096]{2,0,1:T(2,128)(2,1)S(1)}, bf16[2,1,4096]{2,0,1:T(2,128)(2,1)}, u32[]{:S(2)}) copy-start(bf16[2,1,4096]{2,0,1:T(2,128)(2,1)} %param.16) | copy-start | bytes 49156
  225.5 1.0 copy-start.5

commit v2 on v0

v2 whole, which is shorter than its diff:
```python
import jax
import jax.numpy as jnp
from jax import lax
from jax.experimental import pallas as pl
from jax.experimental.pallas import tpu as pltpu
from jax.sharding import PartitionSpec as P

EPS = 1e-05
F32 = jnp.float32
BF16 = jnp.bfloat16
PAD_MARK = 64.0
PAD_LIMIT = 32.0
SWAP = [(0, 1), (1, 0)]
VMEM = pl.BlockSpec(memory_space=pltpu.VMEM)
SMEM = pl.BlockSpec(memory_space=pltpu.SMEM)


def dot_nn(a, b):
    return lax.dot_general(a, b, (((1,), (0,)), ((), ())), preferred_element_type=F32)


def dot_nt(a, b):
    return lax.dot_general(a, b, (((1,), (1,)), ((), ())), preferred_element_type=F32)


def dot_tn(a, b):
    return lax.dot_general(a, b, (((0,), (0,)), ((), ())), preferred_element_type=F32)


def gelu_and_slope(v):
    phi = 0.5 + 0.5 * lax.erf(v * 0.7071067811865476)
    return v * phi, phi + v * (jnp.exp(v * v * -0.5) * 0.3989422804014327)


def sds(shape, dtype):
    return jax.ShapeDtypeStruct(shape, dtype)


def large(a):
    return len(a.shape) > 1 and a.shape[0] * a.shape[1] >= 1 << 16


def to_hbm(a):
    return pltpu.with_memory_space_constraint(a, pltpu.HBM) if large(a) else a


def in_hbm(o):
    return pltpu.HBM(o.shape, o.dtype) if large(o) else o


def cost():
    return pl.CostEstimate(flops=0, bytes_accessed=0, transcendentals=0)


def params(mib=52):
    return pltpu.CompilerParams(vmem_limit_bytes=mib << 20)


def call(kernel, name, args, outs, smem_in=0):
    return pl.pallas_call(
        kernel,
        in_specs=[SMEM] * smem_in + [VMEM] * (len(args) - smem_in),
        out_specs=[VMEM] * len(outs),
        out_shape=outs,
        compiler_params=params(),
        cost_estimate=cost(),
        name=name,
    )(*args)


def row_call(kernel, name, rows, args, outs, sums=0, weights=(), far=(), scratch=(), tile=256):
    steps = rows // tile
    half = steps // 2
    first = {
        "r": lambda i: i,
        "o": lambda i: jnp.minimum(i, half - 1),
        "p": lambda i: jnp.maximum(i - half, 0),
        "s": lambda i: lax.rem(i + half, steps),
    }

    def spec(kind, shape):
        if kind == "w":
            return pl.BlockSpec(tuple(shape), lambda i: (0,) * len(shape), pipeline_mode=pl.Buffered(1))
        return pl.BlockSpec((tile, shape[1]), lambda i: (first[kind](i), 0), **({"pipeline_mode": pl.Buffered(1)} if kind in "op" and shape[0] == tile else {}))

    cut = len(outs) - sums
    return pl.pallas_call(
        kernel,
        grid=(steps,),
        in_specs=[spec(kind, a.shape) for kind, a in args] + [pl.BlockSpec(memory_space=pl.ANY)] * len(weights),
        out_specs=[spec(kind, o.shape) for kind, o in outs[:cut]]
        + [pl.BlockSpec(o.shape, lambda i: (0, 0)) for _, o in outs[cut:]]
        + [pl.BlockSpec(memory_space=pl.ANY)] * len(far),
        out_shape=[in_hbm(o) for _, o in outs] + list(far),
        scratch_shapes=[pltpu.VMEM(w.shape[2:], BF16) for w in weights]
        + ([pltpu.SemaphoreType.DMA((2,))] if weights else [])
        + list(scratch),
        compiler_params=params(),
        cost_estimate=cost(),
        name=name,
    )(*(to_hbm(a) for _, a in args), *(pltpu.with_memory_space_constraint(w, pltpu.HBM) for w in weights))


def in_own_half():
    return pl.program_id(0) < pl.num_programs(0) // 2


def pick(own_ref, par_ref):
    return jnp.where(in_own_half(), own_ref[...], par_ref[...]).astype(F32)


def row_sum(v):
    return jnp.sum(v, axis=0, keepdims=True)


def vec(ref, layer):
    return ref[layer : layer + 1].astype(F32)


def slots_of(experts, capacity, routes):
    n = routes.shape[1]
    onehot = routes == lax.broadcasted_iota(jnp.int32, (experts, n), 0)
    hot = jnp.where(onehot, 1.0, 0.0)
    before = lax.broadcasted_iota(jnp.int32, (n, n), 0) < lax.broadcasted_iota(jnp.int32, (n, n), 1)
    earlier = dot_nn(hot.astype(BF16), jnp.where(before, 1.0, 0.0).astype(BF16))
    return routes * capacity + row_sum(earlier * hot).astype(jnp.int32)


def pack_first_kernel(experts, capacity, routes_ref, tokens_ref, out_ref, place_ref):
    slots = out_ref.shape[0]
    n = tokens_ref.shape[0]
    slot = slots_of(experts, capacity, routes_ref[...])
    hit = slot == lax.broadcasted_iota(jnp.int32, (slots, n), 0)
    hot = jnp.where(hit, 1.0, 0.0)
    place_ref[...] = hot.astype(BF16)
    packed = dot_nn(place_ref[...], tokens_ref[...])
    out_ref[...] = packed.astype(BF16)
    empty = 1.0 - jnp.sum(hot, axis=1, keepdims=True)
    out_ref[:, :128] = (packed[:, :128] + empty * PAD_MARK).astype(BF16)


def pack_kernel(place_ref, values_ref, out_ref):
    out_ref[...] = dot_nn(place_ref[...], values_ref[...]).astype(BF16)


def unpack_kernel(place_ref, returned_ref, base_ref, out_ref):
    picked = dot_tn(place_ref[...], returned_ref[...])
    out_ref[...] = (base_ref[...].astype(F32) + picked).astype(BF16)


class Weights:
    def __init__(self, layer, refs, order):
        first, second, self.bufs, self.sems = refs[0], refs[1], refs[2:4], refs[4]
        self.copies = [
            pltpu.make_async_copy(ref.at[layer, 0], self.bufs[k], self.sems.at[k]) for k, ref in enumerate((first, second))
        ]

        @pl.when(pl.program_id(0) == 0)
        def _():
            for k in order:
                self.copies[k].start()

    def take(self, k):
        @pl.when(pl.program_id(0) == 0)
        def _():
            self.copies[k].wait()

        return self.bufs[k][...]


def norm_stats(h):
    mu = jnp.mean(h, axis=1, keepdims=True)
    c = h - mu
    r = lax.rsqrt(jnp.mean(c * c, axis=1, keepdims=True) + EPS)
    return mu, r, c * r


def feed_forward(layer, low, weights, b_in_ref, act_ref, slope_ref):
    hidden = dot_nn(low, weights.take(0)) + vec(b_in_ref, layer)
    act, slope = gelu_and_slope(hidden)
    act = act.astype(BF16)
    act_ref[...] = act
    slope_ref[...] = slope.astype(BF16)
    return dot_nn(act, weights.take(1))


def first_kernel(
    own_ref, par_ref, gain_ref, shift_ref, center_ref, b_in_ref, w_in_ref, w_out_ref,
    low_ref, act_ref, slope_ref, part_ref, row_ref, *bufs,
):
    weights = Weights(0, (w_in_ref, w_out_ref, *bufs), (0, 1))
    x = pick(own_ref, par_ref)
    mu, r, xhat = norm_stats(x)
    low = (xhat * vec(gain_ref, 0) + vec(shift_ref, 0)).astype(BF16)
    low_ref[...] = low
    logit = jnp.sum(x * center_ref[...].astype(F32), axis=1, keepdims=True)
    gate = jax.nn.sigmoid(logit)
    live = jnp.where(x[:, :1] < PAD_LIMIT, 1.0, 0.0)
    lane = lax.broadcasted_iota(jnp.int32, row_ref.shape, 1)
    row_ref[...] = jnp.where(lane == 0, mu, jnp.where(lane == 1, r, jnp.where(lane == 2, gate, live)))
    part = feed_forward(0, low, weights, b_in_ref, act_ref, slope_ref)
    part_ref[...] = part.astype(BF16)


def branch_kernel(part_ref, theirs_ref, row_ref, out_ref, branch_ref):
    out = part_ref[...] + theirs_ref[...].astype(F32)
    out_ref[...] = out.astype(BF16)
    branch_ref[...] = (row_ref[:, 2:3] * out).astype(BF16)


def start_sums(sums_ref):
    @pl.when(pl.program_id(0) == 0)
    def _():
        sums_ref[...] = jnp.zeros_like(sums_ref)


def back_feed(ds, weights, slope_ref, dh_ref, sums_ref):
    depth = ds.shape[1]
    dact = dot_nt(ds, weights.take(1))
    dh = (dact * slope_ref[...].astype(F32)).astype(BF16)
    dh_ref[...] = dh
    bias = row_sum(dh.astype(F32))
    for j in range(bias.shape[1] // depth):
        sums_ref[3 + j : 4 + j] += bias[:, j * depth : (j + 1) * depth]
    return dot_nt(dh, weights.take(0))


def second_kernel(
    x_own_ref, x_par_ref, mine_ref, theirs_ref, dy_own_ref, dy_par_ref, gate_ref,
    b_out_ref, gain_ref, shift_ref, b_in_ref, w_in_ref, w_out_ref,
    part_own_ref, part_par_ref, xhat_ref, row_ref, back_ref, sums_ref, grad_in_ref, grad_out_ref,
    w_in_buf, w_out_buf, sems, low_ref, act_ref, slope_ref, ds_ref, dh_ref, sum_in_ref, sum_out_ref, out_sems,
):
    weights = Weights(1, (w_in_ref, w_out_ref, w_in_buf, w_out_buf, sems), (0, 1))
    start_sums(sums_ref)
    start_sums(sum_in_ref)
    start_sums(sum_out_ref)
    own = in_own_half()
    last = pl.program_id(0) == pl.num_programs(0) - 1
    depth, half = sum_in_ref.shape
    h = pick(x_own_ref, x_par_ref) + vec(b_out_ref, 0) + (mine_ref[...].astype(F32) + theirs_ref[...].astype(F32))
    mu, r, xhat = norm_stats(h)
    low_ref[...] = (xhat * vec(gain_ref, 1) + vec(shift_ref, 1)).astype(BF16)
    xhat_ref[...] = xhat.astype(BF16)
    row_ref[...] = jnp.broadcast_to(r, row_ref.shape)
    ds = gate_ref[:, 2:3] * pick(dy_own_ref, dy_par_ref)
    ds_ref[...] = ds.astype(BF16)

    @pl.when(own)
    def _():
        part_own_ref[...] = h + vec(b_out_ref, 1)

    part = feed_forward(1, low_ref[...], weights, b_in_ref, act_ref, slope_ref)

    @pl.when(own)
    def _():
        part_own_ref[...] += part

    @pl.when(jnp.logical_not(own))
    def _():
        part_par_ref[...] = part.astype(BF16)

    sum_out_ref[...] += dot_tn(act_ref[...], ds_ref[...])
    out_copy = pltpu.make_async_copy(sum_out_ref, grad_out_ref.at[1, 0], out_sems.at[0])
    pl.when(last)(out_copy.start)
    dact = dot_nt(ds_ref[...], w_out_buf[...])
    dh_ref[...] = (dact * slope_ref[...].astype(F32)).astype(BF16)
    bias = row_sum(dh_ref[...].astype(F32))
    for j in range(half // depth):
        sums_ref[3 + j : 4 + j] += bias[:, j * depth : (j + 1) * depth]
    in_copies = []
    for j in range(2):
        part = pl.ds(j * half // 2, half // 2)
        sum_in_ref[:, part] += dot_tn(low_ref[...], dh_ref[:, part])
        copy = pltpu.make_async_copy(sum_in_ref.at[:, part], grad_in_ref.at[1, 0, :, part], out_sems.at[1 + j])
        pl.when(last)(copy.start)
        in_copies.append(copy)
    dn = dot_nt(dh_ref[...], w_in_buf[...])
    back_ref[...] = dn.astype(BF16)
    sums_ref[0:1] += row_sum(dn * xhat)
    sums_ref[1:2] += row_sum(dn)
    sums_ref[2:3] += row_sum(ds_ref[...].astype(F32))

    @pl.when(last)
    def _():
        for copy in (out_copy, *in_copies):
            copy.wait()


def norm_back(dn, gain, xhat, r):
    dxhat = dn * gain
    m1 = jnp.mean(dxhat, axis=1, keepdims=True)
    m2 = jnp.mean(dxhat * xhat, axis=1, keepdims=True)
    return r * (dxhat - m1 - xhat * m2)


def back_first_kernel(
    own_ref, par_ref, row_ref, mine_ref, theirs_ref, xhat_ref, row1_ref, gain_ref, x_own_ref, x_par_ref, slope_ref,
    w_in_ref, w_out_ref, ds_ref, dh_ref, part_own_ref, carry_ref, part_par_ref, sums_ref, *bufs,
):
    weights = Weights(0, (w_in_ref, w_out_ref, *bufs), (1, 0))
    start_sums(sums_ref)
    own = in_own_half()
    dn = mine_ref[...].astype(F32) + theirs_ref[...].astype(F32)
    carry = row_ref[:, 2:3] * pick(own_ref, par_ref) + norm_back(
        dn, vec(gain_ref, 1), xhat_ref[...].astype(F32), row1_ref[:, 0:1]
    )
    ds = carry.astype(BF16)
    ds_ref[...] = ds

    @pl.when(own)
    def _():
        carry_ref[...] = carry

    dn = back_feed(ds, weights, slope_ref, dh_ref, sums_ref)
    xhat = (pick(x_own_ref, x_par_ref) - row_ref[:, 0:1]) * row_ref[:, 1:2]
    sums_ref[0:1] += row_sum(dn * xhat)
    sums_ref[1:2] += row_sum(dn)
    sums_ref[2:3] += row_sum(ds.astype(F32))

    @pl.when(own)
    def _():
        part_own_ref[...] = dn

    @pl.when(jnp.logical_not(own))
    def _():
        part_par_ref[...] = dn.astype(BF16)


def input_kernel(
    dy_ref, out_ref, row_ref, x_ref, part_ref, theirs_ref, carry_ref, gain_ref, center_ref, s0_ref, s1_ref,
    drow_ref, local_ref,
):
    @pl.when(pl.program_id(0) == 0)
    def _():
        local_ref[0:8] = s0_ref[...]
        local_ref[8:16] = s1_ref[...]
        local_ref[16:24] = jnp.zeros_like(local_ref[16:24])

    x = x_ref[...].astype(F32)
    gate = row_ref[:, 2:3]
    live = row_ref[:, 3:4]
    dgate = jnp.sum(dy_ref[...].astype(F32) * out_ref[...].astype(F32), axis=1, keepdims=True)
    dlogit = dgate * gate * (1.0 - gate)
    dn = part_ref[...] + theirs_ref[...].astype(F32)
    r = row_ref[:, 1:2]
    carry = carry_ref[...] + norm_back(dn, vec(gain_ref, 0), (x - row_ref[:, 0:1]) * r, r)
    drow_ref[...] = (carry + dlogit * center_ref[...].astype(F32)).astype(BF16)
    local_ref[16:17] += row_sum(dlogit * x)
    local_ref[17:18] += jnp.broadcast_to(row_sum(gate * live), (1, x.shape[1]))
    local_ref[18:19] += jnp.broadcast_to(row_sum(live), (1, x.shape[1]))


def finish_kernel(
    mean_load, here_ref, local_ref, other_ref, b_in_ref, b_out_ref, gain_ref, shift_ref, center_ref, gate_ref, load_ref
):
    depth = local_ref.shape[1]
    for layer in range(2):
        base = 8 * layer
        gain_ref[layer] = local_ref[base : base + 1] + other_ref[base : base + 1]
        shift_ref[layer] = local_ref[base + 1 : base + 2] + other_ref[base + 1 : base + 2]
        b_out_ref[layer] = local_ref[base + 2 : base + 3]
        parts = b_in_ref.shape[2] // (2 * depth)
        for side in range(2):

            @pl.when(here_ref[0] == side)
            def _():
                for j in range(parts):
                    low = (side * parts + j) * depth
                    b_in_ref[layer, :, low : low + depth] = local_ref[base + 3 + j : base + 4 + j]
                    low = ((1 - side) * parts + j) * depth
                    b_in_ref[layer, :, low : low + depth] = other_ref[base + 3 + j : base + 4 + j]

    total = local_ref[16:24] + other_ref[16:24]
    center_ref[...] = total[0:1]
    gate_ref[...] = total[1:2, :128] / total[2:3, :128]
    load_ref[...] = total[2:3, :128] / mean_load


def weight_kernel(by_left, moving_ref, fixed_ref, _, out_ref):
    if by_left:
        out_ref[...] = dot_tn(moving_ref[...], fixed_ref[...])
    else:
        out_ref[...] = dot_tn(fixed_ref[...], moving_ref[...])


def weight_gradient(by_left, moving, fixed, into, blk):
    rows, width = moving.shape
    other = fixed.shape[1]
    if by_left:
        out_spec = pl.BlockSpec((None, None, blk, other), lambda i: (0, 0, i, 0))
    else:
        out_spec = pl.BlockSpec((None, None, other, blk), lambda i: (0, 0, 0, i))
    return pl.pallas_call(
        lambda *refs: weight_kernel(by_left, *refs),
        grid=(width // blk,),
        in_specs=[
            pl.BlockSpec((rows, blk), lambda i: (0, i)),
            pl.BlockSpec((rows, other), lambda i: (0, 0), pipeline_mode=pl.Buffered(1)),
            pl.BlockSpec(memory_space=pl.ANY),
        ],
        out_specs=out_spec,
        out_shape=sds(into.shape, F32),
        input_output_aliases={2: 0},
        compiler_params=params(),
        cost_estimate=cost(),
        name="weight_gradient",
    )(to_hbm(moving), to_hbm(fixed), into)


def on_device(tokens, routes, cotangent, ln_gain, ln_shift, w_in, b_in, w_out, b_out, centroid):
    experts = lax.axis_size("expert")
    replicas = lax.axis_size("replica")
    here = lax.axis_index("replica")
    tok_dev, depth = tokens.shape
    half = w_in.shape[3]
    capacity = 2 * tok_dev // experts
    slots = experts * capacity
    both = 2 * slots
    gain, shift, b_out = (v.reshape(2, depth) for v in (ln_gain, ln_shift, b_out))

    def exchange(v):
        moved = lax.all_to_all(
            v.reshape(experts, capacity, depth), "expert", split_axis=0, concat_axis=0, tiled=True
        )
        return moved.reshape(slots, depth)

    def swap(v):
        return lax.ppermute(v, "replica", SWAP)

    sent_tok, place = call(
        lambda *refs: pack_first_kernel(experts, capacity, *refs),
        "pack_first",
        (routes.reshape(1, tok_dev), tokens),
        [sds((slots, depth), BF16), sds((slots, tok_dev), BF16)],
    )
    b_half = lax.dynamic_slice_in_dim(b_in.reshape(2, 2 * half), here * half, half, axis=1)
    x_own = exchange(sent_tok)
    x_par = swap(x_own)
    [sent_cot] = call(pack_kernel, "pack", (place, cotangent), [sds((slots, depth), BF16)])
    sent_cot, x_own = lax.optimization_barrier((sent_cot, x_own))
    dy_own = exchange(sent_cot)

    narrow, wide = ("r", sds((both, depth), BF16)), ("r", sds((both, half), BF16))
    per_row = ("r", sds((both, 128), F32))
    own_sum, par_sum = ("o", sds((slots, depth), F32)), ("p", sds((slots, depth), BF16))
    sums = ("w", sds((8, depth), F32))
    x = (("o", x_own), ("p", x_par))
    low0, act0, slope0, p0, row = row_call(
        first_kernel,
        "forward_first",
        both,
        (*x, ("w", gain), ("w", shift), ("w", centroid), ("w", b_half)),
        [narrow, wide, wide, narrow, per_row],
        weights=(w_in, w_out),
        tile=256,
    )
    dy = (("o", dy_own), ("p", swap(dy_own)))
    p1_own, p1_par, xhat1, row1, n1, sums1, grad_in, grad_out = row_call(
        second_kernel,
        "second",
        both,
        (
            *x, ("r", p0), ("s", swap(p0)), *dy, ("r", row),
            ("w", b_out), ("w", gain), ("w", shift), ("w", b_half),
        ),
        [own_sum, par_sum, narrow, per_row, narrow, sums],
        sums=1,
        weights=(w_in, w_out),
        tile=256,
        far=(sds((2, 1, depth, half), F32), sds((2, 1, half, depth), F32)),
        scratch=[
            pltpu.VMEM((256, depth), BF16),
            pltpu.VMEM((256, half), BF16),
            pltpu.VMEM((256, half), BF16),
            pltpu.VMEM((256, depth), BF16),
            pltpu.VMEM((256, half), BF16),
            pltpu.VMEM((depth, half), F32),
            pltpu.VMEM((half, depth), F32),
            pltpu.SemaphoreType.DMA((3,)),
        ],
    )
    p1_there, n1 = lax.optimization_barrier((swap(p1_par), n1))
    out, branch = row_call(
        branch_kernel,
        "branch",
        slots,
        (("r", p1_own), ("r", p1_there), ("r", row)),
        [("r", sds((slots, depth), BF16))] * 2,
        tile=256,
    )
    returned = exchange(branch)
    ds0, dh0, n0_own, carry_own, n0_par, sums0 = row_call(
        back_first_kernel,
        "backward_first",
        both,
        (
            *dy, ("r", row), ("r", n1), ("s", swap(n1)), ("r", xhat1), ("r", row1), ("w", gain), *x, ("r", slope0),
        ),
        [narrow, wide, own_sum, own_sum, par_sum, sums],
        sums=1,
        tile=256,
        weights=(w_in, w_out),
    )
    drow, local = row_call(
        input_kernel,
        "input_gradient",
        slots,
        (
            ("r", dy_own), ("r", out), ("r", row), ("r", x_own), ("r", n0_own), ("r", swap(n0_par)), ("r", carry_own),
            ("w", gain), ("w", centroid), ("w", sums0), ("w", sums1),
        ),
        [("r", sds((slots, depth), BF16)), ("w", sds((24, depth), F32))],
        sums=1,
        tile=256,
    )
    drow, returned = lax.optimization_barrier((drow, returned))
    grad_returned = exchange(drow)

    grad_out = weight_gradient(True, act0, ds0, grad_out, 512)
    grad_in = weight_gradient(False, dh0, low0, grad_in, 512)
    [mixed] = call(unpack_kernel, "unpack", (place, returned, tokens), [sds(tokens.shape, BF16)])
    other = swap(local)
    one = sds((2, 1, depth), F32)
    grad_b_in, grad_b_out, grad_gain, grad_shift, grad_center, mean_gate, load = call(
        lambda *refs: finish_kernel(float(tok_dev * replicas), *refs),
        "finish",
        (here.astype(jnp.int32).reshape(1), local, other),
        [sds((2, 1, 2 * half), F32), one, one, one, sds((1, depth), F32), sds((1, 128), F32), sds((1, 128), F32)],
        smem_in=1,
    )
    [grad_tokens] = call(unpack_kernel, "unpack", (place, grad_returned, cotangent), [sds(tokens.shape, BF16)])
    return (
        mixed, grad_tokens, grad_in, grad_out, grad_b_in, grad_b_out, grad_gain, grad_shift, grad_center,
        mean_gate[0, :1], load[0, :1],
    )


def solution(mesh):
    rows = P(("expert", "replica"), None)
    by_expert = P(None, "expert", None)
    first_weight = P(None, "expert", None, "replica")
    second_weight = P(None, "expert", "replica", None)
    return jax.shard_map(
        on_device,
        mesh=mesh,
        in_specs=(
            rows, rows, rows, by_expert, by_expert, first_weight, by_expert, second_weight, by_expert,
            P("expert", None),
        ),
        out_specs=(
            rows, rows, first_weight, second_weight, by_expert, by_expert, by_expert, by_expert,
            P("expert", None), P("expert"), P("expert"),
        ),
        check_vma=False,
    )
```

time: 354 us -> 194 us (0.55); the launches traced: 349 us -> 193 us
  matrix products: 158 us -> 0 us
  Pallas kernels: 0 us -> 116 us
  waiting for transfers between devices: 60 us -> 21 us
  other arithmetic: 33.5 us -> 0 us
  between operations: 19.4 us -> 0.8 us
  local copies, waits for them, and re-layouts: 19.6 us -> 4.68 us
  starting transfers between devices: 23.9 us -> 17.6 us
    dot_general x13 -> x0, matrix products: 158 us -> none  [the longest x2 51.8 us: on_device(): jnp.dot(lowered, full_first[layer, 0], preferred_element_type=jnp.float32)]
    pallas_call x0 -> x12, Pallas kernels: none -> 116 us  [the longest x5 92.7 us: row_call(): pl.pallas_call(kernel, grid=(steps,), in_specs=[spec(kind, a.shape) for k...]
    all_to_all x4 -> x3, waiting for transfers between devices: 58.5 us -> 12.5 us  [exchange(): lax.all_to_all(v.reshape(experts, capacity, depth), 'expert', split_axis=...]
    unnamed x4 -> x0, other arithmetic: 23.9 us -> none
    ppermute x0 -> x7, waiting for transfers between devices: none -> 8.47 us  [swap(): return lax.ppermute(v, 'replica', SWAP)]
    gather x4 -> x0, local copies, waits for them, and re-layouts: 8.46 us -> none  [the longest x2 4.34 us: unpack_slots(): jnp.take(returned.reshape(slot_count, row_width), slot_ids, axis=0)]
    all_to_all x4 -> x3, starting transfers between devices: 23.5 us -> 16.9 us  [exchange(): lax.all_to_all(v.reshape(experts, capacity, depth), 'expert', split_axis=...]
    psum x1 -> x0, blocking collectives: 5.05 us -> none  [on_device(): lax.psum((jnp.stack(grads_gain), jnp.stack(grads_shift), jnp.stack(grads_...]
  transfers between devices with their start and end apart: 10 -> 10, of which waited for: 3 -> 5; matrix products, arithmetic and copies ran while one was open for 40% -> 0% of each run, Pallas kernels for 0% -> 37%
where the time goes in v2:
time: 194 us; the launch traced here: 193 us
  Pallas kernels  116 us (60%)
  blocking collectives  32.8 us (17%)
  waiting for transfers between devices  21 us (11%)
  starting transfers between devices  17.6 us (9%)
  local copies, waits for them, and re-layouts  4.68 us (2%)
    pallas_call x5, Pallas kernels, row_call(): pl.pallas_call(kernel, grid=(steps,), in_specs=[spec(kind, a.shape) for k...  92.7 us
    all_to_all x1, blocking collectives, exchange(): lax.all_to_all(v.reshape(experts, capacity, depth), 'expert', split_axis=...  32.8 us
    pallas_call x2, Pallas kernels, weight_gradient(): pl.pallas_call(lambda *refs: weight_kernel(by_left, *refs), grid=(width /...  18.4 us
    all_to_all x3, starting transfers between devices, exchange(): lax.all_to_all(v.reshape(experts, capacity, depth), 'expert', split_axis=...  16.9 us
    all_to_all x3, waiting for transfers between devices, exchange(): lax.all_to_all(v.reshape(experts, capacity, depth), 'expert', split_axis=...  12.5 us
    ppermute x7, waiting for transfers between devices, swap(): return lax.ppermute(v, 'replica', SWAP)  8.47 us
    pallas_call x5, Pallas kernels, call(): pl.pallas_call(kernel, in_specs=[SMEM] * smem_in + [VMEM] * (len(args) -...  5.23 us
    unnamed x26, local copies, waits for them, and re-layouts  4.67 us
  transfers between devices with their start and end apart: 10, of which 5 were waited for; matrix products, arithmetic and copies ran while one was open for 0% of the time, Pallas kernels for 37%

profile of v2, /device:TPU:8, one launch (start us, length us, event | category | flops | bytes accessed | tf_op | source)
XLA Modules:
  0.0 193.3 jit_solution(1707493644021349219)
XLA Ops:
  0.6 0.0 copy-start
  0.7 0.0 copy-start.2
  0.7 0.0 copy-start.3
  0.7 1.1 copy-done.3
  1.8 0.7 copy-done.9
  2.5 0.6 pack_first.1
  3.1 32.8 %all_to_all.20 = bf16[16,32,1024]{2,1,0:T(8,128)(2,1)} all-to-all(bf16[16,32,1024]{2,1,0:T(8,128)(2,1)S(1)} %bitcast.21), channel_id=1, replica_groups=mesh['expert'=16,'replica'=2] {'expert'}, dimensions={0} | all-to-all | bytes 2097152 | tf_op jit(solution)/shard_map/all_to_all | solution.py:423
  35.9 0.0 collective-permute-start
  35.9 0.0 copy-done.2
  35.9 1.4 pack.1
  37.4 4.8 %all-to-all-start.1 = ((bf16[16,32,1024]{2,1,0:T(8,128)(2,1)}), bf16[16,32,1024]{2,1,0:T(8,128)(2,1)}, u32[]{:S(2)}, u32[]{:S(2)}) async-start(bf16[16,32,1024]{2,1,0:T(8,128)(2,1)} %bitcast.3), calls=%async_computation.1 | async-start | bytes 2097152 | tf_op jit(solution)/shard_map/all_to_all | solution.py:423
  42.2 0.0 copy-done
  42.2 0.0 collective-permute-done.par_ref.x_par_ref
  42.2 0.0 copy-done.5
  42.3 0.0 copy-done.6
  42.3 0.0 copy-done.7
  42.3 0.0 copy-start.8
  42.3 19.4 %forward_first.1 = (bf16[1024,1024]{1,0:T(8,128)(2,1)}, bf16[1024,2048]{1,0:T(8,128)(2,1)}, bf16[1024,2048]{1,0:T(8,128)(2,1)}, bf16[1024,1024]{1,0:T(8,128)(2,1)}, f32[1024,128]{1,0:T(8,128)}) custom-call(bf16[512,1024]{1,0:T(8,128)(2,1)} %bitcast.2.own_ref.x_own_ref.x_ref, bf16[512,1024]{1,0:T(8,128)(2,1)} %collective-permute-done.par_ref.x_par_ref, ...), custom_call_target="tpu_custom_call" | custom-call | tf_op jit(solution)/shard_map/forward_first/pallas_call | solution.py:87
  61.7 0.3 collective-permute-start.1
  62.0 7.2 %all-to-all-done.1 = bf16[16,32,1024]{2,1,0:T(8,128)(2,1)} async-done(((bf16[16,32,1024]{2,1,0:T(8,128)(2,1)}), bf16[16,32,1024]{2,1,0:T(8,128)(2,1)}, u32[]{:S(2)}, u32[]{:S(2)}) %all-to-all-start.1) | async-done | bytes 1048608 | tf_op jit(solution)/shard_map/all_to_all | solution.py:423
  69.2 0.0 collective-permute-start.2
  69.2 2.9 %collective-permute-done.2.dy_par_ref.par_ref = bf16[512,1024]{1,0:T(8,128)(2,1)S(1)} collective-permute-done((bf16[512,1024]{1,0:T(8,128)(2,1)}, bf16[512,1024]{1,0:T(8,128)(2,1)S(1)}, u32[]{:S(2)}, u32[]{:S(2)}) %collective-permute-start.2) | collective-permute-done | bytes 1048608 | tf_op jit(solution)/shard_map/ppermute | solution.py:429
  72.0 0.0 collective-permute-done.1.theirs_ref
  72.0 1.0 copy-done.10
  73.0 43.8 %second.1 = (f32[512,1024]{1,0:T(8,128)}, bf16[512,1024]{1,0:T(8,128)(2,1)}, bf16[1024,1024]{1,0:T(8,128)(2,1)}, f32[1024,128]{1,0:T(8,128)}, bf16[1024,1024]{1,...) custom-call(bf16[512,1024]{1,0:T(8,128)(2,1)} %bitcast.2.own_ref.x_own_ref.x_ref,, ...), custom_call_target="tpu_custom_call" | custom-call | tf_op jit(solution)/shard_map/second/pallas_call | solution.py:87
  116.8 0.2 collective-permute-start.3
  117.0 2.7 %collective-permute-done.3.theirs_ref = bf16[512,1024]{1,0:T(8,128)(2,1)S(1)} collective-permute-done((bf16[512,1024]{1,0:T(8,128)(2,1)}, bf16[512,1024]{1,0:T(8,128)(2,1)S(1)}, u32[]{:S(2)}, u32[]{:S(2)}) %collective-permute-start.3) | collective-permute-done | bytes 1048608 | tf_op jit(solution)/shard_map/ppermute | solution.py:429
  119.8 0.1 collective-permute-start.4
  119.9 0.8 copy-done.12
  120.8 3.1 %branch.1 = (bf16[512,1024]{1,0:T(8,128)(2,1)}, bf16[512,1024]{1,0:T(8,128)(2,1)}) custom-call(f32[512,1024]{1,0:T(8,128)} %get-tuple-element.55.part_ref, bf16[512,1024]{1,0:T(8,128)(2,1)} %copy-done.12, f32[1024,128]{1,0:T(8,128)} %get-tuple-element.54.gate_ref.row_ref), custom_call_target="tpu_custom_call" | custom-call | tf_op jit(solution)/shard_map/branch/pallas_call | solution.py:87
  123.9 5.1 %all-to-all-start.2 = ((bf16[16,32,1024]{2,1,0:T(8,128)(2,1)}), bf16[16,32,1024]{2,1,0:T(8,128)(2,1)S(1)}, u32[]{:S(2)}, u32[]{:S(2)}) async-start(bf16[16,32,1024]{2,1,0:T(8,128)(2,1)} %bitcast.31), calls=%async_computation.2 | async-start | bytes 2097152 | tf_op jit(solution)/shard_map/all_to_all | solution.py:423
  129.0 0.0 collective-permute-done.4.theirs_ref
  129.0 21.2 %backward_first.1 = (bf16[1024,1024]{1,0:T(8,128)(2,1)}, bf16[1024,2048]{1,0:T(8,128)(2,1)}, f32[512,1024]{1,0:T(8,128)}, f32[512,1024]{1,0:T(8,128)}, bf16[512,1024]{1,0:T(8,128)(2,1)}, /*index=5*/f32[8,1024]{1,0:T(8,128)S(1)}) custom-call(bf16[512,1024]{1,0:T(8,128)(2,1)} %bitcast.4.dy_own_ref.own_ref.dy_ref, bf16[512,1024]{1,0:T(8,128)(2,1)} %copy-done.10, ...), custom_call_target="tpu_custom_call" | custom-call | tf_op jit(solution)/shard_map/backward_first/pallas_call | solution.py:87
  150.2 0.1 collective-permute-start.5
  150.3 2.9 %collective-permute-done.5.theirs_ref = bf16[512,1024]{1,0:T(8,128)(2,1)S(1)} collective-permute-done((bf16[512,1024]{1,0:T(8,128)(2,1)}, bf16[512,1024]{1,0:T(8,128)(2,1)S(1)}, u32[]{:S(2)}, u32[]{:S(2)}) %collective-permute-start.5) | collective-permute-done | bytes 1048608 | tf_op jit(solution)/shard_map/ppermute | solution.py:429
  153.1 1.0 copy-done.11
  154.1 5.3 %input_gradient.1 = (bf16[512,1024]{1,0:T(8,128)(2,1)}, f32[24,1024]{1,0:T(8,128)S(1)}) custom-call(bf16[512,1024]{1,0:T(8,128)(2,1)} %bitcast.4.dy_own_ref.own_ref.dy_ref, bf16[512,1024]{1,0:T(8,128)(2,1)} %get-tuple-element.59.out_ref, f32[1024,128]{1,0:T(8,128)} %get-tuple-element.54.gate_ref.row_ref, bf16[512,1024]{1,0:T(8,128)(2,1)} %bitcast.2.own_ref.x_own_ref.x_ref, ...), custom_call_target="tpu_custom_call" | custom-call | tf_op jit(solution)/shard_map/input_gradient/pallas_call | solution.py:87
  159.4 0.0 all-to-all-done.2
  159.4 6.9 %all-to-all-start.3 = ((bf16[16,32,1024]{2,1,0:T(8,128)(2,1)}), bf16[16,32,1024]{2,1,0:T(8,128)(2,1)S(1)}, u32[]{:S(2)}, u32[]{:S(2)}) async-start(bf16[16,32,1024]{2,1,0:T(8,128)(2,1)} %bitcast.30), calls=%async_computation.3 | async-start | bytes 2097152 | tf_op jit(solution)/shard_map/all_to_all | solution.py:423
  166.3 0.0 collective-permute-start.6
  166.3 9.2 %weight_gradient.2 = f32[2,1,1024,2048]{3,2,1,0:T(8,128)} custom-call(bf16[1024,2048]{1,0:T(8,128)(2,1)} %get-tuple-element.73.refs_0_, bf16[1024,1024]{1,0:T(8,128)(2,1)} %get-tuple-element.74.refs_1_, f32[2,1,1024,2048]{3,2,1,0:T(8,128)} %get-tuple-element.75.refs_2_), custom_call_target="tpu_custom_call", output_to_operand_aliasing={{}: (2, {})} | custom-call | tf_op jit(solution)/shard_map/weight_gradient/pallas_call | solution.py:394
  175.5 9.2 %weight_gradient.3 = f32[2,1,2048,1024]{3,2,1,0:T(8,128)} custom-call(bf16[1024,2048]{1,0:T(8,128)(2,1)} %get-tuple-element.76.refs_0_, bf16[1024,1024]{1,0:T(8,128)(2,1)} %get-tuple-element.77.refs_1_, f32[2,1,2048,1024]{3,2,1,0:T(8,128)} %get-tuple-element.78.refs_2_), custom_call_target="tpu_custom_call", output_to_operand_aliasing={{}: (2, {})} | custom-call | tf_op jit(solution)/shard_map/weight_gradient/pallas_call | solution.py:394
  184.8 0.0 copy-done.4
  184.8 1.3 unpack.2
  186.0 0.0 collective-permute-done.6.refs_2_
  186.0 0.7 finish.1
  186.7 5.4 %all-to-all-done.3 = bf16[16,32,1024]{2,1,0:T(8,128)(2,1)S(1)} async-done(((bf16[16,32,1024]{2,1,0:T(8,128)(2,1)}), bf16[16,32,1024]{2,1,0:T(8,128)(2,1)S(1)}, u32[]{:S(2)}, u32[]{:S(2)}) %all-to-all-start.3) | async-done | bytes 1048608 | tf_op jit(solution)/shard_map/all_to_all | solution.py:423
  192.1 1.3 unpack.3
  (12 shorter events, 0.0 us)
Async XLA Ops:
  0.6 41.6 %copy-start = (bf16[2,1,4096]{2,0,1:T(2,128)(2,1)S(1)}, bf16[2,1,4096]{2,0,1:T(2,128)(2,1)}, u32[]{:S(2)}) copy-start(bf16[2,1,4096]{2,0,1:T(2,128)(2,1)} %param.16) | copy-start | bytes 49156
  0.7 35.3 %copy-start.2 = (bf16[256,1024]{1,0:T(8,128)(2,1)S(1)}, bf16[256,1024]{1,0:T(8,128)(2,1)}, u32[]{:S(2)}) copy-start(bf16[256,1024]{1,0:T(8,128)(2,1)} %base_ref.3) | copy-start | bytes 1572868
  0.7 1.1 copy-start.3
  1.8 0.7 copy-start.9
  35.9 6.3 %copy-start.5 = (bf16[2,1,1024]{2,0,1:T(2,128)(2,1)S(1)}, bf16[2,1,1024]{2,0,1:T(2,128)(2,1)}, u32[]{:S(2)}) copy-start(bf16[2,1,1024]{2,0,1:T(2,128)(2,1)} %param.13) | copy-start | bytes 12292
  35.9 6.3 %copy-start.6 = (bf16[1,1024]{1,0:T(2,128)(2,1)S(1)}, bf16[1,1024]{1,0:T(2,128)(2,1)}, u32[]{:S(2)}) copy-start(bf16[1,1024]{1,0:T(2,128)(2,1)} %center_ref.3) | copy-start | bytes 6148
  35.9 6.3 %copy-start.7 = (bf16[2,1,1024]{2,0,1:T(2,128)(2,1)S(1)}, bf16[2,1,1024]{2,0,1:T(2,128)(2,1)}, u32[]{:S(2)}) copy-start(bf16[2,1,1024]{2,0,1:T(2,128)(2,1)} %param.14) | copy-start | bytes 12292
  35.9 6.3 %collective-permute-start = (bf16[512,1024]{1,0:T(8,128)(2,1)}, bf16[512,1024]{1,0:T(8,128)(2,1)}, u32[]{:S(2)}, u32[]{:S(2)}) collective-permute-start(bf16[512,1024]{1,0:T(8,128)(2,1)} %bitcast.2.own_ref.x_own_ref.x_ref), channel_id=1, source_target_pairs={{0,1},{1,0},{2,3},{3,2},{4,5},{5,4},{6,7},{7,6},{8,9},{9,8},{10,11... | collective-permute-start | bytes 3145736 | tf_op jit(solution)/shard_map/ppermute | solution.py:429
  37.4 31.8 %all-to-all-start.1 = ((bf16[16,32,1024]{2,1,0:T(8,128)(2,1)}), bf16[16,32,1024]{2,1,0:T(8,128)(2,1)}, u32[]{:S(2)}, u32[]{:S(2)}) async-start(bf16[16,32,1024]{2,1,0:T(8,128)(2,1)} %bitcast.3), calls=%async_computation.1 | async-start | bytes 2097152 | tf_op jit(solution)/shard_map/all_to_all | solution.py:423
  42.3 30.8 %copy-start.8 = (bf16[2,1,1024]{2,0,1:T(2,128)(2,1)S(1)}, bf16[2,1,1024]{2,0,1:T(2,128)(2,1)}, u32[]{:S(2)}) copy-start(bf16[2,1,1024]{2,0,1:T(2,128)(2,1)} %param.18) | copy-start | bytes 12292
  61.7 10.3 %collective-permute-start.1 = (bf16[1024,1024]{1,0:T(8,128)(2,1)}, bf16[1024,1024]{1,0:T(8,128)(2,1)}, u32[]{:S(2)}, u32[]{:S(2)}) collective-permute-start(bf16[1024,1024]{1,0:T(8,128)(2,1)} %get-tuple-element.53.mine_ref), channel_id=1, source_target_pairs={{0,1},{1,0},{2,3},{3,2},{4,5},{5,4},{6,7},{7,6},{8,9},{9,8},{10,11... | collective-permute-start | bytes 6291464 | tf_op jit(solution)/shard_map/ppermute | solution.py:429
  69.2 2.9 %collective-permute-start.2 = (bf16[512,1024]{1,0:T(8,128)(2,1)}, bf16[512,1024]{1,0:T(8,128)(2,1)S(1)}, u32[]{:S(2)}, u32[]{:S(2)}) collective-permute-start(bf16[512,1024]{1,0:T(8,128)(2,1)} %bitcast.4.dy_own_ref.own_ref.dy_ref), channel_id=1, source_target_pairs={{0,1},{1,0},{2,3},{3,2},{4,5},{5,4},{6,7},{7,6},{8,9},{9,8},{10,11... | collective-permute-start | bytes 3145736 | tf_op jit(solution)/shard_map/ppermute | solution.py:429
  72.0 1.0 copy-start.10
  116.8 2.9 %collective-permute-start.3 = (bf16[512,1024]{1,0:T(8,128)(2,1)}, bf16[512,1024]{1,0:T(8,128)(2,1)S(1)}, u32[]{:S(2)}, u32[]{:S(2)}) collective-permute-start(bf16[512,1024]{1,0:T(8,128)(2,1)} %get-tuple-element.56), channel_id=1, source_target_pairs={{0,1},{1,0},{2,3},{3,2},{4,5},{5,4},{6,7},{7,6},{8,9},{9,8},{10,11... | collective-permute-start | bytes 3145736 | tf_op jit(solution)/shard_map/ppermute | solution.py:429
  119.8 1.0 copy-start.12
  119.8 9.2 %collective-permute-start.4 = (bf16[1024,1024]{1,0:T(8,128)(2,1)}, bf16[1024,1024]{1,0:T(8,128)(2,1)}, u32[]{:S(2)}, u32[]{:S(2)}) collective-permute-start(bf16[1024,1024]{1,0:T(8,128)(2,1)} %get-tuple-element.60.mine_ref), channel_id=1, source_target_pairs={{0,1},{1,0},{2,3},{3,2},{4,5},{5,4},{6,7},{7,6},{8,9},{9,8},{10,11... | collective-permute-start | bytes 6291464 | tf_op jit(solution)/shard_map/ppermute | solution.py:429
  123.9 35.5 %all-to-all-start.2 = ((bf16[16,32,1024]{2,1,0:T(8,128)(2,1)}), bf16[16,32,1024]{2,1,0:T(8,128)(2,1)S(1)}, u32[]{:S(2)}, u32[]{:S(2)}) async-start(bf16[16,32,1024]{2,1,0:T(8,128)(2,1)} %bitcast.31), calls=%async_computation.2 | async-start | bytes 2097152 | tf_op jit(solution)/shard_map/all_to_all | solution.py:423
  150.2 2.9 %collective-permute-start.5 = (bf16[512,1024]{1,0:T(8,128)(2,1)}, bf16[512,1024]{1,0:T(8,128)(2,1)S(1)}, u32[]{:S(2)}, u32[]{:S(2)}) collective-permute-start(bf16[512,1024]{1,0:T(8,128)(2,1)} %get-tuple-element.65), channel_id=1, source_target_pairs={{0,1},{1,0},{2,3},{3,2},{4,5},{5,4},{6,7},{7,6},{8,9},{9,8},{10,11... | collective-permute-start | bytes 3145736 | tf_op jit(solution)/shard_map/ppermute | solution.py:429
  153.1 1.0 copy-start.11
  159.4 32.7 %all-to-all-start.3 = ((bf16[16,32,1024]{2,1,0:T(8,128)(2,1)}), bf16[16,32,1024]{2,1,0:T(8,128)(2,1)S(1)}, u32[]{:S(2)}, u32[]{:S(2)}) async-start(bf16[16,32,1024]{2,1,0:T(8,128)(2,1)} %bitcast.30), calls=%async_computation.3 | async-start | bytes 2097152 | tf_op jit(solution)/shard_map/all_to_all | solution.py:423
  166.3 19.7 %collective-permute-start.6 = (f32[24,1024]{1,0:T(8,128)S(1)}, f32[24,1024]{1,0:T(8,128)S(1)}, u32[]{:S(2)}, u32[]{:S(2)}) collective-permute-start(f32[24,1024]{1,0:T(8,128)S(1)} %get-tuple-element.79.refs_1_), channel_id=1, source_target_pairs={{0,1},{1,0},{2,3},{3,2},{4,5},{5,4},{6,7},{7,6},{8,9},{9,8},{10,11... | collective-permute-start | bytes 294920 | tf_op jit(solution)/shard_map/ppermute | solution.py:429
  175.5 9.2 %copy-start.4 = (bf16[256,1024]{1,0:T(8,128)(2,1)S(1)}, bf16[256,1024]{1,0:T(8,128)(2,1)}, u32[]{:S(2)}) copy-start(bf16[256,1024]{1,0:T(8,128)(2,1)} %base_ref.2) | copy-start | bytes 1572868
  175.5 17.8 %copy-start.1 = (bf16[2,1,4096]{2,0,1:T(2,128)(2,1)S(1)}, bf16[2,1,4096]{2,0,1:T(2,128)(2,1)}, u32[]{:S(2)}) copy-start(bf16[2,1,4096]{2,0,1:T(2,128)(2,1)} %param.16) | copy-start | bytes 49156

commit v3 on v2

--- a/solution.py
+++ b/solution.py
@@ -68,7 +68,7 @@
     )(*args)
 
 
-def row_call(kernel, name, rows, args, outs, sums=0, weights=(), far=(), scratch=(), tile=256):
+def row_call(kernel, name, rows, args, outs, sums=0, weights=(), far=(), scratch=(), tile=256, mib=52):
     steps = rows // tile
     half = steps // 2
     first = {
@@ -95,10 +95,10 @@
         scratch_shapes=[pltpu.VMEM(w.shape[2:], BF16) for w in weights]
         + ([pltpu.SemaphoreType.DMA((2,))] if weights else [])
         + list(scratch),
-        compiler_params=params(),
+        compiler_params=params(mib),
         cost_estimate=cost(),
         name=name,
-    )(*(to_hbm(a) for _, a in args), *(pltpu.with_memory_space_constraint(w, pltpu.HBM) for w in weights))
+    )(*(to_hbm(a) if weights and kind != "p" else a for kind, a in args), *(pltpu.with_memory_space_constraint(w, pltpu.HBM) for w in weights))
 
 
 def in_own_half():
@@ -228,8 +228,8 @@
 def second_kernel(
     x_own_ref, x_par_ref, mine_ref, theirs_ref, dy_own_ref, dy_par_ref, gate_ref,
     b_out_ref, gain_ref, shift_ref, b_in_ref, w_in_ref, w_out_ref,
-    part_own_ref, part_par_ref, xhat_ref, row_ref, back_ref, sums_ref, grad_in_ref, grad_out_ref,
-    w_in_buf, w_out_buf, sems, low_ref, act_ref, slope_ref, ds_ref, dh_ref, sum_in_ref, sum_out_ref, out_sems,
+    part_own_ref, part_par_ref, xhat_ref, row_ref, back_ref, low_ref, later_ref, sums_ref, grad_in_ref, grad_out_ref,
+    w_in_buf, w_out_buf, sems, act_ref, slope_ref, ds_ref, dh_ref, sum_in_ref, sum_out_ref, out_sems,
 ):
     weights = Weights(1, (w_in_ref, w_out_ref, w_in_buf, w_out_buf, sems), (0, 1))
     start_sums(sums_ref)
@@ -237,7 +237,8 @@
     start_sums(sum_out_ref)
     own = in_own_half()
     last = pl.program_id(0) == pl.num_programs(0) - 1
-    depth, half = sum_in_ref.shape
+    half, depth = sum_out_ref.shape
+    now = sum_in_ref.shape[1]
     h = pick(x_own_ref, x_par_ref) + vec(b_out_ref, 0) + (mine_ref[...].astype(F32) + theirs_ref[...].astype(F32))
     mu, r, xhat = norm_stats(h)
     low_ref[...] = (xhat * vec(gain_ref, 1) + vec(shift_ref, 1)).astype(BF16)
@@ -268,13 +269,10 @@
     bias = row_sum(dh_ref[...].astype(F32))
     for j in range(half // depth):
         sums_ref[3 + j : 4 + j] += bias[:, j * depth : (j + 1) * depth]
-    in_copies = []
-    for j in range(2):
-        part = pl.ds(j * half // 2, half // 2)
-        sum_in_ref[:, part] += dot_tn(low_ref[...], dh_ref[:, part])
-        copy = pltpu.make_async_copy(sum_in_ref.at[:, part], grad_in_ref.at[1, 0, :, part], out_sems.at[1 + j])
-        pl.when(last)(copy.start)
-        in_copies.append(copy)
+    sum_in_ref[...] += dot_tn(low_ref[...], dh_ref[:, :now])
+    later_ref[...] = dh_ref[:, now:]
+    in_copy = pltpu.make_async_copy(sum_in_ref, grad_in_ref.at[1, 0, :, pl.ds(0, now)], out_sems.at[1])
+    pl.when(last)(in_copy.start)
     dn = dot_nt(dh_ref[...], w_in_buf[...])
     back_ref[...] = dn.astype(BF16)
     sums_ref[0:1] += row_sum(dn * xhat)
@@ -283,8 +281,8 @@
 
     @pl.when(last)
     def _():
-        for copy in (out_copy, *in_copies):
-            copy.wait()
+        out_copy.wait()
+        in_copy.wait()
 
 
 def norm_back(dn, gain, xhat, r):
@@ -320,7 +318,7 @@
 
     @pl.when(own)
     def _():
-        part_own_ref[...] = dn
+        part_own_ref[...] = dn.astype(BF16)
 
     @pl.when(jnp.logical_not(own))
     def _():
@@ -342,7 +340,7 @@
     live = row_ref[:, 3:4]
     dgate = jnp.sum(dy_ref[...].astype(F32) * out_ref[...].astype(F32), axis=1, keepdims=True)
     dlogit = dgate * gate * (1.0 - gate)
-    dn = part_ref[...] + theirs_ref[...].astype(F32)
+    dn = part_ref[...].astype(F32) + theirs_ref[...].astype(F32)
     r = row_ref[:, 1:2]
     carry = carry_ref[...] + norm_back(dn, vec(gain_ref, 0), (x - row_ref[:, 0:1]) * r, r)
     drow_ref[...] = (carry + dlogit * center_ref[...].astype(F32)).astype(BF16)
@@ -377,35 +375,68 @@
     load_ref[...] = total[2:3, :128] / mean_load
 
 
-def weight_kernel(by_left, moving_ref, fixed_ref, _, out_ref):
-    if by_left:
-        out_ref[...] = dot_tn(moving_ref[...], fixed_ref[...])
-    else:
-        out_ref[...] = dot_tn(fixed_ref[...], moving_ref[...])
-
-
-def weight_gradient(by_left, moving, fixed, into, blk):
-    rows, width = moving.shape
-    other = fixed.shape[1]
-    if by_left:
-        out_spec = pl.BlockSpec((None, None, blk, other), lambda i: (0, 0, i, 0))
-    else:
-        out_spec = pl.BlockSpec((None, None, other, blk), lambda i: (0, 0, 0, i))
+def out_kernel(act_ref, ds_ref, _, out_ref):
+    out_ref[...] = dot_tn(act_ref[...], ds_ref[...])
+
+
+def out_gradient(act, ds, into, blk):
+    rows, half = act.shape
+    depth = ds.shape[1]
     return pl.pallas_call(
-        lambda *refs: weight_kernel(by_left, *refs),
-        grid=(width // blk,),
+        out_kernel,
+        grid=(half // blk,),
         in_specs=[
             pl.BlockSpec((rows, blk), lambda i: (0, i)),
-            pl.BlockSpec((rows, other), lambda i: (0, 0), pipeline_mode=pl.Buffered(1)),
+            pl.BlockSpec((rows, depth), lambda i: (0, 0), pipeline_mode=pl.Buffered(1)),
             pl.BlockSpec(memory_space=pl.ANY),
         ],
-        out_specs=out_spec,
+        out_specs=pl.BlockSpec((None, None, blk, depth), lambda i: (0, 0, i, 0)),
         out_shape=sds(into.shape, F32),
         input_output_aliases={2: 0},
         compiler_params=params(),
         cost_estimate=cost(),
-        name="weight_gradient",
-    )(to_hbm(moving), to_hbm(fixed), into)
+        name="out_gradient",
+    )(to_hbm(act), to_hbm(ds), into)
+
+
+def in_kernel(first, low0_ref, dh0_ref, low1_ref, dh1_ref, _, out_ref):
+    step = pl.program_id(0)
+
+    @pl.when(step < first)
+    def _():
+        out_ref[...] = dot_tn(low0_ref[...], dh0_ref[...])
+
+    @pl.when(step >= first)
+    def _():
+        out_ref[...] = dot_tn(low1_ref[...], dh1_ref[...])
+
+
+def in_gradient(low0, dh0, low1, dh1, into, blk):
+    rows, half = dh0.shape
+    depth = low0.shape[1]
+    first, steps = half // blk, (half + dh1.shape[1]) // blk
+    skip = first - dh1.shape[1] // blk
+    fixed = pl.BlockSpec((rows, depth), lambda i: (0, 0), pipeline_mode=pl.Buffered(1))
+    return pl.pallas_call(
+        lambda *refs: in_kernel(first, *refs),
+        grid=(steps,),
+        in_specs=[
+            fixed,
+            pl.BlockSpec((rows, blk), lambda i: (0, jnp.minimum(i, first - 1))),
+            fixed,
+            pl.BlockSpec((rows, blk), lambda i: (0, jnp.maximum(i - first, 0))),
+            pl.BlockSpec(memory_space=pl.ANY),
+        ],
+        out_specs=pl.BlockSpec(
+            (None, None, depth, blk),
+            lambda i: (i // first, 0, 0, jnp.where(i < first, i, i - first + skip)),
+        ),
+        out_shape=sds(into.shape, F32),
+        input_output_aliases={4: 0},
+        compiler_params=params(),
+        cost_estimate=cost(),
+        name="in_gradient",
+    )(*(to_hbm(v) for v in (low0, dh0, low1, dh1)), into)
 
 
 def on_device(tokens, routes, cotangent, ln_gain, ln_shift, w_in, b_in, w_out, b_out, centroid):
@@ -436,9 +467,9 @@
     )
     b_half = lax.dynamic_slice_in_dim(b_in.reshape(2, 2 * half), here * half, half, axis=1)
     x_own = exchange(sent_tok)
-    x_par = swap(x_own)
     [sent_cot] = call(pack_kernel, "pack", (place, cotangent), [sds((slots, depth), BF16)])
     sent_cot, x_own = lax.optimization_barrier((sent_cot, x_own))
+    x_par = swap(x_own)
     dy_own = exchange(sent_cot)
 
     narrow, wide = ("r", sds((both, depth), BF16)), ("r", sds((both, half), BF16))
@@ -456,7 +487,7 @@
         tile=256,
     )
     dy = (("o", dy_own), ("p", swap(dy_own)))
-    p1_own, p1_par, xhat1, row1, n1, sums1, grad_in, grad_out = row_call(
+    p1_own, p1_par, xhat1, row1, n1, low1, dh1, sums1, grad_in, grad_out = row_call(
         second_kernel,
         "second",
         both,
@@ -464,20 +495,19 @@
             *x, ("r", p0), ("s", swap(p0)), *dy, ("r", row),
             ("w", b_out), ("w", gain), ("w", shift), ("w", b_half),
         ),
-        [own_sum, par_sum, narrow, per_row, narrow, sums],
+        [own_sum, par_sum, narrow, per_row, narrow, narrow, ("r", sds((both, half // 2), BF16)), sums],
         sums=1,
         weights=(w_in, w_out),
-        tile=256,
+        mib=46,
         far=(sds((2, 1, depth, half), F32), sds((2, 1, half, depth), F32)),
         scratch=[
-            pltpu.VMEM((256, depth), BF16),
             pltpu.VMEM((256, half), BF16),
             pltpu.VMEM((256, half), BF16),
             pltpu.VMEM((256, depth), BF16),
             pltpu.VMEM((256, half), BF16),
-            pltpu.VMEM((depth, half), F32),
+            pltpu.VMEM((depth, half // 2), F32),
             pltpu.VMEM((half, depth), F32),
-            pltpu.SemaphoreType.DMA((3,)),
+            pltpu.SemaphoreType.DMA((2,)),
         ],
     )
     p1_there, n1 = lax.optimization_barrier((swap(p1_par), n1))
@@ -487,7 +517,7 @@
         slots,
         (("r", p1_own), ("r", p1_there), ("r", row)),
         [("r", sds((slots, depth), BF16))] * 2,
-        tile=256,
+        mib=24,
     )
     returned = exchange(branch)
     ds0, dh0, n0_own, carry_own, n0_par, sums0 = row_call(
@@ -497,7 +527,7 @@
         (
             *dy, ("r", row), ("r", n1), ("s", swap(n1)), ("r", xhat1), ("r", row1), ("w", gain), *x, ("r", slope0),
         ),
-        [narrow, wide, own_sum, own_sum, par_sum, sums],
+        [narrow, wide, ("o", sds((slots, depth), BF16)), own_sum, par_sum, sums],
         sums=1,
         tile=256,
         weights=(w_in, w_out),
@@ -512,13 +542,13 @@
         ),
         [("r", sds((slots, depth), BF16)), ("w", sds((24, depth), F32))],
         sums=1,
-        tile=256,
+        mib=24,
     )
     drow, returned = lax.optimization_barrier((drow, returned))
     grad_returned = exchange(drow)
 
-    grad_out = weight_gradient(True, act0, ds0, grad_out, 512)
-    grad_in = weight_gradient(False, dh0, low0, grad_in, 512)
+    grad_out = out_gradient(act0, ds0, grad_out, 512)
+    grad_in = in_gradient(low0, dh0, low1, dh1, grad_in, 512)
     [mixed] = call(unpack_kernel, "unpack", (place, returned, tokens), [sds(tokens.shape, BF16)])
     other = swap(local)
     one = sds((2, 1, depth), F32)

time: 194 us -> 189 us (0.974)
  blocking collectives: 32.8 us -> 0 us
  waiting for transfers between devices: 21 us -> 39.9 us
  starting transfers between devices: 17.6 us -> 24.7 us
  local copies, waits for them, and re-layouts: 4.68 us -> 7.86 us
    all_to_all x1 -> x0, blocking collectives: 32.8 us -> none  [exchange(): lax.all_to_all(v.reshape(experts, capacity, depth), 'expert', split_axis=...]
    all_to_all x3 -> x4, waiting for transfers between devices: 12.5 us -> 31.7 us  [exchange(): lax.all_to_all(v.reshape(experts, capacity, depth), 'expert', split_axis=...]
    all_to_all x3 -> x4, starting transfers between devices: 16.9 us -> 24.2 us  [exchange(): lax.all_to_all(v.reshape(experts, capacity, depth), 'expert', split_axis=...]
    pallas_call x5, Pallas kernels: 92.7 us -> 87 us  [row_call(): pl.pallas_call(kernel, grid=(steps,), in_specs=[spec(kind, a.shape) for k...]
    pallas_call x2, Pallas kernels: 18.4 us -> 22.7 us  [the longest x1 13.6 us: in_gradient(): pl.pallas_call(lambda *refs: in_kernel(first, *refs), grid=(steps,), in_s...]
    unnamed x26 -> x54, local copies, waits for them, and re-layouts: 4.67 us -> 7.85 us
  transfers between devices with their start and end apart: 10 -> 11, of which waited for: 5 -> 6; matrix products, arithmetic and copies ran while one was open for 0% -> 0% of each run, Pallas kernels for 37% -> 38%
where the time goes in v3:
time: 189 us; the launch traced here: 188 us
  Pallas kernels  115 us (61%)
  waiting for transfers between devices  39.9 us (21%)
  starting transfers between devices  24.7 us (13%)
  local copies, waits for them, and re-layouts  7.86 us (4%)
    pallas_call x5, Pallas kernels, row_call(): pl.pallas_call(kernel, grid=(steps,), in_specs=[spec(kind, a.shape) for k...  87 us
    all_to_all x4, waiting for transfers between devices, exchange(): lax.all_to_all(v.reshape(experts, capacity, depth), 'expert', split_axis=...  31.7 us
    all_to_all x4, starting transfers between devices, exchange(): lax.all_to_all(v.reshape(experts, capacity, depth), 'expert', split_axis=...  24.2 us
    pallas_call x1, Pallas kernels, in_gradient(): pl.pallas_call(lambda *refs: in_kernel(first, *refs), grid=(steps,), in_s...  13.6 us
    pallas_call x1, Pallas kernels, out_gradient(): pl.pallas_call(out_kernel, grid=(half // blk,), in_specs=[pl.BlockSpec((r...  9.19 us
    ppermute x7, waiting for transfers between devices, swap(): return lax.ppermute(v, 'replica', SWAP)  8.26 us
    unnamed x54, local copies, waits for them, and re-layouts  7.85 us
    pallas_call x5, Pallas kernels, call(): pl.pallas_call(kernel, in_specs=[SMEM] * smem_in + [VMEM] * (len(args) -...  5.23 us
  transfers between devices with their start and end apart: 11, of which 6 were waited for; matrix products, arithmetic and copies ran while one was open for 0% of the time, Pallas kernels for 38%

profile of v3, /device:TPU:8, one launch (start us, length us, event | category | flops | bytes accessed | tf_op | source)
XLA Modules:
  0.0 188.4 jit_solution(3153322224431378718)
XLA Ops:
  0.6 0.0 copy-start
  0.7 0.0 copy-start.14
  0.7 0.0 copy-start.16
  0.7 1.1 copy-done.16
  1.8 0.7 copy-done.26
  2.5 1.6 pack_first.1
  4.1 7.2 %all-to-all-start = ((bf16[16,32,1024]{2,1,0:T(8,128)(2,1)}), bf16[16,32,1024]{2,1,0:T(8,128)(2,1)S(1)}, u32[]{:S(2)}, u32[]{:S(2)}) async-start(bf16[16,32,1024]{2,1,0:T(8,128)(2,1)} %bitcast.1), calls=%async_computation | async-start | bytes 2097152 | tf_op jit(solution)/shard_map/all_to_all | solution.py:454
  11.3 0.0 copy-start.23
  11.3 0.0 copy-start.24
  11.3 0.4 pack.1
  11.8 0.0 copy-start.11
  11.8 1.0 copy-done.11
  12.7 24.1 %all-to-all-done = bf16[16,32,1024]{2,1,0:T(8,128)(2,1)S(1)} async-done(((bf16[16,32,1024]{2,1,0:T(8,128)(2,1)}), bf16[16,32,1024]{2,1,0:T(8,128)(2,1)S(1)}, u32[]{:S(2)}, u32[]{:S(2)}) %all-to-all-start) | async-done | bytes 1048608 | tf_op jit(solution)/shard_map/all_to_all | solution.py:454
  36.8 0.0 collective-permute-start
  36.8 4.7 %all-to-all-start.1 = ((bf16[16,32,1024]{2,1,0:T(8,128)(2,1)}), bf16[16,32,1024]{2,1,0:T(8,128)(2,1)S(1)}, u32[]{:S(2)}, u32[]{:S(2)}) async-start(bf16[16,32,1024]{2,1,0:T(8,128)(2,1)} %bitcast.28), calls=%async_computation.1 | async-start | bytes 2097152 | tf_op jit(solution)/shard_map/all_to_all | solution.py:454
  41.6 0.0 collective-permute-done.par_ref.x_par_ref
  41.6 0.0 copy-start.25
  41.7 19.6 %forward_first.1 = (bf16[1024,1024]{1,0:T(8,128)(2,1)}, bf16[1024,2048]{1,0:T(8,128)(2,1)}, bf16[1024,2048]{1,0:T(8,128)(2,1)}, bf16[1024,1024]{1,0:T(8,128)(2,1)}, f32[1024,128]{1,0:T(8,128)}) custom-call(bf16[512,1024]{1,0:T(8,128)(2,1)} %bitcast.20, bf16[512,1024]{1,0:T(8,128)(2,1)S(1)} %collective-permute-done.par_ref.x_par_ref, ...), custom_call_target="tpu_custom_call" | custom-call | tf_op jit(solution)/shard_map/forward_first/pallas_call | solution.py:87
  61.2 0.1 collective-permute-start.1
  61.3 6.5 %all-to-all-done.1 = bf16[16,32,1024]{2,1,0:T(8,128)(2,1)S(1)} async-done(((bf16[16,32,1024]{2,1,0:T(8,128)(2,1)}), bf16[16,32,1024]{2,1,0:T(8,128)(2,1)S(1)}, u32[]{:S(2)}, u32[]{:S(2)}) %all-to-all-start.1) | async-done | bytes 1048608 | tf_op jit(solution)/shard_map/all_to_all | solution.py:454
  67.8 2.7 %collective-permute-done.2.dy_par_ref.par_ref = bf16[512,1024]{1,0:T(8,128)(2,1)S(1)} collective-permute-done((bf16[512,1024]{1,0:T(8,128)(2,1)S(1)}, bf16[512,1024]{1,0:T(8,128)(2,1)S(1)}, u32[]{:S(2)}, u32[]{:S(2)}) %collective-permute-start.2) | collective-permute-done | bytes 1048608 | tf_op jit(solution)/shard_map/ppermute | solution.py:460
  70.5 0.0 copy-start.7
  70.5 41.3 %second.1 = (f32[512,1024]{1,0:T(8,128)}, bf16[512,1024]{1,0:T(8,128)(2,1)}, bf16[1024,1024]{1,0:T(8,128)(2,1)}, f32[1024,128]{1,0:T(8,128)}, bf16[1024,1024]{1,...) custom-call(bf16[512,1024]{1,0:T(8,128)(2,1)} %bitcast.21, ...), custom_call_target="tpu_custom_call" | custom-call | tf_op jit(solution)/shard_map/second/pallas_call | solution.py:87
  111.9 0.0 copy-start.21
  111.9 0.6 copy-done.21
  112.5 0.1 collective-permute-start.3
  112.6 2.7 %collective-permute-done.3.theirs_ref = bf16[512,1024]{1,0:T(8,128)(2,1)S(1)} collective-permute-done((bf16[512,1024]{1,0:T(8,128)(2,1)}, bf16[512,1024]{1,0:T(8,128)(2,1)S(1)}, u32[]{:S(2)}, u32[]{:S(2)}) %collective-permute-start.3) | collective-permute-done | bytes 1048608 | tf_op jit(solution)/shard_map/ppermute | solution.py:460
  115.4 0.1 collective-permute-start.4
  115.5 1.6 copy-done.13
  117.1 1.5 branch.1
  118.6 5.4 %all-to-all-start.2 = ((bf16[16,32,1024]{2,1,0:T(8,128)(2,1)}), bf16[16,32,1024]{2,1,0:T(8,128)(2,1)S(1)}, u32[]{:S(2)}, u32[]{:S(2)}) async-start(bf16[16,32,1024]{2,1,0:T(8,128)(2,1)} %bitcast.40), calls=%async_computation.2 | async-start | bytes 2097152 | tf_op jit(solution)/shard_map/all_to_all | solution.py:454
  124.0 0.0 copy-start.8
  124.0 0.0 copy-start.22
  124.0 21.6 %backward_first.1 = (bf16[1024,1024]{1,0:T(8,128)(2,1)}, bf16[1024,2048]{1,0:T(8,128)(2,1)}, bf16[512,1024]{1,0:T(8,128)(2,1)}, f32[512,1024]{1,0:T(8,128)}, bf1...) custom-call(bf16[512,1024]{1,0:T(8,128)(2,1)} %bitcast.26, bf16[512,1024]{1,0:T(8,128)(2,1)S(1)} %copy-done.10, ...), custom_call_target="tpu_custom_call" | custom-call | tf_op jit(solution)/shard_map/backward_first/pallas_call | solution.py:87
  145.6 0.1 collective-permute-start.5
  145.7 2.9 %collective-permute-done.5.theirs_ref = bf16[512,1024]{1,0:T(8,128)(2,1)S(1)} collective-permute-done((bf16[512,1024]{1,0:T(8,128)(2,1)}, bf16[512,1024]{1,0:T(8,128)(2,1)S(1)}, u32[]{:S(2)}, u32[]{:S(2)}) %collective-permute-start.5) | collective-permute-done | bytes 1048608 | tf_op jit(solution)/shard_map/ppermute | solution.py:460
  148.6 1.6 copy-done.12
  150.2 1.2 copy-done.19
  151.4 3.0 %input_gradient.1 = (bf16[512,1024]{1,0:T(8,128)(2,1)}, f32[24,1024]{1,0:T(8,128)S(1)}) custom-call(bf16[512,1024]{1,0:T(8,128)(2,1)S(1)} %bitcast.27, bf16[512,1024]{1,0:T(8,128)(2,1)S(1)} %copy-done.18, f32[1024,128]{1,0:T(8,128)S(1)} %copy-done.8, bf16[512,1024]{1,0:T(8,128)(2,1)S(1)} %bitcast.23, bf16[512,1024]{1,0:T(8,128)(2,1)S(1)} %copy-done.19, ...), custom_call_target="tpu_custom_call" | custom-call | tf_op jit(solution)/shard_map/input_gradient/pallas_call | solution.py:87
  154.4 0.0 all-to-all-done.2
  154.4 6.9 %all-to-all-start.3 = ((bf16[16,32,1024]{2,1,0:T(8,128)(2,1)}), bf16[16,32,1024]{2,1,0:T(8,128)(2,1)S(1)}, u32[]{:S(2)}, u32[]{:S(2)}) async-start(bf16[16,32,1024]{2,1,0:T(8,128)(2,1)} %bitcast.39), calls=%async_computation.3 | async-start | bytes 2097152 | tf_op jit(solution)/shard_map/all_to_all | solution.py:454
  161.3 0.0 collective-permute-start.6
  161.4 9.2 %out_gradient.1 = f32[2,1,2048,1024]{3,2,1,0:T(8,128)} custom-call(bf16[1024,2048]{1,0:T(8,128)(2,1)} %get-tuple-element.80.act_ref, bf16[1024,1024]{1,0:T(8,128)(2,1)} %get-tuple-element.81.ds_ref, f32[2,1,2048,1024]{3,2,1,0:T(8,128)} %get-tuple-element.82._), custom_call_target="tpu_custom_call", output_to_operand_aliasing={{}: (2, {})} | custom-call | tf_op jit(solution)/shard_map/out_gradient/pallas_call | solution.py:385
  170.5 13.6 %in_gradient.1 = f32[2,1,1024,2048]{3,2,1,0:T(8,128)} custom-call(bf16[1024,1024]{1,0:T(8,128)(2,1)} %get-tuple-element.75.refs_0_, bf16[1024,2048]{1,0:T(8,128)(2,1)} %get-tuple-element.76.refs_1_, bf16[1024,1024]{1,0:T(8,128)(2,1)} %get-tuple-element.77.refs_2_, bf16[1024,1024]{1,0:T(8,128)(2,1)} %get-tuple-element.78.refs_3_, ...), custom_call_target="tpu_custom_call", output_to_operand_aliasing={{}: (4, {})} | custom-call | tf_op jit(solution)/shard_map/in_gradient/pallas_call | solution.py:420
  184.1 1.3 unpack.2
  185.4 0.7 finish.1
  186.0 1.1 all-to-all-done.3
  187.1 1.3 unpack.3
  (41 shorter events, 0.1 us)
Async XLA Ops:
  0.6 40.9 %copy-start = (bf16[2,1,4096]{2,0,1:T(2,128)(2,1)S(1)}, bf16[2,1,4096]{2,0,1:T(2,128)(2,1)}, u32[]{:S(2)}) copy-start(bf16[2,1,4096]{2,0,1:T(2,128)(2,1)} %param.16) | copy-start | bytes 49156
  0.7 10.7 %copy-start.14 = (bf16[256,1024]{1,0:T(8,128)(2,1)S(1)}, bf16[256,1024]{1,0:T(8,128)(2,1)}, u32[]{:S(2)}) copy-start(bf16[256,1024]{1,0:T(8,128)(2,1)} %base_ref.3) | copy-start | bytes 1572868
  0.7 1.1 copy-start.16
  1.8 0.7 copy-start.26
  4.1 32.8 %all-to-all-start = ((bf16[16,32,1024]{2,1,0:T(8,128)(2,1)}), bf16[16,32,1024]{2,1,0:T(8,128)(2,1)S(1)}, u32[]{:S(2)}, u32[]{:S(2)}) async-start(bf16[16,32,1024]{2,1,0:T(8,128)(2,1)} %bitcast.1), calls=%async_computation | async-start | bytes 2097152 | tf_op jit(solution)/shard_map/all_to_all | solution.py:454
  11.3 30.3 %copy-start.20 = (bf16[2,1,1024]{2,0,1:T(2,128)(2,1)S(1)}, bf16[2,1,1024]{2,0,1:T(2,128)(2,1)}, u32[]{:S(2)}) copy-start(bf16[2,1,1024]{2,0,1:T(2,128)(2,1)} %param.13) | copy-start | bytes 12292
  11.3 30.3 %copy-start.23 = (bf16[2,1,1024]{2,0,1:T(2,128)(2,1)S(1)}, bf16[2,1,1024]{2,0,1:T(2,128)(2,1)}, u32[]{:S(2)}) copy-start(bf16[2,1,1024]{2,0,1:T(2,128)(2,1)} %param.14) | copy-start | bytes 12292
  11.3 30.3 %copy-start.24 = (bf16[1,1024]{1,0:T(2,128)(2,1)S(1)}, bf16[1,1024]{1,0:T(2,128)(2,1)}, u32[]{:S(2)}) copy-start(bf16[1,1024]{1,0:T(2,128)(2,1)} %center_ref.3) | copy-start | bytes 6148
  11.8 1.0 copy-start.11
  36.8 4.8 %copy-start.2 = (bf16[16,32,1024]{2,1,0:T(8,128)(2,1)}, bf16[16,32,1024]{2,1,0:T(8,128)(2,1)S(1)}, u32[]{:S(2)}) copy-start(bf16[16,32,1024]{2,1,0:T(8,128)(2,1)S(1)} %all-to-all-done) | copy-start | bytes 3145732
  36.8 4.8 %collective-permute-start = (bf16[512,1024]{1,0:T(8,128)(2,1)S(1)}, bf16[512,1024]{1,0:T(8,128)(2,1)S(1)}, u32[]{:S(2)}, u32[]{:S(2)}) collective-permute-start(bf16[512,1024]{1,0:T(8,128)(2,1)S(1)} %bitcast.19), channel_id=1, source_target_pairs={{0,1},{1,0},{2,3},{3,2},{4,5},{5,4},{6,7},{7,6},{8,9},{9,8},{10,11... | collective-permute-start | bytes 3145736 | tf_op jit(solution)/shard_map/ppermute | solution.py:460
  36.8 31.0 %all-to-all-start.1 = ((bf16[16,32,1024]{2,1,0:T(8,128)(2,1)}), bf16[16,32,1024]{2,1,0:T(8,128)(2,1)S(1)}, u32[]{:S(2)}, u32[]{:S(2)}) async-start(bf16[16,32,1024]{2,1,0:T(8,128)(2,1)} %bitcast.28), calls=%async_computation.1 | async-start | bytes 2097152 | tf_op jit(solution)/shard_map/all_to_all | solution.py:454
  41.6 28.9 %copy-start.6 = (bf16[512,1024]{1,0:T(8,128)(2,1)}, bf16[512,1024]{1,0:T(8,128)(2,1)S(1)}, u32[]{:S(2)}) copy-start(bf16[512,1024]{1,0:T(8,128)(2,1)S(1)} %collective-permute-done.par_ref.x_par_ref) | copy-start | bytes 3145732
  41.6 28.9 %copy-start.25 = (bf16[2,1,1024]{2,0,1:T(2,128)(2,1)S(1)}, bf16[2,1,1024]{2,0,1:T(2,128)(2,1)}, u32[]{:S(2)}) copy-start(bf16[2,1,1024]{2,0,1:T(2,128)(2,1)} %param.18) | copy-start | bytes 12292
  61.2 9.3 %collective-permute-start.1 = (bf16[1024,1024]{1,0:T(8,128)(2,1)}, bf16[1024,1024]{1,0:T(8,128)(2,1)}, u32[]{:S(2)}, u32[]{:S(2)}) collective-permute-start(bf16[1024,1024]{1,0:T(8,128)(2,1)} %get-tuple-element.55.mine_ref), channel_id=1, source_target_pairs={{0,1},{1,0},{2,3},{3,2},{4,5},{5,4},{6,7},{7,6},{8,9},{9,8},{10,11... | collective-permute-start | bytes 6291464 | tf_op jit(solution)/shard_map/ppermute | solution.py:460
  67.8 2.7 %copy-start.4 = (bf16[16,32,1024]{2,1,0:T(8,128)(2,1)}, bf16[16,32,1024]{2,1,0:T(8,128)(2,1)S(1)}, u32[]{:S(2)}) copy-start(bf16[16,32,1024]{2,1,0:T(8,128)(2,1)S(1)} %all-to-all-done.1) | copy-start | bytes 3145732
  67.8 2.7 %collective-permute-start.2 = (bf16[512,1024]{1,0:T(8,128)(2,1)S(1)}, bf16[512,1024]{1,0:T(8,128)(2,1)S(1)}, u32[]{:S(2)}, u32[]{:S(2)}) collective-permute-start(bf16[512,1024]{1,0:T(8,128)(2,1)S(1)} %bitcast.24), channel_id=1, source_target_pairs={{0,1},{1,0},{2,3},{3,2},{4,5},{5,4},{6,7},{7,6},{8,9},{9,8},{10,11... | collective-permute-start | bytes 3145736 | tf_op jit(solution)/shard_map/ppermute | solution.py:460
  70.5 41.4 %copy-start.9 = (bf16[512,1024]{1,0:T(8,128)(2,1)}, bf16[512,1024]{1,0:T(8,128)(2,1)S(1)}, u32[]{:S(2)}) copy-start(bf16[512,1024]{1,0:T(8,128)(2,1)S(1)} %collective-permute-done.2.dy_par_ref.par_ref) | copy-start | bytes 3145732
  70.5 45.0 %copy-start.7 = (f32[1024,128]{1,0:T(8,128)S(1)}, f32[1024,128]{1,0:T(8,128)}, u32[]{:S(2)}) copy-start(f32[1024,128]{1,0:T(8,128)} %get-tuple-element.56.gate_ref.row_ref) | copy-start | bytes 1572868
  111.9 0.6 copy-start.21
  112.5 2.9 %collective-permute-start.3 = (bf16[512,1024]{1,0:T(8,128)(2,1)}, bf16[512,1024]{1,0:T(8,128)(2,1)S(1)}, u32[]{:S(2)}, u32[]{:S(2)}) collective-permute-start(bf16[512,1024]{1,0:T(8,128)(2,1)} %get-tuple-element.58), channel_id=1, source_target_pairs={{0,1},{1,0},{2,3},{3,2},{4,5},{5,4},{6,7},{7,6},{8,9},{9,8},{10,11... | collective-permute-start | bytes 3145736 | tf_op jit(solution)/shard_map/ppermute | solution.py:460
  115.4 8.6 %collective-permute-start.4 = (bf16[1024,1024]{1,0:T(8,128)(2,1)}, bf16[1024,1024]{1,0:T(8,128)(2,1)}, u32[]{:S(2)}, u32[]{:S(2)}) collective-permute-start(bf16[1024,1024]{1,0:T(8,128)(2,1)} %get-tuple-element.62.mine_ref), channel_id=1, source_target_pairs={{0,1},{1,0},{2,3},{3,2},{4,5},{5,4},{6,7},{7,6},{8,9},{9,8},{10,11... | collective-permute-start | bytes 6291464 | tf_op jit(solution)/shard_map/ppermute | solution.py:460
  115.5 1.6 copy-start.13
  117.1 6.9 %copy-start.10 = (bf16[512,1024]{1,0:T(8,128)(2,1)S(1)}, bf16[512,1024]{1,0:T(8,128)(2,1)}, u32[]{:S(2)}) copy-start(bf16[512,1024]{1,0:T(8,128)(2,1)} %copy-done.9) | copy-start | bytes 3145732
  118.6 35.8 %all-to-all-start.2 = ((bf16[16,32,1024]{2,1,0:T(8,128)(2,1)}), bf16[16,32,1024]{2,1,0:T(8,128)(2,1)S(1)}, u32[]{:S(2)}, u32[]{:S(2)}) async-start(bf16[16,32,1024]{2,1,0:T(8,128)(2,1)} %bitcast.40), calls=%async_computation.2 | async-start | bytes 2097152 | tf_op jit(solution)/shard_map/all_to_all | solution.py:454
  124.0 24.6 %copy-start.3 = (bf16[16,32,1024]{2,1,0:T(8,128)(2,1)S(1)}, bf16[16,32,1024]{2,1,0:T(8,128)(2,1)}, u32[]{:S(2)}) copy-start(bf16[16,32,1024]{2,1,0:T(8,128)(2,1)} %copy-done.2) | copy-start | bytes 3145732
  124.0 24.6 %copy-start.5 = (bf16[16,32,1024]{2,1,0:T(8,128)(2,1)S(1)}, bf16[16,32,1024]{2,1,0:T(8,128)(2,1)}, u32[]{:S(2)}) copy-start(bf16[16,32,1024]{2,1,0:T(8,128)(2,1)} %copy-done.4) | copy-start | bytes 3145732
  124.0 24.6 %copy-start.8 = (f32[1024,128]{1,0:T(8,128)S(1)}, f32[1024,128]{1,0:T(8,128)}, u32[]{:S(2)}) copy-start(f32[1024,128]{1,0:T(8,128)} %get-tuple-element.56.gate_ref.row_ref) | copy-start | bytes 1572868
  124.0 24.6 %copy-start.18 = (bf16[512,1024]{1,0:T(8,128)(2,1)S(1)}, bf16[512,1024]{1,0:T(8,128)(2,1)}, u32[]{:S(2)}) copy-start(bf16[512,1024]{1,0:T(8,128)(2,1)} %get-tuple-element.61.out_ref) | copy-start | bytes 3145732
  124.0 24.6 %copy-start.22 = (f32[8,1024]{1,0:T(8,128)S(1)}, f32[8,1024]{1,0:T(8,128)}, u32[]{:S(2)}) copy-start(f32[8,1024]{1,0:T(8,128)} %copy-done.21) | copy-start | bytes 98308
  145.6 2.9 %collective-permute-start.5 = (bf16[512,1024]{1,0:T(8,128)(2,1)}, bf16[512,1024]{1,0:T(8,128)(2,1)S(1)}, u32[]{:S(2)}, u32[]{:S(2)}) collective-permute-start(bf16[512,1024]{1,0:T(8,128)(2,1)} %get-tuple-element.67), channel_id=1, source_target_pairs={{0,1},{1,0},{2,3},{3,2},{4,5},{5,4},{6,7},{7,6},{8,9},{9,8},{10,11... | collective-permute-start | bytes 3145736 | tf_op jit(solution)/shard_map/ppermute | solution.py:460
  148.6 1.6 copy-start.12
  150.2 1.2 copy-start.19
  154.4 32.7 %all-to-all-start.3 = ((bf16[16,32,1024]{2,1,0:T(8,128)(2,1)}), bf16[16,32,1024]{2,1,0:T(8,128)(2,1)S(1)}, u32[]{:S(2)}, u32[]{:S(2)}) async-start(bf16[16,32,1024]{2,1,0:T(8,128)(2,1)} %bitcast.39), calls=%async_computation.3 | async-start | bytes 2097152 | tf_op jit(solution)/shard_map/all_to_all | solution.py:454
  161.3 24.0 %collective-permute-start.6 = (f32[24,1024]{1,0:T(8,128)S(1)}, f32[24,1024]{1,0:T(8,128)S(1)}, u32[]{:S(2)}, u32[]{:S(2)}) collective-permute-start(f32[24,1024]{1,0:T(8,128)S(1)} %get-tuple-element.83.refs_1_), channel_id=1, source_target_pairs={{0,1},{1,0},{2,3},{3,2},{4,5},{5,4},{6,7},{7,6},{8,9},{9,8},{10,11... | collective-permute-start | bytes 294920 | tf_op jit(solution)/shard_map/ppermute | solution.py:460
  170.5 13.6 %copy-start.17 = (bf16[256,1024]{1,0:T(8,128)(2,1)S(1)}, bf16[256,1024]{1,0:T(8,128)(2,1)}, u32[]{:S(2)}) copy-start(bf16[256,1024]{1,0:T(8,128)(2,1)} %base_ref.2) | copy-start | bytes 1572868
  170.5 17.8 %copy-start.1 = (bf16[2,1,4096]{2,0,1:T(2,128)(2,1)S(1)}, bf16[2,1,4096]{2,0,1:T(2,128)(2,1)}, u32[]{:S(2)}) copy-start(bf16[2,1,4096]{2,0,1:T(2,128)(2,1)} %param.16) | copy-start | bytes 49156
  184.1 3.0 %copy-start.15 = (bf16[256,1024]{1,0:T(8,128)(2,1)S(1)}, bf16[256,1024]{1,0:T(8,128)(2,1)}, u32[]{:S(2)}) copy-start(bf16[256,1024]{1,0:T(8,128)(2,1)} %base_ref.3) | copy-start | bytes 1572868

commit v4 on v3

--- a/solution.py
+++ b/solution.py
@@ -495,7 +495,7 @@
             *x, ("r", p0), ("s", swap(p0)), *dy, ("r", row),
             ("w", b_out), ("w", gain), ("w", shift), ("w", b_half),
         ),
-        [own_sum, par_sum, narrow, per_row, narrow, narrow, ("r", sds((both, half // 2), BF16)), sums],
+        [own_sum, par_sum, narrow, per_row, narrow, narrow, ("r", sds((both, half // 4), BF16)), sums],
         sums=1,
         weights=(w_in, w_out),
         mib=46,
@@ -505,7 +505,7 @@
             pltpu.VMEM((256, half), BF16),
             pltpu.VMEM((256, depth), BF16),
             pltpu.VMEM((256, half), BF16),
-            pltpu.VMEM((depth, half // 2), F32),
+            pltpu.VMEM((depth, 3 * half // 4), F32),
             pltpu.VMEM((half, depth), F32),
             pltpu.SemaphoreType.DMA((2,)),
         ],

time: 189 us -> 191 us (1.011)
  waiting for transfers between devices: 39.9 us -> 41.9 us
    pallas_call x1, Pallas kernels: 13.6 us -> 11.6 us  [in_gradient(): pl.pallas_call(lambda *refs: in_kernel(first, *refs), grid=(steps,), in_s...]
    all_to_all x4, waiting for transfers between devices: 31.7 us -> 33.6 us  [exchange(): lax.all_to_all(v.reshape(experts, capacity, depth), 'expert', split_axis=...]
  transfers between devices with their start and end apart: 11 -> 11, of which waited for: 6 -> 6; matrix products, arithmetic and copies ran while one was open for 0% -> 0% of each run, Pallas kernels for 38% -> 36%
where the time goes in v4:
time: 191 us; the launch traced here: 190 us
  Pallas kernels  114 us (60%)
  waiting for transfers between devices  41.9 us (22%)
  starting transfers between devices  24.7 us (13%)
  local copies, waits for them, and re-layouts  7.86 us (4%)
    pallas_call x5, Pallas kernels, row_call(): pl.pallas_call(kernel, grid=(steps,), in_specs=[spec(kind, a.shape) for k...  88.4 us
    all_to_all x4, waiting for transfers between devices, exchange(): lax.all_to_all(v.reshape(experts, capacity, depth), 'expert', split_axis=...  33.6 us
    all_to_all x4, starting transfers between devices, exchange(): lax.all_to_all(v.reshape(experts, capacity, depth), 'expert', split_axis=...  24.3 us
    pallas_call x1, Pallas kernels, in_gradient(): pl.pallas_call(lambda *refs: in_kernel(first, *refs), grid=(steps,), in_s...  11.6 us
    pallas_call x1, Pallas kernels, out_gradient(): pl.pallas_call(out_kernel, grid=(half // blk,), in_specs=[pl.BlockSpec((r...  9.19 us
    ppermute x7, waiting for transfers between devices, swap(): return lax.ppermute(v, 'replica', SWAP)  8.27 us
    unnamed x54, local copies, waits for them, and re-layouts  7.85 us
    pallas_call x5, Pallas kernels, call(): pl.pallas_call(kernel, in_specs=[SMEM] * smem_in + [VMEM] * (len(args) -...  5.23 us
  transfers between devices with their start and end apart: 11, of which 6 were waited for; matrix products, arithmetic and copies ran while one was open for 0% of the time, Pallas kernels for 36%

profile of v4, /device:TPU:8, one launch (start us, length us, event | category | flops | bytes accessed | tf_op | source)
XLA Modules:
  0.0 189.8 jit_solution(8697982159146309825)
XLA Ops:
  0.6 0.0 copy-start
  0.7 0.0 copy-start.14
  0.7 0.0 copy-start.16
  0.7 1.1 copy-done.16
  1.8 0.7 copy-done.26
  2.5 1.6 pack_first.1
  4.1 7.2 %all-to-all-start = ((bf16[16,32,1024]{2,1,0:T(8,128)(2,1)}), bf16[16,32,1024]{2,1,0:T(8,128)(2,1)S(1)}, u32[]{:S(2)}, u32[]{:S(2)}) async-start(bf16[16,32,1024]{2,1,0:T(8,128)(2,1)} %bitcast.1), calls=%async_computation | async-start | bytes 2097152 | tf_op jit(solution)/shard_map/all_to_all | solution.py:454
  11.3 0.0 copy-start.23
  11.3 0.0 copy-start.24
  11.3 0.4 pack.1
  11.8 0.0 copy-start.11
  11.8 1.0 copy-done.11
  12.7 24.1 %all-to-all-done = bf16[16,32,1024]{2,1,0:T(8,128)(2,1)S(1)} async-done(((bf16[16,32,1024]{2,1,0:T(8,128)(2,1)}), bf16[16,32,1024]{2,1,0:T(8,128)(2,1)S(1)}, u32[]{:S(2)}, u32[]{:S(2)}) %all-to-all-start) | async-done | bytes 1048608 | tf_op jit(solution)/shard_map/all_to_all | solution.py:454
  36.8 4.7 %all-to-all-start.1 = ((bf16[16,32,1024]{2,1,0:T(8,128)(2,1)}), bf16[16,32,1024]{2,1,0:T(8,128)(2,1)S(1)}, u32[]{:S(2)}, u32[]{:S(2)}) async-start(bf16[16,32,1024]{2,1,0:T(8,128)(2,1)} %bitcast.28), calls=%async_computation.1 | async-start | bytes 2097152 | tf_op jit(solution)/shard_map/all_to_all | solution.py:454
  41.6 0.0 collective-permute-done.par_ref.x_par_ref
  41.6 0.0 copy-start.25
  41.7 19.6 %forward_first.1 = (bf16[1024,1024]{1,0:T(8,128)(2,1)}, bf16[1024,2048]{1,0:T(8,128)(2,1)}, bf16[1024,2048]{1,0:T(8,128)(2,1)}, bf16[1024,1024]{1,0:T(8,128)(2,1)}, f32[1024,128]{1,0:T(8,128)}) custom-call(bf16[512,1024]{1,0:T(8,128)(2,1)} %bitcast.20, bf16[512,1024]{1,0:T(8,128)(2,1)S(1)} %collective-permute-done.par_ref.x_par_ref, ...), custom_call_target="tpu_custom_call" | custom-call | tf_op jit(solution)/shard_map/forward_first/pallas_call | solution.py:87
  61.2 0.1 collective-permute-start.1
  61.3 6.5 %all-to-all-done.1 = bf16[16,32,1024]{2,1,0:T(8,128)(2,1)S(1)} async-done(((bf16[16,32,1024]{2,1,0:T(8,128)(2,1)}), bf16[16,32,1024]{2,1,0:T(8,128)(2,1)S(1)}, u32[]{:S(2)}, u32[]{:S(2)}) %all-to-all-start.1) | async-done | bytes 1048608 | tf_op jit(solution)/shard_map/all_to_all | solution.py:454
  67.8 0.0 collective-permute-start.2
  67.8 2.7 %collective-permute-done.2.dy_par_ref.par_ref = bf16[512,1024]{1,0:T(8,128)(2,1)S(1)} collective-permute-done((bf16[512,1024]{1,0:T(8,128)(2,1)S(1)}, bf16[512,1024]{1,0:T(8,128)(2,1)S(1)}, u32[]{:S(2)}, u32[]{:S(2)}) %collective-permute-start.2) | collective-permute-done | bytes 1048608 | tf_op jit(solution)/shard_map/ppermute | solution.py:460
  70.5 0.0 collective-permute-done.1.theirs_ref
  70.5 0.0 copy-start.7
  70.5 42.9 %second.1 = (f32[512,1024]{1,0:T(8,128)}, bf16[512,1024]{1,0:T(8,128)(2,1)}, bf16[1024,1024]{1,0:T(8,128)(2,1)}, f32[1024,128]{1,0:T(8,128)}, bf16[1024,1024]{1,...) custom-call(bf16[512,1024]{1,0:T(8,128)(2,1)} %bitcast.21, ...), custom_call_target="tpu_custom_call" | custom-call | tf_op jit(solution)/shard_map/second/pallas_call | solution.py:87
  113.4 0.0 copy-start.21
  113.4 0.6 copy-done.21
  114.0 0.1 collective-permute-start.3
  114.2 2.7 %collective-permute-done.3.theirs_ref = bf16[512,1024]{1,0:T(8,128)(2,1)S(1)} collective-permute-done((bf16[512,1024]{1,0:T(8,128)(2,1)}, bf16[512,1024]{1,0:T(8,128)(2,1)S(1)}, u32[]{:S(2)}, u32[]{:S(2)}) %collective-permute-start.3) | collective-permute-done | bytes 1048608 | tf_op jit(solution)/shard_map/ppermute | solution.py:460
  116.9 0.1 collective-permute-start.4
  117.0 1.6 copy-done.13
  118.6 1.5 branch.1
  120.1 5.4 %all-to-all-start.2 = ((bf16[16,32,1024]{2,1,0:T(8,128)(2,1)}), bf16[16,32,1024]{2,1,0:T(8,128)(2,1)S(1)}, u32[]{:S(2)}, u32[]{:S(2)}) async-start(bf16[16,32,1024]{2,1,0:T(8,128)(2,1)} %bitcast.40), calls=%async_computation.2 | async-start | bytes 2097152 | tf_op jit(solution)/shard_map/all_to_all | solution.py:454
  125.5 0.0 collective-permute-done.4.theirs_ref
  125.5 0.0 copy-start.8
  125.6 0.0 copy-start.22
  125.6 21.6 %backward_first.1 = (bf16[1024,1024]{1,0:T(8,128)(2,1)}, bf16[1024,2048]{1,0:T(8,128)(2,1)}, bf16[512,1024]{1,0:T(8,128)(2,1)}, f32[512,1024]{1,0:T(8,128)}, bf1...) custom-call(bf16[512,1024]{1,0:T(8,128)(2,1)} %bitcast.26, bf16[512,1024]{1,0:T(8,128)(2,1)S(1)} %copy-done.10, ...), custom_call_target="tpu_custom_call" | custom-call | tf_op jit(solution)/shard_map/backward_first/pallas_call | solution.py:87
  147.1 0.1 collective-permute-start.5
  147.2 2.9 %collective-permute-done.5.theirs_ref = bf16[512,1024]{1,0:T(8,128)(2,1)S(1)} collective-permute-done((bf16[512,1024]{1,0:T(8,128)(2,1)}, bf16[512,1024]{1,0:T(8,128)(2,1)S(1)}, u32[]{:S(2)}, u32[]{:S(2)}) %collective-permute-start.5) | collective-permute-done | bytes 1048608 | tf_op jit(solution)/shard_map/ppermute | solution.py:460
  150.1 1.6 copy-done.12
  151.7 1.2 copy-done.19
  152.9 3.0 %input_gradient.1 = (bf16[512,1024]{1,0:T(8,128)(2,1)}, f32[24,1024]{1,0:T(8,128)S(1)}) custom-call(bf16[512,1024]{1,0:T(8,128)(2,1)S(1)} %bitcast.27, bf16[512,1024]{1,0:T(8,128)(2,1)S(1)} %copy-done.18, f32[1024,128]{1,0:T(8,128)S(1)} %copy-done.8, bf16[512,1024]{1,0:T(8,128)(2,1)S(1)} %bitcast.23, bf16[512,1024]{1,0:T(8,128)(2,1)S(1)} %copy-done.19, ...), custom_call_target="tpu_custom_call" | custom-call | tf_op jit(solution)/shard_map/input_gradient/pallas_call | solution.py:87
  155.9 6.9 %all-to-all-start.3 = ((bf16[16,32,1024]{2,1,0:T(8,128)(2,1)}), bf16[16,32,1024]{2,1,0:T(8,128)(2,1)S(1)}, u32[]{:S(2)}, u32[]{:S(2)}) async-start(bf16[16,32,1024]{2,1,0:T(8,128)(2,1)} %bitcast.39), calls=%async_computation.3 | async-start | bytes 2097152 | tf_op jit(solution)/shard_map/all_to_all | solution.py:454
  162.8 9.2 %out_gradient.1 = f32[2,1,2048,1024]{3,2,1,0:T(8,128)} custom-call(bf16[1024,2048]{1,0:T(8,128)(2,1)} %get-tuple-element.80.act_ref, bf16[1024,1024]{1,0:T(8,128)(2,1)} %get-tuple-element.81.ds_ref, f32[2,1,2048,1024]{3,2,1,0:T(8,128)} %get-tuple-element.82._), custom_call_target="tpu_custom_call", output_to_operand_aliasing={{}: (2, {})} | custom-call | tf_op jit(solution)/shard_map/out_gradient/pallas_call | solution.py:385
  172.0 11.6 %in_gradient.1 = f32[2,1,1024,2048]{3,2,1,0:T(8,128)} custom-call(bf16[1024,1024]{1,0:T(8,128)(2,1)} %get-tuple-element.75.refs_0_, bf16[1024,2048]{1,0:T(8,128)(2,1)} %get-tuple-element.76.refs_1_, bf16[1024,1024]{1,0:T(8,128)(2,1)} %get-tuple-element.77.refs_2_, bf16[1024,512]{1,0:T(8,128)(2,1)} %get-tuple-element.78.refs_3_, ...), custom_call_target="tpu_custom_call", output_to_operand_aliasing={{}: (4, {})} | custom-call | tf_op jit(solution)/shard_map/in_gradient/pallas_call | solution.py:420
  183.6 1.3 unpack.2
  184.9 0.7 finish.1
  185.6 3.0 %all-to-all-done.3 = bf16[16,32,1024]{2,1,0:T(8,128)(2,1)S(1)} async-done(((bf16[16,32,1024]{2,1,0:T(8,128)(2,1)}), bf16[16,32,1024]{2,1,0:T(8,128)(2,1)S(1)}, u32[]{:S(2)}, u32[]{:S(2)}) %all-to-all-start.3) | async-done | bytes 1048608 | tf_op jit(solution)/shard_map/all_to_all | solution.py:454
  188.6 1.3 unpack.3
  (41 shorter events, 0.1 us)
Async XLA Ops:
  0.6 40.9 %copy-start = (bf16[2,1,4096]{2,0,1:T(2,128)(2,1)S(1)}, bf16[2,1,4096]{2,0,1:T(2,128)(2,1)}, u32[]{:S(2)}) copy-start(bf16[2,1,4096]{2,0,1:T(2,128)(2,1)} %param.16) | copy-start | bytes 49156
  0.7 10.7 %copy-start.14 = (bf16[256,1024]{1,0:T(8,128)(2,1)S(1)}, bf16[256,1024]{1,0:T(8,128)(2,1)}, u32[]{:S(2)}) copy-start(bf16[256,1024]{1,0:T(8,128)(2,1)} %base_ref.3) | copy-start | bytes 1572868
  0.7 1.1 copy-start.16
  1.8 0.7 copy-start.26
  4.1 32.8 %all-to-all-start = ((bf16[16,32,1024]{2,1,0:T(8,128)(2,1)}), bf16[16,32,1024]{2,1,0:T(8,128)(2,1)S(1)}, u32[]{:S(2)}, u32[]{:S(2)}) async-start(bf16[16,32,1024]{2,1,0:T(8,128)(2,1)} %bitcast.1), calls=%async_computation | async-start | bytes 2097152 | tf_op jit(solution)/shard_map/all_to_all | solution.py:454
  11.3 30.3 %copy-start.20 = (bf16[2,1,1024]{2,0,1:T(2,128)(2,1)S(1)}, bf16[2,1,1024]{2,0,1:T(2,128)(2,1)}, u32[]{:S(2)}) copy-start(bf16[2,1,1024]{2,0,1:T(2,128)(2,1)} %param.13) | copy-start | bytes 12292
  11.3 30.3 %copy-start.23 = (bf16[2,1,1024]{2,0,1:T(2,128)(2,1)S(1)}, bf16[2,1,1024]{2,0,1:T(2,128)(2,1)}, u32[]{:S(2)}) copy-start(bf16[2,1,1024]{2,0,1:T(2,128)(2,1)} %param.14) | copy-start | bytes 12292
  11.3 30.3 %copy-start.24 = (bf16[1,1024]{1,0:T(2,128)(2,1)S(1)}, bf16[1,1024]{1,0:T(2,128)(2,1)}, u32[]{:S(2)}) copy-start(bf16[1,1024]{1,0:T(2,128)(2,1)} %center_ref.3) | copy-start | bytes 6148
  11.8 1.0 copy-start.11
  36.8 4.8 %copy-start.2 = (bf16[16,32,1024]{2,1,0:T(8,128)(2,1)}, bf16[16,32,1024]{2,1,0:T(8,128)(2,1)S(1)}, u32[]{:S(2)}) copy-start(bf16[16,32,1024]{2,1,0:T(8,128)(2,1)S(1)} %all-to-all-done) | copy-start | bytes 3145732
  36.8 4.8 %collective-permute-start = (bf16[512,1024]{1,0:T(8,128)(2,1)S(1)}, bf16[512,1024]{1,0:T(8,128)(2,1)S(1)}, u32[]{:S(2)}, u32[]{:S(2)}) collective-permute-start(bf16[512,1024]{1,0:T(8,128)(2,1)S(1)} %bitcast.19), channel_id=1, source_target_pairs={{0,1},{1,0},{2,3},{3,2},{4,5},{5,4},{6,7},{7,6},{8,9},{9,8},{10,11... | collective-permute-start | bytes 3145736 | tf_op jit(solution)/shard_map/ppermute | solution.py:460
  36.8 31.0 %all-to-all-start.1 = ((bf16[16,32,1024]{2,1,0:T(8,128)(2,1)}), bf16[16,32,1024]{2,1,0:T(8,128)(2,1)S(1)}, u32[]{:S(2)}, u32[]{:S(2)}) async-start(bf16[16,32,1024]{2,1,0:T(8,128)(2,1)} %bitcast.28), calls=%async_computation.1 | async-start | bytes 2097152 | tf_op jit(solution)/shard_map/all_to_all | solution.py:454
  41.6 28.9 %copy-start.6 = (bf16[512,1024]{1,0:T(8,128)(2,1)}, bf16[512,1024]{1,0:T(8,128)(2,1)S(1)}, u32[]{:S(2)}) copy-start(bf16[512,1024]{1,0:T(8,128)(2,1)S(1)} %collective-permute-done.par_ref.x_par_ref) | copy-start | bytes 3145732
  41.6 28.9 %copy-start.25 = (bf16[2,1,1024]{2,0,1:T(2,128)(2,1)S(1)}, bf16[2,1,1024]{2,0,1:T(2,128)(2,1)}, u32[]{:S(2)}) copy-start(bf16[2,1,1024]{2,0,1:T(2,128)(2,1)} %param.18) | copy-start | bytes 12292
  61.2 9.3 %collective-permute-start.1 = (bf16[1024,1024]{1,0:T(8,128)(2,1)}, bf16[1024,1024]{1,0:T(8,128)(2,1)}, u32[]{:S(2)}, u32[]{:S(2)}) collective-permute-start(bf16[1024,1024]{1,0:T(8,128)(2,1)} %get-tuple-element.55.mine_ref), channel_id=1, source_target_pairs={{0,1},{1,0},{2,3},{3,2},{4,5},{5,4},{6,7},{7,6},{8,9},{9,8},{10,11... | collective-permute-start | bytes 6291464 | tf_op jit(solution)/shard_map/ppermute | solution.py:460
  67.8 2.7 %copy-start.4 = (bf16[16,32,1024]{2,1,0:T(8,128)(2,1)}, bf16[16,32,1024]{2,1,0:T(8,128)(2,1)S(1)}, u32[]{:S(2)}) copy-start(bf16[16,32,1024]{2,1,0:T(8,128)(2,1)S(1)} %all-to-all-done.1) | copy-start | bytes 3145732
  67.8 2.7 %collective-permute-start.2 = (bf16[512,1024]{1,0:T(8,128)(2,1)S(1)}, bf16[512,1024]{1,0:T(8,128)(2,1)S(1)}, u32[]{:S(2)}, u32[]{:S(2)}) collective-permute-start(bf16[512,1024]{1,0:T(8,128)(2,1)S(1)} %bitcast.24), channel_id=1, source_target_pairs={{0,1},{1,0},{2,3},{3,2},{4,5},{5,4},{6,7},{7,6},{8,9},{9,8},{10,11... | collective-permute-start | bytes 3145736 | tf_op jit(solution)/shard_map/ppermute | solution.py:460
  70.5 42.9 %copy-start.9 = (bf16[512,1024]{1,0:T(8,128)(2,1)}, bf16[512,1024]{1,0:T(8,128)(2,1)S(1)}, u32[]{:S(2)}) copy-start(bf16[512,1024]{1,0:T(8,128)(2,1)S(1)} %collective-permute-done.2.dy_par_ref.par_ref) | copy-start | bytes 3145732
  70.5 46.5 %copy-start.7 = (f32[1024,128]{1,0:T(8,128)S(1)}, f32[1024,128]{1,0:T(8,128)}, u32[]{:S(2)}) copy-start(f32[1024,128]{1,0:T(8,128)} %get-tuple-element.56.gate_ref.row_ref) | copy-start | bytes 1572868
  113.4 0.6 copy-start.21
  114.0 2.9 %collective-permute-start.3 = (bf16[512,1024]{1,0:T(8,128)(2,1)}, bf16[512,1024]{1,0:T(8,128)(2,1)S(1)}, u32[]{:S(2)}, u32[]{:S(2)}) collective-permute-start(bf16[512,1024]{1,0:T(8,128)(2,1)} %get-tuple-element.58), channel_id=1, source_target_pairs={{0,1},{1,0},{2,3},{3,2},{4,5},{5,4},{6,7},{7,6},{8,9},{9,8},{10,11... | collective-permute-start | bytes 3145736 | tf_op jit(solution)/shard_map/ppermute | solution.py:460
  116.9 8.6 %collective-permute-start.4 = (bf16[1024,1024]{1,0:T(8,128)(2,1)}, bf16[1024,1024]{1,0:T(8,128)(2,1)}, u32[]{:S(2)}, u32[]{:S(2)}) collective-permute-start(bf16[1024,1024]{1,0:T(8,128)(2,1)} %get-tuple-element.62.mine_ref), channel_id=1, source_target_pairs={{0,1},{1,0},{2,3},{3,2},{4,5},{5,4},{6,7},{7,6},{8,9},{9,8},{10,11... | collective-permute-start | bytes 6291464 | tf_op jit(solution)/shard_map/ppermute | solution.py:460
  117.0 1.6 copy-start.13
  118.6 6.9 %copy-start.10 = (bf16[512,1024]{1,0:T(8,128)(2,1)S(1)}, bf16[512,1024]{1,0:T(8,128)(2,1)}, u32[]{:S(2)}) copy-start(bf16[512,1024]{1,0:T(8,128)(2,1)} %copy-done.9) | copy-start | bytes 3145732
  120.1 35.8 %all-to-all-start.2 = ((bf16[16,32,1024]{2,1,0:T(8,128)(2,1)}), bf16[16,32,1024]{2,1,0:T(8,128)(2,1)S(1)}, u32[]{:S(2)}, u32[]{:S(2)}) async-start(bf16[16,32,1024]{2,1,0:T(8,128)(2,1)} %bitcast.40), calls=%async_computation.2 | async-start | bytes 2097152 | tf_op jit(solution)/shard_map/all_to_all | solution.py:454
  125.5 24.6 %copy-start.3 = (bf16[16,32,1024]{2,1,0:T(8,128)(2,1)S(1)}, bf16[16,32,1024]{2,1,0:T(8,128)(2,1)}, u32[]{:S(2)}) copy-start(bf16[16,32,1024]{2,1,0:T(8,128)(2,1)} %copy-done.2) | copy-start | bytes 3145732
  125.5 24.5 %copy-start.5 = (bf16[16,32,1024]{2,1,0:T(8,128)(2,1)S(1)}, bf16[16,32,1024]{2,1,0:T(8,128)(2,1)}, u32[]{:S(2)}) copy-start(bf16[16,32,1024]{2,1,0:T(8,128)(2,1)} %copy-done.4) | copy-start | bytes 3145732
  125.5 24.5 %copy-start.8 = (f32[1024,128]{1,0:T(8,128)S(1)}, f32[1024,128]{1,0:T(8,128)}, u32[]{:S(2)}) copy-start(f32[1024,128]{1,0:T(8,128)} %get-tuple-element.56.gate_ref.row_ref) | copy-start | bytes 1572868
  125.5 24.5 %copy-start.18 = (bf16[512,1024]{1,0:T(8,128)(2,1)S(1)}, bf16[512,1024]{1,0:T(8,128)(2,1)}, u32[]{:S(2)}) copy-start(bf16[512,1024]{1,0:T(8,128)(2,1)} %get-tuple-element.61.out_ref) | copy-start | bytes 3145732
  125.6 24.5 %copy-start.22 = (f32[8,1024]{1,0:T(8,128)S(1)}, f32[8,1024]{1,0:T(8,128)}, u32[]{:S(2)}) copy-start(f32[8,1024]{1,0:T(8,128)} %copy-done.21) | copy-start | bytes 98308
  147.1 2.9 %collective-permute-start.5 = (bf16[512,1024]{1,0:T(8,128)(2,1)}, bf16[512,1024]{1,0:T(8,128)(2,1)S(1)}, u32[]{:S(2)}, u32[]{:S(2)}) collective-permute-start(bf16[512,1024]{1,0:T(8,128)(2,1)} %get-tuple-element.67), channel_id=1, source_target_pairs={{0,1},{1,0},{2,3},{3,2},{4,5},{5,4},{6,7},{7,6},{8,9},{9,8},{10,11... | collective-permute-start | bytes 3145736 | tf_op jit(solution)/shard_map/ppermute | solution.py:460
  150.1 1.6 copy-start.12
  151.7 1.2 copy-start.19
  155.9 32.7 %all-to-all-start.3 = ((bf16[16,32,1024]{2,1,0:T(8,128)(2,1)}), bf16[16,32,1024]{2,1,0:T(8,128)(2,1)S(1)}, u32[]{:S(2)}, u32[]{:S(2)}) async-start(bf16[16,32,1024]{2,1,0:T(8,128)(2,1)} %bitcast.39), calls=%async_computation.3 | async-start | bytes 2097152 | tf_op jit(solution)/shard_map/all_to_all | solution.py:454
  162.8 22.1 %collective-permute-start.6 = (f32[24,1024]{1,0:T(8,128)S(1)}, f32[24,1024]{1,0:T(8,128)S(1)}, u32[]{:S(2)}, u32[]{:S(2)}) collective-permute-start(f32[24,1024]{1,0:T(8,128)S(1)} %get-tuple-element.83.refs_1_), channel_id=1, source_target_pairs={{0,1},{1,0},{2,3},{3,2},{4,5},{5,4},{6,7},{7,6},{8,9},{9,8},{10,11... | collective-permute-start | bytes 294920 | tf_op jit(solution)/shard_map/ppermute | solution.py:460
  172.0 11.6 %copy-start.17 = (bf16[256,1024]{1,0:T(8,128)(2,1)S(1)}, bf16[256,1024]{1,0:T(8,128)(2,1)}, u32[]{:S(2)}) copy-start(bf16[256,1024]{1,0:T(8,128)(2,1)} %base_ref.2) | copy-start | bytes 1572868
  172.0 17.8 %copy-start.1 = (bf16[2,1,4096]{2,0,1:T(2,128)(2,1)S(1)}, bf16[2,1,4096]{2,0,1:T(2,128)(2,1)}, u32[]{:S(2)}) copy-start(bf16[2,1,4096]{2,0,1:T(2,128)(2,1)} %param.16) | copy-start | bytes 49156
  183.6 4.9 %copy-start.15 = (bf16[256,1024]{1,0:T(8,128)(2,1)S(1)}, bf16[256,1024]{1,0:T(8,128)(2,1)}, u32[]{:S(2)}) copy-start(bf16[256,1024]{1,0:T(8,128)(2,1)} %base_ref.3) | copy-start | bytes 1572868
